TPU v7x, 32 devices: a whole 2x2x4 slice. The times are simulated.
32 devices in a mesh: maps: 2 (over y), row: 4 (over x, core), col: 4 (over z).
Axes of the slice: x: 2, y: 2, z: 4, core: 2. Of those that a mesh axis runs over, the one named last changes fastest.
Arguments:
- positions: float32 [512, 2, 384], P(('maps', 'row', 'col')), parts along dimension 0, may hold values from 0 to 127
- destination: int32 [512, 1], P(('maps', 'row', 'col')), parts along dimension 0, may hold values from 0 to 15; in each aligned block of 16 rows (0 to 15, 16 to 31, ...) at most 4 rows name the same one
- profile: float32 [65, 65], replicated, may hold values from 0.03 to 1
Outputs:
- magnification: float32 [1024, 512], P(('maps', 'row'), 'col'), parts along dimension 0
There are 2 independent parts, one for each index of `maps`. A program takes and returns all parts, laid end to end along the dimension named above; an argument that names none is the same for every part. Nothing has to cross between parts.
Inputs may be any that keep to these rules, and one draw needn't show every extreme that they name: `destination`: at most 4 of the blocks of one device name one tile.
All inputs are finite; a program needn't handle non-finite values.
Results may differ from a plain program's by a relative error of at most 0.0003.
Values may be sent and summed in bfloat16 or wider, within the bound.
No kernel may reach another device: no remote copies, remote signals or barrier semaphores. Data moves between devices by JAX's collectives and lax.ppermute only.
A program may use at most 64 MiB of HBM per device.

v0:
```python
import jax
import jax.numpy as jnp
from jax import lax
from jax.sharding import PartitionSpec as P

TILE = 128
HALO = 32
MOST = 4


group_size = 16


def extended_2(cells, sides, width):
    for axis, dim in sides:
        count = lax.axis_size(axis)
        ends = count - 1
        head = lax.slice_in_dim(cells, 0, width, axis=dim)
        tail = lax.slice_in_dim(cells, cells.shape[dim] - width, cells.shape[dim], axis=dim)
        cells = jnp.concatenate(
            [
                lax.ppermute(tail, axis, [(i, (i + 1) % count) for i in range(ends)]),
                cells,
                lax.ppermute(head, axis, [((i + 1) % count, i) for i in range(ends)]),
            ],
            axis=dim,
        )
    return cells


def hat_table(coords, extent):
    cellular = jnp.arange(extent, dtype=jnp.float32)
    return jnp.maximum(0.0, 1.0 - jnp.abs(coords[:, None] - cellular[None, :])).astype(jnp.bfloat16)


def local_ranks(labels, extent):
    onehot = (labels[:, None] == jnp.arange(extent, dtype=jnp.int32)[None, :]).astype(jnp.int32)
    before = jnp.cumsum(onehot, axis=0) - onehot
    return jnp.sum(before * onehot, axis=1)


def deposit(received, recv_labels, wanted, extent):
    slot_count = recv_labels.shape[0]
    ray_count = received.shape[2]
    padded = jnp.concatenate([received, jnp.full((1, 2, ray_count), -2.0, jnp.float32)], axis=0)
    ordering = jnp.argsort((recv_labels != wanted).astype(jnp.int32), stable=True)
    ordering = jnp.concatenate([ordering, jnp.full((group_size,), slot_count, jnp.int32)])
    valid_count = jnp.sum((recv_labels == wanted).astype(jnp.int32))
    group_count = (valid_count + group_size - 1) // group_size

    def add_group(group_idx, group_total):
        picked = lax.dynamic_slice_in_dim(ordering, group_idx * group_size, group_size)
        within = group_idx * group_size + jnp.arange(group_size, dtype=jnp.int32) < valid_count
        picked = jnp.where(within, picked, slot_count)
        chosen = padded[picked]
        first_hat = hat_table(chosen[:, 0, :].reshape(-1), extent)
        second_hat = hat_table(chosen[:, 1, :].reshape(-1), extent)
        return group_total + lax.dot_general(
            first_hat, second_hat, (((0,), (0,)), ((), ())), preferred_element_type=jnp.float32
        )

    return lax.fori_loop(0, group_count, add_group, jnp.zeros((extent, extent), jnp.float32))


def shards(positions, destination, profile):
    row_count = lax.axis_size("row")
    col_count = lax.axis_size("col")
    tile_count = row_count * col_count
    block_count = positions.shape[0]
    ray_count = positions.shape[2]
    targets = destination[:, 0]
    block_labels = jnp.zeros((block_count,), jnp.int32)
    placed = targets * MOST + local_ranks(targets, tile_count)
    outgoing = (
        jnp.full((tile_count * MOST, 2, ray_count), -2.0, jnp.float32).at[placed].set(positions)
    )
    labels_out = jnp.full((tile_count * MOST,), -1, jnp.int32).at[placed].set(block_labels)
    received, recv_labels = (
        lax.all_to_all(
            outgoing.reshape(tile_count, MOST, 2, ray_count),
            ("row", "col"),
            split_axis=0,
            concat_axis=0,
            tiled=True,
        ),
        lax.all_to_all(
            labels_out.reshape(tile_count, MOST),
            ("row", "col"),
            split_axis=0,
            concat_axis=0,
            tiled=True,
        ),
    )
    received = received.reshape(tile_count * MOST, 2, ray_count)
    recv_labels = recv_labels.reshape(tile_count * MOST)
    tile_sum = deposit(received, recv_labels, 0, TILE)
    source_map = tile_sum.astype(jnp.bfloat16)
    extended = extended_2(source_map, (("row", 0), ("col", 1)), HALO)
    disc_side = 2 * HALO + 1
    span = jnp.arange(disc_side).astype(jnp.float32) - HALO
    inside = (span[:, None] ** 2 + span[None, :] ** 2 <= HALO * HALO).astype(jnp.float32)
    weights = profile * inside
    kernel = (weights / jnp.sum(weights)).astype(jnp.bfloat16)
    extent_wide = TILE + 2 * HALO
    lagged = (
        jnp.arange(extent_wide, dtype=jnp.int32)[:, None]
        - jnp.arange(TILE, dtype=jnp.int32)[None, :]
    )
    onehot = (lagged[None, :, :] == jnp.arange(disc_side, dtype=jnp.int32)[:, None, None]).astype(
        jnp.bfloat16
    )
    toeplitz = jnp.einsum("ab,bqj->qaj", kernel, onehot, preferred_element_type=jnp.float32).astype(
        jnp.bfloat16
    )
    lagged_sums = jnp.dot(
        extended,
        toeplitz.reshape(extent_wide, disc_side * TILE),
        preferred_element_type=jnp.float32,
    )
    stacked = lagged_sums.reshape(extent_wide * disc_side, TILE)
    column_index = jnp.arange(extent_wide * disc_side, dtype=jnp.int32)
    wide_row = column_index // disc_side
    disc_row = column_index % disc_side
    selector = (
        wide_row[None, :] == jnp.arange(TILE, dtype=jnp.int32)[:, None] + disc_row[None, :]
    ).astype(jnp.float32)
    convolved = jnp.dot(
        selector, stacked, precision=lax.Precision.HIGHEST, preferred_element_type=jnp.float32
    )
    density = block_count * ray_count / (TILE * TILE)
    return convolved / density


def solution(mesh):
    placed = (P(("maps", "row", "col"), None, None), P(("maps", "row", "col"), None), P())
    return jax.shard_map(
        shards, mesh=mesh, in_specs=placed, out_specs=P(("maps", "row"), "col"), check_vma=False
    )
```

profile of v0, /device:TPU:1, one launch (start us, length us, event | category | flops | bytes accessed | tf_op | source)
XLA Modules:
  0.0 69.0 jit_solution(3743885884673343755)
XLA Ops:
  0.0 0.7 %fusion.43 = s32[16,16]{1,0:T(8,128)S(1)} fusion(s32[16]{0:T(128)} %bitcast.29), kind=kLoop, calls=%fused_computation.65 | loop fusion | flops 512 | bytes 1088 | tf_op jit(solution)/shard_map/convert_element_type | solution.py:37
  0.8 0.8 %select_reduce_fusion = s32[16]{0:T(128)S(1)} fusion(s32[16,16]{1,0:T(8,128)S(1)} %reduce_window_sum.11, s32[16]{0:T(128)} %bitcast.30), kind=kLoop, calls=%fused_computation.63 | loop fusion | flops 1264 | bytes 1152 | tf_op jit(solution)/shard_map/reduce_sum | solution.py:39
  2.9 0.7 all_to_all.9
  3.6 7.3 %all-to-all-start = ((s32[16,1,4]{2,1,0:T(1,128)}), s32[16,1,4]{2,1,0:T(1,128)S(1)}, u32[]{:S(2)}, u32[]{:S(2)}) async-start(s32[16,1,4]{2,1,0:T(1,128)} %bitcast.5), calls=%async_computation | async-start | bytes 16384 | tf_op jit(solution)/shard_map/all_to_all | solution.py:86
  10.9 0.7 %broadcast_in_dim.17 = f32[64,2,384]{2,1,0:T(2,128)} broadcast(f32[]{:T(128)} %constant.75.clone.1), dimensions={} | broadcast | bytes 196612 | tf_op jit(solution)/shard_map/broadcast_in_dim | solution.py:75
  11.6 2.4 %scatter_fusion = f32[64,2,384]{2,1,0:T(2,128)} fusion(f32[64,2,384]{2,1,0:T(2,128)} %broadcast_in_dim.17, s32[16]{0:T(128)S(1)} %fusion.44, f32[16,2,384]{2,1,0:T(2,128)} %param.5), kind=kCustom, calls=%fused_computation.2 | custom fusion | bytes 147520 | tf_op jit(solution)/shard_map/scatter | solution.py:75
  14.0 2.6 %all-to-all-done = s32[16,1,4]{2,1,0:T(1,128)S(1)} async-done(((s32[16,1,4]{2,1,0:T(1,128)}), s32[16,1,4]{2,1,0:T(1,128)S(1)}, u32[]{:S(2)}, u32[]{:S(2)}) %all-to-all-start) | async-done | bytes 288 | tf_op jit(solution)/shard_map/all_to_all | solution.py:86
  16.6 4.0 %all-to-all-start.1 = ((f32[16,4,2,384]{3,2,1,0:T(2,128)}), f32[16,4,2,384]{3,2,1,0:T(2,128)S(1)}, u32[]{:S(2)}, u32[]{:S(2)}) async-start(f32[16,4,2,384]{3,2,1,0:T(2,128)} %bitcast.6), calls=%async_computation.1 | async-start | bytes 393216 | tf_op jit(solution)/shard_map/all_to_all | solution.py:79
  20.7 1.5 %fusion.35 = f32[]{:T(128)} fusion(f32[65,65]{1,0:T(8,128)} %param.7, f32[65]{0:T(128)S(1)} %add_multiply_fusion), kind=kLoop, calls=%fused_computation.55 | loop fusion | flops 16899 | bytes 17164 | tf_op jit(solution)/shard_map/reduce_sum | solution.py:103
  22.1 0.7 %fusion.42 = (s32[16,4]{1,0:T(8,128)S(1)}, s32[]{:T(128)}) fusion(s32[16,1,4]{2,1,0:T(1,128)S(1)} %all-to-all-done), kind=kLoop, calls=%fused_computation.62 | loop fusion | flops 319 | bytes 516 | tf_op jit(solution)/shard_map/convert_element_type | solution.py:46
  23.6 2.1 %sort.17 = (s32[64]{0:T(128)}, s32[64]{0:T(128)S(1)}) sort(s32[64]{0:T(128)S(1)} %reshape.77, s32[64]{0:T(128)S(1)} %iota.54), dimensions={0}, to_apply=%region_4.5 | sort | flops 384 | bytes 1024 | tf_op jit(solution)/shard_map/jit(argsort)/sort | solution.py:46
  25.7 2.9 %all-to-all-done.1 = f32[16,4,2,384]{3,2,1,0:T(2,128)S(1)} async-done(((f32[16,4,2,384]{3,2,1,0:T(2,128)}), f32[16,4,2,384]{3,2,1,0:T(2,128)S(1)}, u32[]{:S(2)}, u32[]{:S(2)}) %all-to-all-start.1) | async-done | bytes 196640 | tf_op jit(solution)/shard_map/all_to_all | solution.py:79
  28.6 3.7 %while.10 = (s32[]{:T(128)}, f32[128,128]{1,0:T(8,128)S(1)}, s32[]{:T(128)}, s32[]{:T(128)}, s32[80]{0:T(128)S(1)}, /*index=5*/f32[65,2,384]{2,1,0:T(2,128)S(1)}, s32[]{:T(128)}, s32[]{:T(128)}, s32[]{:T(128)}, s32[]{:T(128)}) while((s32[]{:T(128)}, f32[128,128]{1,0:T(8,128)S(1)}, s32[]{:T(128)}, s32[]{:T(128)}, s32[80]{0:T(128)S(1)}, ...), condition=%wide.region_7.8_spmd, body=%wide.region_6.7_spmd.sunk | while | flops 209208416 | bytes 381343 | solution.py:62
  28.7 0.7 %compare_select_fusion.4 = s32[16]{0:T(128)S(1)} fusion(s32[80]{0:T(128)S(1)} %get-tuple-element.129, s32[]{:T(128)S(6)} %select_n.57, s32[]{:T(128)} %get-tuple-element.128, s32[]{:T(128)S(6)} %mul.28), kind=kLoop, calls=%fused_computation.12.clone.1 | loop fusion | flops 96 | bytes 140 | tf_op jit(solution)/shard_map/while/body/select_n | solution.py:55
  30.0 2.3 %fusion.57 = f32[128,128]{1,0:T(8,128)S(1)} fusion(f32[128,128]{1,0:T(8,128)S(1)} %get-tuple-element.116, f32[6144]{0:T(1024)S(1)} %bitcast.28, f32[6144]{0:T(1024)S(1)} %bitcast.27), kind=kOutput, calls=%fused_computation.10.clone.1 | convolution fusion | flops 209207296 | bytes 180224 | tf_op jit(solution)/shard_map/while/body/dot_general | solution.py:58
  32.4 3.1 %collective-permute-start = (bf16[32,128]{1,0:T(8,128)(2,1)S(1)}, bf16[32,128]{1,0:T(8,128)(2,1)S(1)}, u32[]{:S(2)}, u32[]{:S(2)}) collective-permute-start(bf16[32,128]{1,0:T(8,128)(2,1)S(1)} %get-tuple-element.59), channel_id=1, source_target_pairs={{0,4},{4,8},{8,12},{1,5},{5,9},{9,13},{2,6},{6,10},{10,14},{3,7},{... | collective-permute-start | bytes 24584 | tf_op jit(solution)/shard_map/ppermute | solution.py:22
  35.5 1.9 %collective-permute-start.1 = (bf16[32,128]{1,0:T(8,128)(2,1)S(1)}, bf16[32,128]{1,0:T(8,128)(2,1)S(1)}, u32[]{:S(2)}, u32[]{:S(2)}) collective-permute-start(bf16[32,128]{1,0:T(8,128)(2,1)S(1)} %get-tuple-element.60), channel_id=1, source_target_pairs={{4,0},{8,4},{12,8},{5,1},{9,5},{13,9},{6,2},{10,6},{14,10},{7,3},{... | collective-permute-start | bytes 24584 | tf_op jit(solution)/shard_map/ppermute | solution.py:24
  37.4 2.7 %fusion.16 = bf16[192,128,65]{1,2,0:T(8,128)(2,1)S(1)} fusion(s32[192,128]{1,0:T(8,128)S(1)} %iota_subtract_fusion, f32[65,65]{1,0:T(8,128)S(1)} %copy-done, f32[]{:T(128)} %fusion.35, f32[65]{0:T(128)S(1)} %add_multiply_fusion), kind=kOutput, calls=%fused_computation.26 | convolution fusion | flops 210883200 | bytes 3310348 | tf_op jit(solution)/shard_map/ab,bqj->qaj/dot_general | solution.py:112
  40.5 2.4 %collective-permute-start.2 = (bf16[192,32]{1,0:T(8,128)(2,1)S(1)}, bf16[192,32]{1,0:T(8,128)(2,1)S(1)}, u32[]{:S(2)}, u32[]{:S(2)}) collective-permute-start(bf16[192,32]{1,0:T(8,128)(2,1)S(1)} %get-tuple-element.57), channel_id=1, source_target_pairs={{0,1},{1,2},{2,3},{4,5},{5,6},{6,7},{8,9},{9,10},{10,11},{12,13},{... | collective-permute-start | bytes 36872 | tf_op jit(solution)/shard_map/ppermute | solution.py:22
  43.0 1.3 %collective-permute-start.3 = (bf16[192,32]{1,0:T(8,128)(2,1)S(1)}, bf16[192,32]{1,0:T(8,128)(2,1)S(1)}, u32[]{:S(2)}, u32[]{:S(2)}) collective-permute-start(bf16[192,32]{1,0:T(8,128)(2,1)S(1)} %get-tuple-element.58), channel_id=1, source_target_pairs={{1,0},{2,1},{3,2},{5,4},{6,5},{7,6},{9,8},{10,9},{11,10},{13,12},{... | collective-permute-start | bytes 36872 | tf_op jit(solution)/shard_map/ppermute | solution.py:24
  44.3 5.9 %collective-permute-done.3 = bf16[192,32]{1,0:T(8,128)(2,1)S(1)} collective-permute-done((bf16[192,32]{1,0:T(8,128)(2,1)S(1)}, bf16[192,32]{1,0:T(8,128)(2,1)S(1)}, u32[]{:S(2)}, u32[]{:S(2)}) %collective-permute-start.3) | collective-permute-done | bytes 12320 | tf_op jit(solution)/shard_map/ppermute | solution.py:24
  50.3 3.7 %fusion.13 = f32[192,8320]{1,0:T(8,128)} fusion(bf16[24,8,65,128]{3,2,1,0:T(8,128)(2,1)S(1)} %bitcast.25, bf16[192,32]{1,0:T(8,128)(2,1)S(1)} %collective-permute-done.3, bf16[32,128]{1,0:T(8,128)(2,1)S(1)} %collective-permute-done.1, bf16[128,128]{1,0:T(8,128)(2,1)S(1)} %convert_element_type.50, bf16[32,128]{1,0:T(8,128)(2,1)S(1)} %collective-permute-done, ...), kind=kOutput, calls=%fused_computation.23 | convolution fusion | flops 613785600 | bytes 9658368 | tf_op jit(solution)/shard_map/dot_general | solution.py:115
  54.0 7.0 %reshape.76 = f32[12480,128]{1,0:T(8,128)} reshape(f32[192,8320]{1,0:T(8,128)} %fusion.13) | data formatting | bytes 12779520 | tf_op jit(solution)/shard_map/reshape | solution.py:120
  61.0 7.9 %fusion.17 = f32[128,128]{1,0:T(8,128)} fusion(f32[12480,128]{1,0:T(8,128)} %reshape.76, s32[12480]{0:T(1024)S(1)} %get-tuple-element.61, s32[12480]{0:T(1024)S(1)} %get-tuple-element.62), kind=kOutput, calls=%fused_computation.27 | convolution fusion | flops 2456879104 | bytes 6555136 | tf_op jit(solution)/shard_map/dot_general | solution.py:127
  (24 shorter events, 2.6 us)
Async XLA Ops:
  3.6 13.0 %all-to-all-start = ((s32[16,1,4]{2,1,0:T(1,128)}), s32[16,1,4]{2,1,0:T(1,128)S(1)}, u32[]{:S(2)}, u32[]{:S(2)}) async-start(s32[16,1,4]{2,1,0:T(1,128)} %bitcast.5), calls=%async_computation | async-start | bytes 16384 | tf_op jit(solution)/shard_map/all_to_all | solution.py:86
  16.6 11.9 %all-to-all-start.1 = ((f32[16,4,2,384]{3,2,1,0:T(2,128)}), f32[16,4,2,384]{3,2,1,0:T(2,128)S(1)}, u32[]{:S(2)}, u32[]{:S(2)}) async-start(f32[16,4,2,384]{3,2,1,0:T(2,128)} %bitcast.6), calls=%async_computation.1 | async-start | bytes 393216 | tf_op jit(solution)/shard_map/all_to_all | solution.py:79
  28.6 8.8 %copy-start = (f32[65,65]{1,0:T(8,128)S(1)}, f32[65,65]{1,0:T(8,128)}, u32[]{:S(2)}) copy-start(f32[65,65]{1,0:T(8,128)} %param.7) | copy-start | bytes 50704
  32.4 7.7 %collective-permute-start = (bf16[32,128]{1,0:T(8,128)(2,1)S(1)}, bf16[32,128]{1,0:T(8,128)(2,1)S(1)}, u32[]{:S(2)}, u32[]{:S(2)}) collective-permute-start(bf16[32,128]{1,0:T(8,128)(2,1)S(1)} %get-tuple-element.59), channel_id=1, source_target_pairs={{0,4},{4,8},{8,12},{1,5},{5,9},{9,13},{2,6},{6,10},{10,14},{3,7},{... | collective-permute-start | bytes 24584 | tf_op jit(solution)/shard_map/ppermute | solution.py:22
  35.5 5.0 %collective-permute-start.1 = (bf16[32,128]{1,0:T(8,128)(2,1)S(1)}, bf16[32,128]{1,0:T(8,128)(2,1)S(1)}, u32[]{:S(2)}, u32[]{:S(2)}) collective-permute-start(bf16[32,128]{1,0:T(8,128)(2,1)S(1)} %get-tuple-element.60), channel_id=1, source_target_pairs={{4,0},{8,4},{12,8},{5,1},{9,5},{13,9},{6,2},{10,6},{14,10},{7,3},{... | collective-permute-start | bytes 24584 | tf_op jit(solution)/shard_map/ppermute | solution.py:24
  40.5 3.8 %collective-permute-start.2 = (bf16[192,32]{1,0:T(8,128)(2,1)S(1)}, bf16[192,32]{1,0:T(8,128)(2,1)S(1)}, u32[]{:S(2)}, u32[]{:S(2)}) collective-permute-start(bf16[192,32]{1,0:T(8,128)(2,1)S(1)} %get-tuple-element.57), channel_id=1, source_target_pairs={{0,1},{1,2},{2,3},{4,5},{5,6},{6,7},{8,9},{9,10},{10,11},{12,13},{... | collective-permute-start | bytes 36872 | tf_op jit(solution)/shard_map/ppermute | solution.py:22
  43.0 7.3 %collective-permute-start.3 = (bf16[192,32]{1,0:T(8,128)(2,1)S(1)}, bf16[192,32]{1,0:T(8,128)(2,1)S(1)}, u32[]{:S(2)}, u32[]{:S(2)}) collective-permute-start(bf16[192,32]{1,0:T(8,128)(2,1)S(1)} %get-tuple-element.58), channel_id=1, source_target_pairs={{1,0},{2,1},{3,2},{5,4},{6,5},{7,6},{9,8},{10,9},{11,10},{13,12},{... | collective-permute-start | bytes 36872 | tf_op jit(solution)/shard_map/ppermute | solution.py:24
where the time goes:
time: 69.4 us; the launch traced here: 69 us
  starting transfers between devices  20 us (29%)
  matrix products  16.7 us (24%)
  local copies, waits for them, and re-layouts  12.4 us (18%)
  waiting for transfers between devices  11.7 us (17%)
  other arithmetic  7.26 us (10%)
  between operations  0.8 us (1%)
    dot_general x1, matrix products, shards(): jnp.dot(selector, stacked, precision=lax.Precision.HIGHEST, preferred_ele...  7.91 us
    all_to_all x1, starting transfers between devices, shards(): lax.all_to_all(labels_out.reshape(tile_count, MOST), ('row', 'col'), spli...  7.32 us
    reshape x1, local copies, waits for them, and re-layouts, shards(): stacked = lagged_sums.reshape(extent_wide * disc_side, TILE)  7.04 us
    ppermute x2, waiting for transfers between devices, extended_2(): lax.ppermute(head, axis, [((i + 1) % count, i) for i in range(ends)])  6.24 us
    ppermute x2, starting transfers between devices, extended_2(): lax.ppermute(tail, axis, [(i, (i + 1) % count) for i in range(ends)])  5.49 us
    all_to_all x1, starting transfers between devices, shards(): lax.all_to_all(outgoing.reshape(tile_count, MOST, 2, ray_count), ('row',...  4.01 us
    dot_general x1, matrix products, shards(): jnp.dot(extended, toeplitz.reshape(extent_wide, disc_side * TILE), prefer...  3.74 us
    ppermute x2, starting transfers between devices, extended_2(): lax.ppermute(head, axis, [((i + 1) % count, i) for i in range(ends)])  3.21 us
  transfers between devices with their start and end apart: 6, of which 4 were waited for; matrix products, arithmetic and copies ran while one was open for 15% of the time, Pallas kernels for 0%

commit v1 on v0

--- a/solution.py
+++ b/solution.py
@@ -69,31 +69,26 @@
     block_count = positions.shape[0]
     ray_count = positions.shape[2]
     targets = destination[:, 0]
-    block_labels = jnp.zeros((block_count,), jnp.int32)
-    placed = targets * MOST + local_ranks(targets, tile_count)
-    outgoing = (
-        jnp.full((tile_count * MOST, 2, ray_count), -2.0, jnp.float32).at[placed].set(positions)
-    )
-    labels_out = jnp.full((tile_count * MOST,), -1, jnp.int32).at[placed].set(block_labels)
-    received, recv_labels = (
-        lax.all_to_all(
+    if block_count <= 9 * MOST:
+        received = lax.all_gather(positions, ("row", "col"), axis=0, tiled=True)
+        recv_labels = lax.all_gather(targets, ("row", "col"), axis=0, tiled=True)
+        wanted = lax.axis_index(("row", "col"))
+    else:
+        placed = targets * MOST + local_ranks(targets, tile_count)
+        outgoing = (
+            jnp.full((tile_count * MOST, 2, ray_count), -2.0, jnp.float32).at[placed].set(positions)
+        )
+        received = lax.all_to_all(
             outgoing.reshape(tile_count, MOST, 2, ray_count),
             ("row", "col"),
             split_axis=0,
             concat_axis=0,
             tiled=True,
-        ),
-        lax.all_to_all(
-            labels_out.reshape(tile_count, MOST),
-            ("row", "col"),
-            split_axis=0,
-            concat_axis=0,
-            tiled=True,
-        ),
-    )
-    received = received.reshape(tile_count * MOST, 2, ray_count)
-    recv_labels = recv_labels.reshape(tile_count * MOST)
-    tile_sum = deposit(received, recv_labels, 0, TILE)
+        )
+        received = received.reshape(tile_count * MOST, 2, ray_count)
+        recv_labels = jnp.where(received[:, 0, 0] < -1.0, 1, 0)
+        wanted = 0
+    tile_sum = deposit(received, recv_labels, wanted, TILE)
     source_map = tile_sum.astype(jnp.bfloat16)
     extended = extended_2(source_map, (("row", 0), ("col", 1)), HALO)
     disc_side = 2 * HALO + 1

time: 69.4 us -> 101 us (1.46)
  the two profiles are of different devices: /device:TPU:1 before, /device:TPU:6 now
where the time goes in v1:
time: 101 us; the launch traced here: 100 us
  blocking collectives  49.7 us (49%)
  matrix products  19.1 us (19%)
  local copies, waits for them, and re-layouts  10.7 us (11%)
  starting transfers between devices  8.15 us (8%)
  other arithmetic  6.17 us (6%)
  waiting for transfers between devices  4.66 us (5%)
  between operations  1.52 us (2%)
    all_gather x1, blocking collectives, shards(): received = lax.all_gather(positions, ('row', 'col'), axis=0, tiled=True)  39.2 us
    unnamed x1, blocking collectives  10.6 us
    dot_general x1, matrix products, shards(): jnp.dot(selector, stacked, precision=lax.Precision.HIGHEST, preferred_ele...  7.91 us
    reshape x1, local copies, waits for them, and re-layouts, shards(): stacked = lagged_sums.reshape(extent_wide * disc_side, TILE)  7.04 us
    ppermute x2, starting transfers between devices, extended_2(): lax.ppermute(head, axis, [((i + 1) % count, i) for i in range(ends)])  4.93 us
    dot_general x2, matrix products, add_group(): lax.dot_general(first_hat, second_hat, (((0,), (0,)), ((), ())), preferre...  4.7 us
    ppermute x2, waiting for transfers between devices, extended_2(): lax.ppermute(head, axis, [((i + 1) % count, i) for i in range(ends)])  4.25 us
    dot_general x1, matrix products, shards(): jnp.dot(extended, toeplitz.reshape(extent_wide, disc_side * TILE), prefer...  3.74 us
  transfers between devices with their start and end apart: 4, of which 2 were waited for; matrix products, arithmetic and copies ran while one was open for 3% of the time, Pallas kernels for 0%

profile of v1, /device:TPU:6, one launch (start us, length us, event | category | flops | bytes accessed | tf_op | source)
XLA Modules:
  0.0 100.1 jit_solution(11754395395307393286)
XLA Ops:
  0.0 1.2 %dynamic-slice = u32[1]{0:T(128)} dynamic-slice(u32[32]{0:T(128)} %constant.86, u32[]{:T(128)S(6)} %add.88), dynamic_slice_sizes={1} | dynamic-slice | bytes 12
  1.9 0.8 bitcast_dynamic-update-slice_fusion
  2.7 10.6 %all-reduce.2 = s32[256]{0:T(256)S(1)} all-reduce(s32[256]{0:T(256)S(1)} %bitcast_dynamic-update-slice_fusion), channel_id=2, replica_groups=mesh['maps'=2,'row'=4,'col'=4] {'row','col'}, use_global_device_ids=true, to_apply=%add.2 | all-reduce | flops 256 | bytes 2048
  13.2 0.7 fusion.41
  14.7 39.2 %all_gather.7 = f32[256,2,384]{2,1,0:T(2,128)S(1)} all-gather(f32[16,2,384]{2,1,0:T(2,128)} %param.5), channel_id=1, replica_groups=mesh['maps'=2,'row'=4,'col'=4] {'row','col'}, dimensions={0}, use_global_device_ids=true | all-gather | bytes 835584 | tf_op jit(solution)/shard_map/all_gather | solution.py:73
  53.8 3.2 %sort.17 = (s32[256]{0:T(256)}, s32[256]{0:T(256)S(1)}) sort(s32[256]{0:T(256)S(1)} %compare_convert_fusion, s32[256]{0:T(256)S(1)} %iota.50), dimensions={0}, to_apply=%region_1.2 | sort | flops 2048 | bytes 4096 | tf_op jit(solution)/shard_map/jit(argsort)/sort | solution.py:46
  57.3 7.6 %while.10 = (s32[]{:T(128)}, f32[128,128]{1,0:T(8,128)S(1)}, s32[]{:T(128)}, s32[]{:T(128)}, s32[272]{0:T(512)S(1)}, /*index=5*/f32[257,2,384]{2,1,0:T(2,128)S(1)}, s32[]{:T(128)}, s32[]{:T(128)}, s32[]{:T(128)}, s32[]{:T(128)}) while((s32[]{:T(128)}, f32[128,128]{1,0:T(8,128)S(1)}, s32[]{:T(128)}, s32[]{:T(128)}, s32[272]{0:T(512)S(1)}, ...), condition=%wide.region_3.4_spmd, body=%wide.region_2.3_spmd.sunk | while | flops 209208416 | bytes 381343 | solution.py:62
  57.3 0.8 compare_select_fusion.3
  58.1 0.6 gather_fusion
  58.8 2.3 %fusion.52 = f32[128,128]{1,0:T(8,128)S(1)} fusion(f32[128,128]{1,0:T(8,128)S(1)} %get-tuple-element.114, f32[6144]{0:T(1024)S(1)} %bitcast.20, f32[6144]{0:T(1024)S(1)} %bitcast.19), kind=kOutput, calls=%fused_computation.8.clone.1 | convolution fusion | flops 209207296 | bytes 180224 | tf_op jit(solution)/shard_map/while/body/dot_general | solution.py:58
  61.2 0.8 compare_select_fusion.3
  61.9 0.6 gather_fusion
  62.6 2.4 %fusion.52 = f32[128,128]{1,0:T(8,128)S(1)} fusion(f32[128,128]{1,0:T(8,128)S(1)} %get-tuple-element.114, f32[6144]{0:T(1024)S(1)} %bitcast.20, f32[6144]{0:T(1024)S(1)} %bitcast.19), kind=kOutput, calls=%fused_computation.8.clone.1 | convolution fusion | flops 209207296 | bytes 180224 | tf_op jit(solution)/shard_map/while/body/dot_general | solution.py:58
  65.0 1.9 %collective-permute-start = (bf16[32,128]{1,0:T(8,128)(2,1)S(1)}, bf16[32,128]{1,0:T(8,128)(2,1)S(1)}, u32[]{:S(2)}, u32[]{:S(2)}) collective-permute-start(bf16[32,128]{1,0:T(8,128)(2,1)S(1)} %get-tuple-element.57), channel_id=1, source_target_pairs={{0,4},{4,8},{8,12},{1,5},{5,9},{9,13},{2,6},{6,10},{10,14},{3,7},{... | collective-permute-start | bytes 24584 | tf_op jit(solution)/shard_map/ppermute | solution.py:22
  66.9 3.6 %collective-permute-start.1 = (bf16[32,128]{1,0:T(8,128)(2,1)S(1)}, bf16[32,128]{1,0:T(8,128)(2,1)S(1)}, u32[]{:S(2)}, u32[]{:S(2)}) collective-permute-start(bf16[32,128]{1,0:T(8,128)(2,1)S(1)} %get-tuple-element.58), channel_id=1, source_target_pairs={{4,0},{8,4},{12,8},{5,1},{9,5},{13,9},{6,2},{10,6},{14,10},{7,3},{... | collective-permute-start | bytes 24584 | tf_op jit(solution)/shard_map/ppermute | solution.py:24
  70.6 0.7 fusion.35
  71.3 2.7 %fusion.16 = bf16[192,128,65]{1,2,0:T(8,128)(2,1)S(1)} fusion(s32[192,128]{1,0:T(8,128)S(1)} %iota_subtract_fusion, f32[65,65]{1,0:T(8,128)S(1)} %copy-done, f32[]{:T(128)} %fusion.35, f32[65]{0:T(128)S(1)} %add_multiply_fusion), kind=kOutput, calls=%fused_computation.24 | convolution fusion | flops 210883200 | bytes 3310348 | tf_op jit(solution)/shard_map/ab,bqj->qaj/dot_general | solution.py:107
  74.1 1.3 %collective-permute-start.2 = (bf16[192,32]{1,0:T(8,128)(2,1)S(1)}, bf16[192,32]{1,0:T(8,128)(2,1)S(1)}, u32[]{:S(2)}, u32[]{:S(2)}) collective-permute-start(bf16[192,32]{1,0:T(8,128)(2,1)S(1)} %get-tuple-element.55), channel_id=1, source_target_pairs={{0,1},{1,2},{2,3},{4,5},{5,6},{6,7},{8,9},{9,10},{10,11},{12,13},{... | collective-permute-start | bytes 36872 | tf_op jit(solution)/shard_map/ppermute | solution.py:22
  75.4 1.3 %collective-permute-start.3 = (bf16[192,32]{1,0:T(8,128)(2,1)S(1)}, bf16[192,32]{1,0:T(8,128)(2,1)S(1)}, u32[]{:S(2)}, u32[]{:S(2)}) collective-permute-start(bf16[192,32]{1,0:T(8,128)(2,1)S(1)} %get-tuple-element.56), channel_id=1, source_target_pairs={{1,0},{2,1},{3,2},{5,4},{6,5},{7,6},{9,8},{10,9},{11,10},{13,12},{... | collective-permute-start | bytes 36872 | tf_op jit(solution)/shard_map/ppermute | solution.py:24
  76.8 0.4 collective-permute-done.2
  77.2 4.3 %collective-permute-done.3 = bf16[192,32]{1,0:T(8,128)(2,1)S(1)} collective-permute-done((bf16[192,32]{1,0:T(8,128)(2,1)S(1)}, bf16[192,32]{1,0:T(8,128)(2,1)S(1)}, u32[]{:S(2)}, u32[]{:S(2)}) %collective-permute-start.3) | collective-permute-done | bytes 12320 | tf_op jit(solution)/shard_map/ppermute | solution.py:24
  81.4 3.7 %fusion.13 = f32[192,8320]{1,0:T(8,128)} fusion(bf16[24,8,65,128]{3,2,1,0:T(8,128)(2,1)S(1)} %bitcast.18, bf16[192,32]{1,0:T(8,128)(2,1)S(1)} %collective-permute-done.3, bf16[32,128]{1,0:T(8,128)(2,1)S(1)} %collective-permute-done.1, bf16[128,128]{1,0:T(8,128)(2,1)S(1)} %convert_element_type.40, bf16[32,128]{1,0:T(8,128)(2,1)S(1)} %collective-permute-done, ...), kind=kOutput, calls=%fused_computation.21 | convolution fusion | flops 613785600 | bytes 9658368 | tf_op jit(solution)/shard_map/dot_general | solution.py:110
  85.1 7.0 %reshape.54 = f32[12480,128]{1,0:T(8,128)} reshape(f32[192,8320]{1,0:T(8,128)} %fusion.13) | data formatting | bytes 12779520 | tf_op jit(solution)/shard_map/reshape | solution.py:115
  92.2 7.9 %fusion.17 = f32[128,128]{1,0:T(8,128)} fusion(f32[12480,128]{1,0:T(8,128)} %reshape.54, s32[12480]{0:T(1024)S(1)} %get-tuple-element.59, s32[12480]{0:T(1024)S(1)} %get-tuple-element.60), kind=kOutput, calls=%fused_computation.25 | convolution fusion | flops 2456879104 | bytes 6555136 | tf_op jit(solution)/shard_map/dot_general | solution.py:122
  (21 shorter events, 0.5 us)
Async XLA Ops:
  57.3 13.3 %copy-start = (f32[65,65]{1,0:T(8,128)S(1)}, f32[65,65]{1,0:T(8,128)}, u32[]{:S(2)}) copy-start(f32[65,65]{1,0:T(8,128)} %param.7) | copy-start | bytes 50704
  65.0 9.0 %collective-permute-start = (bf16[32,128]{1,0:T(8,128)(2,1)S(1)}, bf16[32,128]{1,0:T(8,128)(2,1)S(1)}, u32[]{:S(2)}, u32[]{:S(2)}) collective-permute-start(bf16[32,128]{1,0:T(8,128)(2,1)S(1)} %get-tuple-element.57), channel_id=1, source_target_pairs={{0,4},{4,8},{8,12},{1,5},{5,9},{9,13},{2,6},{6,10},{10,14},{3,7},{... | collective-permute-start | bytes 24584 | tf_op jit(solution)/shard_map/ppermute | solution.py:22
  66.9 7.1 %collective-permute-start.1 = (bf16[32,128]{1,0:T(8,128)(2,1)S(1)}, bf16[32,128]{1,0:T(8,128)(2,1)S(1)}, u32[]{:S(2)}, u32[]{:S(2)}) collective-permute-start(bf16[32,128]{1,0:T(8,128)(2,1)S(1)} %get-tuple-element.58), channel_id=1, source_target_pairs={{4,0},{8,4},{12,8},{5,1},{9,5},{13,9},{6,2},{10,6},{14,10},{7,3},{... | collective-permute-start | bytes 24584 | tf_op jit(solution)/shard_map/ppermute | solution.py:24
  74.1 3.0 %collective-permute-start.2 = (bf16[192,32]{1,0:T(8,128)(2,1)S(1)}, bf16[192,32]{1,0:T(8,128)(2,1)S(1)}, u32[]{:S(2)}, u32[]{:S(2)}) collective-permute-start(bf16[192,32]{1,0:T(8,128)(2,1)S(1)} %get-tuple-element.55), channel_id=1, source_target_pairs={{0,1},{1,2},{2,3},{4,5},{5,6},{6,7},{8,9},{9,10},{10,11},{12,13},{... | collective-permute-start | bytes 36872 | tf_op jit(solution)/shard_map/ppermute | solution.py:22
  75.4 6.0 %collective-permute-start.3 = (bf16[192,32]{1,0:T(8,128)(2,1)S(1)}, bf16[192,32]{1,0:T(8,128)(2,1)S(1)}, u32[]{:S(2)}, u32[]{:S(2)}) collective-permute-start(bf16[192,32]{1,0:T(8,128)(2,1)S(1)} %get-tuple-element.56), channel_id=1, source_target_pairs={{1,0},{2,1},{3,2},{5,4},{6,5},{7,6},{9,8},{10,9},{11,10},{13,12},{... | collective-permute-start | bytes 36872 | tf_op jit(solution)/shard_map/ppermute | solution.py:24

commit v2 on v1

v2 whole, which is shorter than its diff:
```python
import functools

import jax
import jax.numpy as jnp
from jax import lax
from jax.experimental import pallas as pl
from jax.experimental.pallas import tpu as pltpu
from jax.sharding import PartitionSpec as P

TILE = 128
HALO = 32
MOST = 4
DISC = 2 * HALO + 1
STEP = 16
LONG = TILE + STEP
TURNS = 2 * HALO // STEP
WIDE = TILE + 2 * HALO
DEPTH = TURNS * WIDE

VMEM = pl.BlockSpec(memory_space=pltpu.VMEM)
SMEM = pl.BlockSpec(memory_space=pltpu.SMEM)


def place_kernel(dest_ref, rays_ref, out_ref, count_ref):
    blocks = rays_ref.shape[0]
    tiles = out_ref.shape[0] // MOST
    empty = jnp.full((MOST,) + rays_ref.shape[1:], -2.0, jnp.float32)

    def clear(t, carry):
        count_ref[t] = 0
        out_ref[pl.ds(t * MOST, MOST)] = empty
        return carry

    lax.fori_loop(0, tiles, clear, 0)

    def place(b, carry):
        t = dest_ref[b, 0]
        rank = count_ref[t]
        count_ref[t] = rank + 1
        out_ref[t * MOST + rank] = rays_ref[b]
        return carry

    lax.fori_loop(0, blocks, place, 0)


def table_kernel(profile_ref, pairs_ref, last_ref):
    a = lax.broadcasted_iota(jnp.int32, (DISC, DISC), 0) - HALO
    c = lax.broadcasted_iota(jnp.int32, (DISC, DISC), 1) - HALO
    weights = jnp.where(a * a + c * c <= HALO * HALO, profile_ref[...], 0.0)
    kernel = (weights / jnp.sum(weights)).astype(jnp.bfloat16)
    source = lax.broadcasted_iota(jnp.int32, (DISC, 2 * TILE), 0)
    target = lax.broadcasted_iota(jnp.int32, (DISC, 2 * TILE), 1)
    mirror = jnp.where((source + target) % (2 * TILE) == 0, 1.0, 0.0).astype(jnp.bfloat16)
    mirrored = jnp.dot(kernel, mirror, preferred_element_type=jnp.float32)

    def band(row, first, rows):
        wide = jnp.broadcast_to(mirrored[row : row + 1, :], (rows, 2 * TILE))
        rolled = pltpu.roll(wide, first, 1, stride=1, stride_axis=0)
        return rolled[:, :TILE].astype(jnp.bfloat16)

    for s in range(STEP):
        half = pl.ds((s % 2) * TILE, TILE)
        for u in range(TURNS):
            row = u * STEP + s
            pairs_ref[s // 2, pl.ds(u * TILE, TILE), half] = band(row, HALO, TILE)
            side = TURNS * TILE + u * 2 * HALO
            pairs_ref[s // 2, pl.ds(side, HALO), half] = band(row, 0, HALO)
            pairs_ref[s // 2, pl.ds(side + HALO, HALO), half] = band(row, HALO + TILE, HALO)
    last_ref[:TILE, :] = band(2 * HALO, HALO, TILE)
    last_ref[TILE : TILE + HALO, :] = band(2 * HALO, 0, HALO)
    last_ref[TILE + HALO :, :] = band(2 * HALO, HALO + TILE, HALO)


def deposit_kernel(rows_axis, cols_axis, rays_ref, tile_ref, send_ref):
    slots, _, rays = rays_ref.shape
    cell = lax.broadcasted_iota(jnp.int32, (TILE, rays), 0).astype(jnp.float32)

    def add(group, total):
        for k in range(MOST):
            block = rays_ref[group * MOST + k]
            first = jnp.maximum(0.0, 1.0 - jnp.abs(block[0:1, :] - cell)).astype(jnp.bfloat16)
            second = jnp.maximum(0.0, 1.0 - jnp.abs(block[1:2, :] - cell)).astype(jnp.bfloat16)
            total = total + lax.dot_general(
                first, second, (((1,), (1,)), ((), ())), preferred_element_type=jnp.float32
            )
        return total

    total = lax.fori_loop(0, slots // MOST, add, jnp.zeros((TILE, TILE), jnp.float32))
    tile = total.astype(jnp.bfloat16)
    turned = tile.astype(jnp.float32).T.astype(jnp.bfloat16)
    tile_ref[...] = tile
    send_ref[...] = jnp.zeros(send_ref.shape, jnp.bfloat16)
    row_count, col_count = lax.axis_size(rows_axis), lax.axis_size(cols_axis)
    row, col = lax.axis_index(rows_axis), lax.axis_index(cols_axis)
    low, high = slice(0, HALO), slice(TILE - HALO, TILE)
    for dr in (-1, 0, 1):
        for dc in (-1, 0, 1):
            if dr == 0 and dc == 0:
                continue
            if dr != 0:
                piece = tile[low if dr < 0 else high, :]
            else:
                piece = turned[low if dc < 0 else high, :]
            r, c = row + dr, col + dc

            @pl.when((r >= 0) & (r < row_count) & (c >= 0) & (c < col_count))
            def _(r=r, c=c, piece=piece):
                send_ref[r * col_count + c] = piece


def spread_kernel(rows_axis, cols_axis, scale, tile_ref, got_ref, pairs_ref, last_ref, out_ref,
                  own, side, left):
    row_count, col_count = lax.axis_size(rows_axis), lax.axis_size(cols_axis)
    row, col = lax.axis_index(rows_axis), lax.axis_index(cols_axis)

    def fetch(dr, dc):
        r, c = row + dr, col + dc
        inside = (r >= 0) & (r < row_count) & (c >= 0) & (c < col_count)
        index = jnp.where(inside, r * col_count + c, 0)
        piece = got_ref[index].astype(jnp.float32)
        return jnp.where(inside, piece, 0.0)

    own[:HALO, :] = fetch(-1, 0).astype(jnp.bfloat16)
    own[HALO : HALO + TILE, :] = tile_ref[...]
    own[HALO + TILE :, :] = fetch(1, 0).astype(jnp.bfloat16)
    for dr, at in ((-1, 0), (1, HALO + TILE)):
        lower = fetch(dr, -1)[:, TILE - HALO :]
        upper = fetch(dr, 1)[:, :HALO]
        side[at : at + HALO, :] = jnp.concatenate([lower, upper], axis=1).astype(jnp.bfloat16)
    strips = jnp.concatenate([fetch(0, -1), fetch(0, 1)], axis=0).T
    side[HALO : HALO + TILE, :] = strips.astype(jnp.bfloat16)
    for u in range(TURNS):
        left[:, u * TILE : (u + 1) * TILE] = own[u * STEP : u * STEP + LONG, :]
        at = TURNS * TILE + u * 2 * HALO
        left[:, at : at + 2 * HALO] = side[u * STEP : u * STEP + LONG, :]
    total = jnp.dot(own[2 * HALO :, :], last_ref[:TILE, :], preferred_element_type=jnp.float32)
    total = total + jnp.dot(
        side[2 * HALO :, :], last_ref[TILE:, :], preferred_element_type=jnp.float32
    )
    for p in range(STEP // 2):
        both = jnp.dot(left[...], pairs_ref[p], preferred_element_type=jnp.float32)
        total = total + both[2 * p : 2 * p + TILE, :TILE]
        total = total + both[2 * p + 1 : 2 * p + 1 + TILE, TILE:]
    out_ref[...] = total / scale


def shards(positions, destination, profile):
    tiles = lax.axis_size("row") * lax.axis_size("col")
    blocks, _, rays = positions.shape
    limit = pltpu.CompilerParams(vmem_limit_bytes=32 * 1024 * 1024)
    outgoing = pl.pallas_call(
        place_kernel,
        out_shape=jax.ShapeDtypeStruct((tiles * MOST, 2, rays), jnp.float32),
        in_specs=[SMEM, VMEM],
        out_specs=VMEM,
        scratch_shapes=[pltpu.SMEM((tiles,), jnp.int32)],
        compiler_params=limit,
        name="place",
    )(destination, positions)
    received = lax.all_to_all(
        outgoing.reshape(tiles, MOST, 2, rays), ("row", "col"), split_axis=0, concat_axis=0, tiled=True
    ).reshape(tiles * MOST, 2, rays)
    pairs, last = pl.pallas_call(
        table_kernel,
        out_shape=(
            jax.ShapeDtypeStruct((STEP // 2, DEPTH, 2 * TILE), jnp.bfloat16),
            jax.ShapeDtypeStruct((WIDE, TILE), jnp.bfloat16),
        ),
        in_specs=[VMEM],
        out_specs=(VMEM, VMEM),
        compiler_params=limit,
        cost_estimate=pl.CostEstimate(flops=10_000_000, bytes_accessed=6_000_000, transcendentals=0),
        name="table",
    )(profile)
    tile, send = pl.pallas_call(
        functools.partial(deposit_kernel, "row", "col"),
        out_shape=(
            jax.ShapeDtypeStruct((TILE, TILE), jnp.bfloat16),
            jax.ShapeDtypeStruct((tiles, HALO, TILE), jnp.bfloat16),
        ),
        in_specs=[VMEM],
        out_specs=(VMEM, VMEM),
        compiler_params=limit,
        name="deposit",
    )(received)
    got = lax.all_to_all(send, ("row", "col"), split_axis=0, concat_axis=0, tiled=True)
    scale = blocks * rays / (TILE * TILE)
    return pl.pallas_call(
        functools.partial(spread_kernel, "row", "col", scale),
        out_shape=jax.ShapeDtypeStruct((TILE, TILE), jnp.float32),
        in_specs=[VMEM, VMEM, VMEM, VMEM],
        out_specs=VMEM,
        scratch_shapes=[
            pltpu.VMEM((WIDE, TILE), jnp.bfloat16),
            pltpu.VMEM((WIDE, 2 * HALO), jnp.bfloat16),
            pltpu.VMEM((LONG, DEPTH), jnp.bfloat16),
        ],
        compiler_params=limit,
        name="spread",
    )(tile, got, pairs, last)


def solution(mesh):
    placed = (P(("maps", "row", "col"), None, None), P(("maps", "row", "col"), None), P())
    return jax.shard_map(
        shards, mesh=mesh, in_specs=placed, out_specs=P(("maps", "row"), "col"), check_vma=False
    )
```

time: 101 us -> 37.3 us (0.37)
  the two profiles are of different devices: /device:TPU:6 before, /device:TPU:1 now
where the time goes in v2:
time: 37.3 us; the launch traced here: 36.7 us
  blocking collectives  15 us (40%)
  Pallas kernels  10.4 us (28%)
  waiting for transfers between devices  4.86 us (13%)
  starting transfers between devices  4.15 us (11%)
  local copies, waits for them, and re-layouts  2.29 us (6%)
    all_to_all x1, blocking collectives, shards(): lax.all_to_all(outgoing.reshape(tiles, MOST, 2, rays), ('row', 'col'), sp...  15 us
    pallas_call x1, Pallas kernels, shards(): pl.pallas_call(functools.partial(deposit_kernel, 'row', 'col'), out_shape...  6.64 us
    all_to_all x1, waiting for transfers between devices, shards(): lax.all_to_all(send, ('row', 'col'), split_axis=0, concat_axis=0, tiled=T...  4.86 us
    all_to_all x1, starting transfers between devices, shards(): lax.all_to_all(send, ('row', 'col'), split_axis=0, concat_axis=0, tiled=T...  4.15 us
    unnamed x5, local copies, waits for them, and re-layouts  2.29 us
    pallas_call x1, Pallas kernels, shards(): pl.pallas_call(table_kernel, out_shape=(jax.ShapeDtypeStruct((STEP // 2,...  1.42 us
    pallas_call x1, Pallas kernels, shards(): pl.pallas_call(functools.partial(spread_kernel, 'row', 'col', scale), out...  1.39 us
    pallas_call x1, Pallas kernels, shards(): pl.pallas_call(place_kernel, out_shape=jax.ShapeDtypeStruct((tiles * MOST...  0.92 us
  transfers between devices with their start and end apart: 1, of which 1 were waited for; matrix products, arithmetic and copies ran while one was open for 0% of the time, Pallas kernels for 4%

profile of v2, /device:TPU:1, one launch (start us, length us, event | category | flops | bytes accessed | tf_op | source)
XLA Modules:
  0.0 36.7 jit_solution(543588889892807919)
XLA Ops:
  0.0 0.7 %copy.4.dest_ref = s32[16,1]{1,0:T(8,128)S(1)} copy(s32[16,1]{0,1:T(1,128)} %param.4) | data formatting | bytes 128 | tf_op args[1]
  0.7 0.0 copy-start
  0.7 0.8 %copy-done = f32[16,2,384]{2,1,0:T(2,128)S(1)} copy-done((f32[16,2,384]{2,1,0:T(2,128)S(1)}, f32[16,2,384]{2,1,0:T(2,128)}, u32[]{:S(2)}) %copy-start) | copy-done | bytes 49176
  1.5 0.9 %place.1 = f32[64,2,384]{2,1,0:T(2,128)S(1)} custom-call(s32[16,1]{1,0:T(8,128)S(1)} %copy.4.dest_ref, f32[16,2,384]{2,1,0:T(2,128)S(1)} %copy-done), custom_call_target="tpu_custom_call" | custom-call | tf_op jit(solution)/shard_map/place/pallas_call | solution.py:151
  2.5 15.0 %all_to_all.10 = f32[16,4,2,384]{3,2,1,0:T(2,128)S(1)} all-to-all(f32[16,4,2,384]{3,2,1,0:T(2,128)S(1)} %bitcast.3), channel_id=1, replica_groups=mesh['maps'=2,'row'=4,'col'=4] {'row','col'}, dimensions={0} | all-to-all | bytes 393216 | tf_op jit(solution)/shard_map/all_to_all | solution.py:160
  17.4 6.6 %deposit.1 = (bf16[128,128]{1,0:T(8,128)(2,1)S(1)}, bf16[16,32,128]{2,1,0:T(8,128)(2,1)}) custom-call(f32[64,2,384]{2,1,0:T(2,128)S(1)} %bitcast.2), custom_call_target="tpu_custom_call" | custom-call | tf_op jit(solution)/shard_map/deposit/pallas_call | solution.py:175
  24.1 4.1 %all-to-all-start.1 = ((bf16[16,32,128]{2,1,0:T(8,128)(2,1)}), bf16[16,32,128]{2,1,0:T(8,128)(2,1)S(1)}, u32[]{:S(2)}, u32[]{:S(2)}) async-start(bf16[16,32,128]{2,1,0:T(8,128)(2,1)} %get-tuple-element.10), calls=%async_computation.1 | async-start | bytes 262144 | tf_op jit(solution)/shard_map/all_to_all | solution.py:186
  28.2 0.0 copy-start.1
  28.2 0.8 %copy-done.1 = f32[65,65]{1,0:T(8,128)S(1)} copy-done((f32[65,65]{1,0:T(8,128)S(1)}, f32[65,65]{1,0:T(8,128)}, u32[]{:S(2)}) %copy-start.1) | copy-done | bytes 16924
  29.0 1.4 %table.1 = (bf16[8,768,256]{2,1,0:T(8,128)(2,1)S(1)}, bf16[192,128]{1,0:T(8,128)(2,1)S(1)}) custom-call(f32[65,65]{1,0:T(8,128)S(1)} %copy-done.1), custom_call_target="tpu_custom_call" | custom-call | flops 10000000 | bytes 6000000 | tf_op jit(solution)/shard_map/table/pallas_call | solution.py:163
  30.4 4.9 %all-to-all-done.1.got_ref = bf16[16,32,128]{2,1,0:T(8,128)(2,1)S(1)} async-done(((bf16[16,32,128]{2,1,0:T(8,128)(2,1)}), bf16[16,32,128]{2,1,0:T(8,128)(2,1)S(1)}, u32[]{:S(2)}, u32[]{:S(2)}) %all-to-all-start.1) | async-done | bytes 131104 | tf_op jit(solution)/shard_map/all_to_all | solution.py:186
  35.3 1.4 %spread.1 = f32[128,128]{1,0:T(8,128)} custom-call(bf16[128,128]{1,0:T(8,128)(2,1)S(1)} %get-tuple-element.9.tile_ref, bf16[16,32,128]{2,1,0:T(8,128)(2,1)S(1)} %all-to-all-done.1.got_ref, bf16[8,768,256]{2,1,0:T(8,128)(2,1)S(1)} %get-tuple-element.11.pairs_ref, bf16[192,128]{1,0:T(8,128)(2,1)S(1)} %get-tuple-element.12.last_ref), custom_call_target="tpu_custom_call" | custom-call | tf_op jit(solution)/shard_map/spread/pallas_call | solution.py:188
Async XLA Ops:
  0.7 0.8 %copy-start = (f32[16,2,384]{2,1,0:T(2,128)S(1)}, f32[16,2,384]{2,1,0:T(2,128)}, u32[]{:S(2)}) copy-start(f32[16,2,384]{2,1,0:T(2,128)} %rays_ref.1) | copy-start | bytes 147460
  24.1 11.2 %all-to-all-start.1 = ((bf16[16,32,128]{2,1,0:T(8,128)(2,1)}), bf16[16,32,128]{2,1,0:T(8,128)(2,1)S(1)}, u32[]{:S(2)}, u32[]{:S(2)}) async-start(bf16[16,32,128]{2,1,0:T(8,128)(2,1)} %get-tuple-element.10), calls=%async_computation.1 | async-start | bytes 262144 | tf_op jit(solution)/shard_map/all_to_all | solution.py:186
  28.2 0.8 %copy-start.1 = (f32[65,65]{1,0:T(8,128)S(1)}, f32[65,65]{1,0:T(8,128)}, u32[]{:S(2)}) copy-start(f32[65,65]{1,0:T(8,128)} %profile_ref.1) | copy-start | bytes 50704

commit v3 on v2

--- a/solution.py
+++ b/solution.py
@@ -16,6 +16,8 @@
 TURNS = 2 * HALO // STEP
 WIDE = TILE + 2 * HALO
 DEPTH = TURNS * WIDE
+BITS = 16
+BATCH = 8
 
 VMEM = pl.BlockSpec(memory_space=pltpu.VMEM)
 SMEM = pl.BlockSpec(memory_space=pltpu.SMEM)
@@ -71,21 +73,49 @@
     last_ref[TILE + HALO :, :] = band(2 * HALO, HALO + TILE, HALO)
 
 
-def deposit_kernel(rows_axis, cols_axis, rays_ref, tile_ref, send_ref):
+def hats(coords, cell):
+    low = jnp.floor(coords)
+    near = jnp.maximum(0.0, 1.0 - jnp.abs(coords - low)).astype(jnp.bfloat16)
+    far = jnp.maximum(0.0, 1.0 - jnp.abs(coords - (low + 1.0))).astype(jnp.bfloat16)
+    low = low.astype(jnp.bfloat16)
+    zero = jnp.zeros((), jnp.bfloat16)
+    one = jnp.ones((), jnp.bfloat16)
+    return jnp.where(cell == low, near, jnp.where(cell == low + one, far, zero))
+
+
+def deposit_kernel(rows_axis, cols_axis, rays_ref, tile_ref, send_ref, list_ref):
     slots, _, rays = rays_ref.shape
+    lane = lax.broadcasted_iota(jnp.int32, (BITS, 128), 1)
+    place = lax.broadcasted_iota(jnp.int32, (BITS, 128), 0)
+    power = jnp.where(lane == 0, (1 << place).astype(jnp.float32), 0.0)
+    count, empty = jnp.int32(0), jnp.int32(0)
+    for at in range(0, slots, BITS):
+        heads = rays_ref[at : at + BITS, 0, :128]
+        mask = jnp.sum(jnp.where(heads > -1.0, power, 0.0)).astype(jnp.int32)
+        for k in range(BITS):
+            filled = (mask >> k) & 1
+            list_ref[count] = at + k
+            empty = jnp.where(filled == 1, empty, at + k)
+            count = count + filled
+    for k in range(BATCH):
+        list_ref[count + k] = empty
+
     cell = lax.broadcasted_iota(jnp.int32, (TILE, rays), 0).astype(jnp.float32)
-
-    def add(group, total):
-        for k in range(MOST):
-            block = rays_ref[group * MOST + k]
-            first = jnp.maximum(0.0, 1.0 - jnp.abs(block[0:1, :] - cell)).astype(jnp.bfloat16)
-            second = jnp.maximum(0.0, 1.0 - jnp.abs(block[1:2, :] - cell)).astype(jnp.bfloat16)
+    cell = cell.astype(jnp.bfloat16)
+
+    def add(batch, total):
+        for k in range(BATCH):
+            block = rays_ref[list_ref[batch * BATCH + k]]
             total = total + lax.dot_general(
-                first, second, (((1,), (1,)), ((), ())), preferred_element_type=jnp.float32
+                hats(block[0:1, :], cell),
+                hats(block[1:2, :], cell),
+                (((1,), (1,)), ((), ())),
+                preferred_element_type=jnp.float32,
             )
         return total
 
-    total = lax.fori_loop(0, slots // MOST, add, jnp.zeros((TILE, TILE), jnp.float32))
+    batches = (count + BATCH - 1) // BATCH
+    total = lax.fori_loop(0, batches, add, jnp.zeros((TILE, TILE), jnp.float32))
     tile = total.astype(jnp.bfloat16)
     turned = tile.astype(jnp.float32).T.astype(jnp.bfloat16)
     tile_ref[...] = tile
@@ -180,6 +210,7 @@
         ),
         in_specs=[VMEM],
         out_specs=(VMEM, VMEM),
+        scratch_shapes=[pltpu.SMEM((tiles * MOST + BATCH,), jnp.int32)],
         compiler_params=limit,
         name="deposit",
     )(received)

time: 37.3 us -> 33.1 us (0.89)
  Pallas kernels: 10.4 us -> 5.81 us
  starting transfers between devices: 4.15 us -> 4.74 us
    pallas_call x1, Pallas kernels: 6.64 us -> 2.07 us  [shards(): pl.pallas_call(functools.partial(deposit_kernel, 'row', 'col'), out_shape...]
    all_to_all x1, starting transfers between devices: 4.15 us -> 4.74 us  [shards(): lax.all_to_all(send, ('row', 'col'), split_axis=0, concat_axis=0, tiled=T...]
where the time goes in v3:
time: 33.1 us; the launch traced here: 32.7 us
  blocking collectives  15 us (45%)
  Pallas kernels  5.81 us (18%)
  waiting for transfers between devices  4.91 us (15%)
  starting transfers between devices  4.74 us (14%)
  local copies, waits for them, and re-layouts  2.29 us (7%)
    all_to_all x1, blocking collectives, shards(): lax.all_to_all(outgoing.reshape(tiles, MOST, 2, rays), ('row', 'col'), sp...  15 us
    all_to_all x1, waiting for transfers between devices, shards(): lax.all_to_all(send, ('row', 'col'), split_axis=0, concat_axis=0, tiled=T...  4.91 us
    all_to_all x1, starting transfers between devices, shards(): lax.all_to_all(send, ('row', 'col'), split_axis=0, concat_axis=0, tiled=T...  4.74 us
    unnamed x5, local copies, waits for them, and re-layouts  2.29 us
    pallas_call x1, Pallas kernels, shards(): pl.pallas_call(functools.partial(deposit_kernel, 'row', 'col'), out_shape...  2.07 us
    pallas_call x1, Pallas kernels, shards(): pl.pallas_call(table_kernel, out_shape=(jax.ShapeDtypeStruct((STEP // 2,...  1.42 us
    pallas_call x1, Pallas kernels, shards(): pl.pallas_call(functools.partial(spread_kernel, 'row', 'col', scale), out...  1.39 us
    pallas_call x1, Pallas kernels, shards(): pl.pallas_call(place_kernel, out_shape=jax.ShapeDtypeStruct((tiles * MOST...  0.92 us
  transfers between devices with their start and end apart: 1, of which 1 were waited for; matrix products, arithmetic and copies ran while one was open for 0% of the time, Pallas kernels for 4%

profile of v3, /device:TPU:1, one launch (start us, length us, event | category | flops | bytes accessed | tf_op | source)
XLA Modules:
  0.0 32.7 jit_solution(13762082213670203301)
XLA Ops:
  0.0 0.7 %copy.4.dest_ref = s32[16,1]{1,0:T(8,128)S(1)} copy(s32[16,1]{0,1:T(1,128)} %param.4) | data formatting | bytes 128 | tf_op args[1]
  0.7 0.0 copy-start
  0.7 0.8 %copy-done = f32[16,2,384]{2,1,0:T(2,128)S(1)} copy-done((f32[16,2,384]{2,1,0:T(2,128)S(1)}, f32[16,2,384]{2,1,0:T(2,128)}, u32[]{:S(2)}) %copy-start) | copy-done | bytes 49176
  1.5 0.9 %place.1 = f32[64,2,384]{2,1,0:T(2,128)S(1)} custom-call(s32[16,1]{1,0:T(8,128)S(1)} %copy.4.dest_ref, f32[16,2,384]{2,1,0:T(2,128)S(1)} %copy-done), custom_call_target="tpu_custom_call" | custom-call | tf_op jit(solution)/shard_map/place/pallas_call | solution.py:181
  2.5 15.0 %all_to_all.10 = f32[16,4,2,384]{3,2,1,0:T(2,128)S(1)} all-to-all(f32[16,4,2,384]{3,2,1,0:T(2,128)S(1)} %bitcast.3), channel_id=1, replica_groups=mesh['maps'=2,'row'=4,'col'=4] {'row','col'}, dimensions={0} | all-to-all | bytes 393216 | tf_op jit(solution)/shard_map/all_to_all | solution.py:190
  17.4 2.1 %deposit.1 = (bf16[128,128]{1,0:T(8,128)(2,1)S(1)}, bf16[16,32,128]{2,1,0:T(8,128)(2,1)}) custom-call(f32[64,2,384]{2,1,0:T(2,128)S(1)} %bitcast.2), custom_call_target="tpu_custom_call" | custom-call | tf_op jit(solution)/shard_map/deposit/pallas_call | solution.py:205
  19.5 4.7 %all-to-all-start.1 = ((bf16[16,32,128]{2,1,0:T(8,128)(2,1)}), bf16[16,32,128]{2,1,0:T(8,128)(2,1)S(1)}, u32[]{:S(2)}, u32[]{:S(2)}) async-start(bf16[16,32,128]{2,1,0:T(8,128)(2,1)} %get-tuple-element.10), calls=%async_computation.1 | async-start | bytes 262144 | tf_op jit(solution)/shard_map/all_to_all | solution.py:217
  24.2 0.0 copy-start.1
  24.2 0.8 %copy-done.1 = f32[65,65]{1,0:T(8,128)S(1)} copy-done((f32[65,65]{1,0:T(8,128)S(1)}, f32[65,65]{1,0:T(8,128)}, u32[]{:S(2)}) %copy-start.1) | copy-done | bytes 16924
  25.0 1.4 %table.1 = (bf16[8,768,256]{2,1,0:T(8,128)(2,1)S(1)}, bf16[192,128]{1,0:T(8,128)(2,1)S(1)}) custom-call(f32[65,65]{1,0:T(8,128)S(1)} %copy-done.1), custom_call_target="tpu_custom_call" | custom-call | flops 10000000 | bytes 6000000 | tf_op jit(solution)/shard_map/table/pallas_call | solution.py:193
  26.4 4.9 %all-to-all-done.1.got_ref = bf16[16,32,128]{2,1,0:T(8,128)(2,1)S(1)} async-done(((bf16[16,32,128]{2,1,0:T(8,128)(2,1)}), bf16[16,32,128]{2,1,0:T(8,128)(2,1)S(1)}, u32[]{:S(2)}, u32[]{:S(2)}) %all-to-all-start.1) | async-done | bytes 131104 | tf_op jit(solution)/shard_map/all_to_all | solution.py:217
  31.3 1.4 %spread.1 = f32[128,128]{1,0:T(8,128)} custom-call(bf16[128,128]{1,0:T(8,128)(2,1)S(1)} %get-tuple-element.9.tile_ref, bf16[16,32,128]{2,1,0:T(8,128)(2,1)S(1)} %all-to-all-done.1.got_ref, bf16[8,768,256]{2,1,0:T(8,128)(2,1)S(1)} %get-tuple-element.11.pairs_ref, bf16[192,128]{1,0:T(8,128)(2,1)S(1)} %get-tuple-element.12.last_ref), custom_call_target="tpu_custom_call" | custom-call | tf_op jit(solution)/shard_map/spread/pallas_call | solution.py:219
Async XLA Ops:
  0.7 0.8 %copy-start = (f32[16,2,384]{2,1,0:T(2,128)S(1)}, f32[16,2,384]{2,1,0:T(2,128)}, u32[]{:S(2)}) copy-start(f32[16,2,384]{2,1,0:T(2,128)} %rays_ref.1) | copy-start | bytes 147460
  19.5 11.8 %all-to-all-start.1 = ((bf16[16,32,128]{2,1,0:T(8,128)(2,1)}), bf16[16,32,128]{2,1,0:T(8,128)(2,1)S(1)}, u32[]{:S(2)}, u32[]{:S(2)}) async-start(bf16[16,32,128]{2,1,0:T(8,128)(2,1)} %get-tuple-element.10), calls=%async_computation.1 | async-start | bytes 262144 | tf_op jit(solution)/shard_map/all_to_all | solution.py:217
  24.2 0.8 %copy-start.1 = (f32[65,65]{1,0:T(8,128)S(1)}, f32[65,65]{1,0:T(8,128)}, u32[]{:S(2)}) copy-start(f32[65,65]{1,0:T(8,128)} %profile_ref.1) | copy-start | bytes 50704

commit v4 on v3

--- a/solution.py
+++ b/solution.py
@@ -83,7 +83,7 @@
     return jnp.where(cell == low, near, jnp.where(cell == low + one, far, zero))
 
 
-def deposit_kernel(rows_axis, cols_axis, rays_ref, tile_ref, send_ref, list_ref):
+def deposit_kernel(rays_ref, tile_ref, low_ref, high_ref, list_ref):
     slots, _, rays = rays_ref.shape
     lane = lax.broadcasted_iota(jnp.int32, (BITS, 128), 1)
     place = lax.broadcasted_iota(jnp.int32, (BITS, 128), 0)
@@ -117,48 +117,18 @@
     batches = (count + BATCH - 1) // BATCH
     total = lax.fori_loop(0, batches, add, jnp.zeros((TILE, TILE), jnp.float32))
     tile = total.astype(jnp.bfloat16)
-    turned = tile.astype(jnp.float32).T.astype(jnp.bfloat16)
     tile_ref[...] = tile
-    send_ref[...] = jnp.zeros(send_ref.shape, jnp.bfloat16)
-    row_count, col_count = lax.axis_size(rows_axis), lax.axis_size(cols_axis)
-    row, col = lax.axis_index(rows_axis), lax.axis_index(cols_axis)
-    low, high = slice(0, HALO), slice(TILE - HALO, TILE)
-    for dr in (-1, 0, 1):
-        for dc in (-1, 0, 1):
-            if dr == 0 and dc == 0:
-                continue
-            if dr != 0:
-                piece = tile[low if dr < 0 else high, :]
-            else:
-                piece = turned[low if dc < 0 else high, :]
-            r, c = row + dr, col + dc
-
-            @pl.when((r >= 0) & (r < row_count) & (c >= 0) & (c < col_count))
-            def _(r=r, c=c, piece=piece):
-                send_ref[r * col_count + c] = piece
-
-
-def spread_kernel(rows_axis, cols_axis, scale, tile_ref, got_ref, pairs_ref, last_ref, out_ref,
-                  own, side, left):
-    row_count, col_count = lax.axis_size(rows_axis), lax.axis_size(cols_axis)
-    row, col = lax.axis_index(rows_axis), lax.axis_index(cols_axis)
-
-    def fetch(dr, dc):
-        r, c = row + dr, col + dc
-        inside = (r >= 0) & (r < row_count) & (c >= 0) & (c < col_count)
-        index = jnp.where(inside, r * col_count + c, 0)
-        piece = got_ref[index].astype(jnp.float32)
-        return jnp.where(inside, piece, 0.0)
-
-    own[:HALO, :] = fetch(-1, 0).astype(jnp.bfloat16)
+    low_ref[...] = tile[:HALO, :]
+    high_ref[...] = tile[TILE - HALO :, :]
+
+
+def spread_kernel(scale, over_ref, tile_ref, under_ref, before_ref, after_ref, pairs_ref, last_ref,
+                  out_ref, own, side, left):
+    own[:HALO, :] = over_ref[...]
     own[HALO : HALO + TILE, :] = tile_ref[...]
-    own[HALO + TILE :, :] = fetch(1, 0).astype(jnp.bfloat16)
-    for dr, at in ((-1, 0), (1, HALO + TILE)):
-        lower = fetch(dr, -1)[:, TILE - HALO :]
-        upper = fetch(dr, 1)[:, :HALO]
-        side[at : at + HALO, :] = jnp.concatenate([lower, upper], axis=1).astype(jnp.bfloat16)
-    strips = jnp.concatenate([fetch(0, -1), fetch(0, 1)], axis=0).T
-    side[HALO : HALO + TILE, :] = strips.astype(jnp.bfloat16)
+    own[HALO + TILE :, :] = under_ref[...]
+    side[:, :HALO] = before_ref[...]
+    side[:, HALO:] = after_ref[...]
     for u in range(TURNS):
         left[:, u * TILE : (u + 1) * TILE] = own[u * STEP : u * STEP + LONG, :]
         at = TURNS * TILE + u * 2 * HALO
@@ -174,6 +144,12 @@
     out_ref[...] = total / scale
 
 
+def shift(cells, axis, step):
+    count = lax.axis_size(axis)
+    pairs = [(i, i + step) for i in range(count) if 0 <= i + step < count]
+    return lax.ppermute(cells, axis, pairs)
+
+
 def shards(positions, destination, profile):
     tiles = lax.axis_size("row") * lax.axis_size("col")
     blocks, _, rays = positions.shape
@@ -202,24 +178,29 @@
         cost_estimate=pl.CostEstimate(flops=10_000_000, bytes_accessed=6_000_000, transcendentals=0),
         name="table",
     )(profile)
-    tile, send = pl.pallas_call(
-        functools.partial(deposit_kernel, "row", "col"),
+    tile, low, high = pl.pallas_call(
+        deposit_kernel,
         out_shape=(
             jax.ShapeDtypeStruct((TILE, TILE), jnp.bfloat16),
-            jax.ShapeDtypeStruct((tiles, HALO, TILE), jnp.bfloat16),
+            jax.ShapeDtypeStruct((HALO, TILE), jnp.bfloat16),
+            jax.ShapeDtypeStruct((HALO, TILE), jnp.bfloat16),
         ),
         in_specs=[VMEM],
-        out_specs=(VMEM, VMEM),
+        out_specs=(VMEM, VMEM, VMEM),
         scratch_shapes=[pltpu.SMEM((tiles * MOST + BATCH,), jnp.int32)],
         compiler_params=limit,
         name="deposit",
     )(received)
-    got = lax.all_to_all(send, ("row", "col"), split_axis=0, concat_axis=0, tiled=True)
+    over = shift(high, "row", 1)
+    under = shift(low, "row", -1)
+    tall = jnp.concatenate([over, tile, under], axis=0)
+    before = shift(tall[:, TILE - HALO :], "col", 1)
+    after = shift(tall[:, :HALO], "col", -1)
     scale = blocks * rays / (TILE * TILE)
     return pl.pallas_call(
-        functools.partial(spread_kernel, "row", "col", scale),
+        functools.partial(spread_kernel, scale),
         out_shape=jax.ShapeDtypeStruct((TILE, TILE), jnp.float32),
-        in_specs=[VMEM, VMEM, VMEM, VMEM],
+        in_specs=[VMEM] * 7,
         out_specs=VMEM,
         scratch_shapes=[
             pltpu.VMEM((WIDE, TILE), jnp.bfloat16),
@@ -228,7 +209,7 @@
         ],
         compiler_params=limit,
         name="spread",
-    )(tile, got, pairs, last)
+    )(over, tile, under, before, after, pairs, last)
 
 
 def solution(mesh):

time: 33.1 us -> 36.2 us (1.094)
  starting transfers between devices: 4.74 us -> 10.3 us
  waiting for transfers between devices: 4.91 us -> 3.01 us
  Pallas kernels: 5.81 us -> 5.02 us
    ppermute x0 -> x4, starting transfers between devices: none -> 10.3 us  [shift(): return lax.ppermute(cells, axis, pairs)]
    all_to_all x1 -> x0, waiting for transfers between devices: 4.91 us -> none  [shards(): lax.all_to_all(send, ('row', 'col'), split_axis=0, concat_axis=0, tiled=T...]
    all_to_all x1 -> x0, starting transfers between devices: 4.74 us -> none  [shards(): lax.all_to_all(send, ('row', 'col'), split_axis=0, concat_axis=0, tiled=T...]
    ppermute x0 -> x4, waiting for transfers between devices: none -> 3.01 us  [shift(): return lax.ppermute(cells, axis, pairs)]
    pallas_call x2, Pallas kernels: 3.46 us -> 2.67 us  [the longest x1 1.36 us: shards(): pl.pallas_call(functools.partial(spread_kernel, scale), out_shape=jax.Sha...]
    unnamed x5 -> x7, local copies, waits for them, and re-layouts: 2.29 us -> 2.31 us
  transfers between devices with their start and end apart: 1 -> 4, of which waited for: 1 -> 1; matrix products, arithmetic and copies ran while one was open for 0% -> 0% of each run, Pallas kernels for 4% -> 4%
where the time goes in v4:
time: 36.2 us; the launch traced here: 35.8 us
  blocking collectives  15 us (41%)
  starting transfers between devices  10.3 us (28%)
  Pallas kernels  5.02 us (14%)
  waiting for transfers between devices  3.01 us (8%)
  local copies, waits for them, and re-layouts  2.4 us (7%)
    all_to_all x1, blocking collectives, shards(): lax.all_to_all(outgoing.reshape(tiles, MOST, 2, rays), ('row', 'col'), sp...  15 us
    ppermute x4, starting transfers between devices, shift(): return lax.ppermute(cells, axis, pairs)  10.3 us
    ppermute x4, waiting for transfers between devices, shift(): return lax.ppermute(cells, axis, pairs)  3.01 us
    unnamed x7, local copies, waits for them, and re-layouts  2.31 us
    pallas_call x1, Pallas kernels, shards(): pl.pallas_call(table_kernel, out_shape=(jax.ShapeDtypeStruct((STEP // 2,...  1.42 us
    pallas_call x1, Pallas kernels, shards(): pl.pallas_call(functools.partial(spread_kernel, scale), out_shape=jax.Sha...  1.36 us
    pallas_call x1, Pallas kernels, shards(): pl.pallas_call(deposit_kernel, out_shape=(jax.ShapeDtypeStruct((TILE, TIL...  1.32 us
    pallas_call x1, Pallas kernels, shards(): pl.pallas_call(place_kernel, out_shape=jax.ShapeDtypeStruct((tiles * MOST...  0.92 us
  transfers between devices with their start and end apart: 4, of which 1 were waited for; matrix products, arithmetic and copies ran while one was open for 0% of the time, Pallas kernels for 4%

profile of v4, /device:TPU:1, one launch (start us, length us, event | category | flops | bytes accessed | tf_op | source)
XLA Modules:
  0.0 35.8 jit_solution(12753149762038011141)
XLA Ops:
  0.0 0.7 %copy.4.dest_ref = s32[16,1]{1,0:T(8,128)S(1)} copy(s32[16,1]{0,1:T(1,128)} %param.4) | data formatting | bytes 128 | tf_op args[1]
  0.7 0.0 copy-start
  0.7 0.8 %copy-done = f32[16,2,384]{2,1,0:T(2,128)S(1)} copy-done((f32[16,2,384]{2,1,0:T(2,128)S(1)}, f32[16,2,384]{2,1,0:T(2,128)}, u32[]{:S(2)}) %copy-start) | copy-done | bytes 49176
  1.5 0.9 %place.1 = f32[64,2,384]{2,1,0:T(2,128)S(1)} custom-call(s32[16,1]{1,0:T(8,128)S(1)} %copy.4.dest_ref, f32[16,2,384]{2,1,0:T(2,128)S(1)} %copy-done), custom_call_target="tpu_custom_call" | custom-call | tf_op jit(solution)/shard_map/place/pallas_call | solution.py:157
  2.5 15.0 %all_to_all.5 = f32[16,4,2,384]{3,2,1,0:T(2,128)S(1)} all-to-all(f32[16,4,2,384]{3,2,1,0:T(2,128)S(1)} %bitcast.3), channel_id=1, replica_groups=mesh['maps'=2,'row'=4,'col'=4] {'row','col'}, dimensions={0} | all-to-all | bytes 393216 | tf_op jit(solution)/shard_map/all_to_all | solution.py:166
  17.4 1.3 %deposit.1 = (bf16[128,128]{1,0:T(8,128)(2,1)S(1)}, bf16[32,128]{1,0:T(8,128)(2,1)S(1)}, bf16[32,128]{1,0:T(8,128)(2,1)S(1)}) custom-call(f32[64,2,384]{2,1,0:T(2,128)S(1)} %bitcast.2), custom_call_target="tpu_custom_call" | custom-call | tf_op jit(solution)/shard_map/deposit/pallas_call | solution.py:181
  18.7 3.1 %collective-permute-start = (bf16[32,128]{1,0:T(8,128)(2,1)S(1)}, bf16[32,128]{1,0:T(8,128)(2,1)S(1)}, u32[]{:S(2)}, u32[]{:S(2)}) collective-permute-start(bf16[32,128]{1,0:T(8,128)(2,1)S(1)} %get-tuple-element.10), channel_id=1, source_target_pairs={{0,4},{4,8},{8,12},{1,5},{5,9},{9,13},{2,6},{6,10},{10,14},{3,7},{... | collective-permute-start | bytes 24584 | tf_op jit(solution)/shard_map/ppermute | solution.py:150
  21.8 1.9 %collective-permute-start.1 = (bf16[32,128]{1,0:T(8,128)(2,1)S(1)}, bf16[32,128]{1,0:T(8,128)(2,1)S(1)}, u32[]{:S(2)}, u32[]{:S(2)}) collective-permute-start(bf16[32,128]{1,0:T(8,128)(2,1)S(1)} %get-tuple-element.12), channel_id=1, source_target_pairs={{4,0},{8,4},{12,8},{5,1},{9,5},{13,9},{6,2},{10,6},{14,10},{7,3},{... | collective-permute-start | bytes 24584 | tf_op jit(solution)/shard_map/ppermute | solution.py:150
  23.7 0.0 collective-permute-done.over_ref
  23.8 3.0 %collective-permute-done.1.under_ref = bf16[32,128]{1,0:T(8,128)(2,1)S(1)} collective-permute-done((bf16[32,128]{1,0:T(8,128)(2,1)S(1)}, bf16[32,128]{1,0:T(8,128)(2,1)S(1)}, u32[]{:S(2)}, u32[]{:S(2)}) %collective-permute-start.1) | collective-permute-done | bytes 8224 | tf_op jit(solution)/shard_map/ppermute | solution.py:150
  26.8 0.1 fusion
  26.9 1.3 %collective-permute-start.3 = (bf16[192,32]{1,0:T(8,128)(2,1)S(1)}, bf16[192,32]{1,0:T(8,128)(2,1)S(1)}, u32[]{:S(2)}, u32[]{:S(2)}) collective-permute-start(bf16[192,32]{1,0:T(8,128)(2,1)S(1)} %get-tuple-element.15), channel_id=1, source_target_pairs={{1,0},{2,1},{3,2},{5,4},{6,5},{7,6},{9,8},{10,9},{11,10},{13,12},{... | collective-permute-start | bytes 36872 | tf_op jit(solution)/shard_map/ppermute | solution.py:150
  28.2 4.0 %collective-permute-start.2 = (bf16[192,32]{1,0:T(8,128)(2,1)S(1)}, bf16[192,32]{1,0:T(8,128)(2,1)S(1)}, u32[]{:S(2)}, u32[]{:S(2)}) collective-permute-start(bf16[192,32]{1,0:T(8,128)(2,1)S(1)} %get-tuple-element.16), channel_id=1, source_target_pairs={{0,1},{1,2},{2,3},{4,5},{5,6},{6,7},{8,9},{9,10},{10,11},{12,13},{... | collective-permute-start | bytes 36872 | tf_op jit(solution)/shard_map/ppermute | solution.py:150
  32.2 0.0 copy-start.1
  32.2 0.8 %copy-done.1 = f32[65,65]{1,0:T(8,128)S(1)} copy-done((f32[65,65]{1,0:T(8,128)S(1)}, f32[65,65]{1,0:T(8,128)}, u32[]{:S(2)}) %copy-start.1) | copy-done | bytes 16924
  32.9 1.4 %table.1 = (bf16[8,768,256]{2,1,0:T(8,128)(2,1)S(1)}, bf16[192,128]{1,0:T(8,128)(2,1)S(1)}) custom-call(f32[65,65]{1,0:T(8,128)S(1)} %copy-done.1), custom_call_target="tpu_custom_call" | custom-call | flops 10000000 | bytes 6000000 | tf_op jit(solution)/shard_map/table/pallas_call | solution.py:169
  34.4 0.0 collective-permute-done.3.after_ref
  34.4 0.0 collective-permute-done.2.before_ref
  34.4 1.4 %spread.1 = f32[128,128]{1,0:T(8,128)} custom-call(bf16[32,128]{1,0:T(8,128)(2,1)S(1)} %collective-permute-done.over_ref, bf16[128,128]{1,0:T(8,128)(2,1)S(1)} %get-tuple-element.11.tile_ref, bf16[32,128]{1,0:T(8,128)(2,1)S(1)} %collective-permute-done.1.under_ref, bf16[192,32]{1,0:T(8,128)(2,1)S(1)} %collective-permute-done.2.before_ref, ...), custom_call_target="tpu_custom_call" | custom-call | tf_op jit(solution)/shard_map/spread/pallas_call | solution.py:200
  (3 shorter events, 0.0 us)
Async XLA Ops:
  0.7 0.8 %copy-start = (f32[16,2,384]{2,1,0:T(2,128)S(1)}, f32[16,2,384]{2,1,0:T(2,128)}, u32[]{:S(2)}) copy-start(f32[16,2,384]{2,1,0:T(2,128)} %rays_ref.1) | copy-start | bytes 147460
  18.7 5.0 %collective-permute-start = (bf16[32,128]{1,0:T(8,128)(2,1)S(1)}, bf16[32,128]{1,0:T(8,128)(2,1)S(1)}, u32[]{:S(2)}, u32[]{:S(2)}) collective-permute-start(bf16[32,128]{1,0:T(8,128)(2,1)S(1)} %get-tuple-element.10), channel_id=1, source_target_pairs={{0,4},{4,8},{8,12},{1,5},{5,9},{9,13},{2,6},{6,10},{10,14},{3,7},{... | collective-permute-start | bytes 24584 | tf_op jit(solution)/shard_map/ppermute | solution.py:150
  21.8 5.0 %collective-permute-start.1 = (bf16[32,128]{1,0:T(8,128)(2,1)S(1)}, bf16[32,128]{1,0:T(8,128)(2,1)S(1)}, u32[]{:S(2)}, u32[]{:S(2)}) collective-permute-start(bf16[32,128]{1,0:T(8,128)(2,1)S(1)} %get-tuple-element.12), channel_id=1, source_target_pairs={{4,0},{8,4},{12,8},{5,1},{9,5},{13,9},{6,2},{10,6},{14,10},{7,3},{... | collective-permute-start | bytes 24584 | tf_op jit(solution)/shard_map/ppermute | solution.py:150
  26.9 7.5 %collective-permute-start.3 = (bf16[192,32]{1,0:T(8,128)(2,1)S(1)}, bf16[192,32]{1,0:T(8,128)(2,1)S(1)}, u32[]{:S(2)}, u32[]{:S(2)}) collective-permute-start(bf16[192,32]{1,0:T(8,128)(2,1)S(1)} %get-tuple-element.15), channel_id=1, source_target_pairs={{1,0},{2,1},{3,2},{5,4},{6,5},{7,6},{9,8},{10,9},{11,10},{13,12},{... | collective-permute-start | bytes 36872 | tf_op jit(solution)/shard_map/ppermute | solution.py:150
  28.2 6.2 %collective-permute-start.2 = (bf16[192,32]{1,0:T(8,128)(2,1)S(1)}, bf16[192,32]{1,0:T(8,128)(2,1)S(1)}, u32[]{:S(2)}, u32[]{:S(2)}) collective-permute-start(bf16[192,32]{1,0:T(8,128)(2,1)S(1)} %get-tuple-element.16), channel_id=1, source_target_pairs={{0,1},{1,2},{2,3},{4,5},{5,6},{6,7},{8,9},{9,10},{10,11},{12,13},{... | collective-permute-start | bytes 36872 | tf_op jit(solution)/shard_map/ppermute | solution.py:150
  32.2 0.8 %copy-start.1 = (f32[65,65]{1,0:T(8,128)S(1)}, f32[65,65]{1,0:T(8,128)}, u32[]{:S(2)}) copy-start(f32[65,65]{1,0:T(8,128)} %profile_ref.1) | copy-start | bytes 50704

commit v5 on v4

--- a/solution.py
+++ b/solution.py
@@ -83,7 +83,7 @@
     return jnp.where(cell == low, near, jnp.where(cell == low + one, far, zero))
 
 
-def deposit_kernel(rays_ref, tile_ref, low_ref, high_ref, list_ref):
+def deposit_kernel(cols_axis, rays_ref, tile_ref, send_ref, list_ref):
     slots, _, rays = rays_ref.shape
     lane = lax.broadcasted_iota(jnp.int32, (BITS, 128), 1)
     place = lax.broadcasted_iota(jnp.int32, (BITS, 128), 0)
@@ -118,17 +118,49 @@
     total = lax.fori_loop(0, batches, add, jnp.zeros((TILE, TILE), jnp.float32))
     tile = total.astype(jnp.bfloat16)
     tile_ref[...] = tile
-    low_ref[...] = tile[:HALO, :]
-    high_ref[...] = tile[TILE - HALO :, :]
-
-
-def spread_kernel(scale, over_ref, tile_ref, under_ref, before_ref, after_ref, pairs_ref, last_ref,
-                  out_ref, own, side, left):
-    own[:HALO, :] = over_ref[...]
+    turned = tile.astype(jnp.float32).T.astype(jnp.bfloat16)
+    offer(cols_axis, send_ref, turned[:HALO, :], turned[TILE - HALO :, :])
+
+
+def offer(axis, send_ref, low, high):
+    count, me = lax.axis_size(axis), lax.axis_index(axis)
+    send_ref[...] = jnp.zeros(send_ref.shape, jnp.bfloat16)
+
+    @pl.when(me > 0)
+    def _():
+        send_ref[me - 1] = low
+
+    @pl.when(me < count - 1)
+    def _():
+        send_ref[me + 1] = high
+
+
+def fetch(axis, got_ref, step):
+    count, me = lax.axis_size(axis), lax.axis_index(axis)
+    at = me + step
+    inside = (at >= 0) & (at < count)
+    piece = got_ref[jnp.where(inside, at, 0)]
+    return jnp.where(inside, piece, jnp.zeros((), jnp.bfloat16))
+
+
+def rows_kernel(rows_axis, cols_axis, tile_ref, got_ref, side_ref, send_ref):
+    before, after = fetch(cols_axis, got_ref, -1), fetch(cols_axis, got_ref, 1)
+    side = jnp.concatenate([before, after], axis=0).astype(jnp.float32).T.astype(jnp.bfloat16)
+    blank = jnp.zeros((HALO, 2 * HALO), jnp.bfloat16)
+    side_ref[...] = side
+    low = jnp.concatenate([tile_ref[:HALO, :], side[:HALO, :], blank], axis=1)
+    high = jnp.concatenate([tile_ref[TILE - HALO :, :], side[TILE - HALO :, :], blank], axis=1)
+    offer(rows_axis, send_ref, low, high)
+
+
+def spread_kernel(rows_axis, scale, tile_ref, side_ref, got_ref, pairs_ref, last_ref, out_ref,
+                  own, side, left):
     own[HALO : HALO + TILE, :] = tile_ref[...]
-    own[HALO + TILE :, :] = under_ref[...]
-    side[:, :HALO] = before_ref[...]
-    side[:, HALO:] = after_ref[...]
+    side[HALO : HALO + TILE, :] = side_ref[...]
+    for step, at in ((-1, 0), (1, HALO + TILE)):
+        piece = fetch(rows_axis, got_ref, step)
+        own[at : at + HALO, :] = piece[:, :TILE]
+        side[at : at + HALO, :] = piece[:, TILE : TILE + 2 * HALO]
     for u in range(TURNS):
         left[:, u * TILE : (u + 1) * TILE] = own[u * STEP : u * STEP + LONG, :]
         at = TURNS * TILE + u * 2 * HALO
@@ -144,12 +176,6 @@
     out_ref[...] = total / scale
 
 
-def shift(cells, axis, step):
-    count = lax.axis_size(axis)
-    pairs = [(i, i + step) for i in range(count) if 0 <= i + step < count]
-    return lax.ppermute(cells, axis, pairs)
-
-
 def shards(positions, destination, profile):
     tiles = lax.axis_size("row") * lax.axis_size("col")
     blocks, _, rays = positions.shape
@@ -178,29 +204,37 @@
         cost_estimate=pl.CostEstimate(flops=10_000_000, bytes_accessed=6_000_000, transcendentals=0),
         name="table",
     )(profile)
-    tile, low, high = pl.pallas_call(
-        deposit_kernel,
+    row_count, col_count = lax.axis_size("row"), lax.axis_size("col")
+    tile, send = pl.pallas_call(
+        functools.partial(deposit_kernel, "col"),
         out_shape=(
             jax.ShapeDtypeStruct((TILE, TILE), jnp.bfloat16),
-            jax.ShapeDtypeStruct((HALO, TILE), jnp.bfloat16),
-            jax.ShapeDtypeStruct((HALO, TILE), jnp.bfloat16),
+            jax.ShapeDtypeStruct((col_count, HALO, TILE), jnp.bfloat16),
         ),
         in_specs=[VMEM],
-        out_specs=(VMEM, VMEM, VMEM),
+        out_specs=(VMEM, VMEM),
         scratch_shapes=[pltpu.SMEM((tiles * MOST + BATCH,), jnp.int32)],
         compiler_params=limit,
         name="deposit",
     )(received)
-    over = shift(high, "row", 1)
-    under = shift(low, "row", -1)
-    tall = jnp.concatenate([over, tile, under], axis=0)
-    before = shift(tall[:, TILE - HALO :], "col", 1)
-    after = shift(tall[:, :HALO], "col", -1)
+    got = lax.all_to_all(send, "col", split_axis=0, concat_axis=0, tiled=True)
+    side, send = pl.pallas_call(
+        functools.partial(rows_kernel, "row", "col"),
+        out_shape=(
+            jax.ShapeDtypeStruct((TILE, 2 * HALO), jnp.bfloat16),
+            jax.ShapeDtypeStruct((row_count, HALO, 2 * TILE), jnp.bfloat16),
+        ),
+        in_specs=[VMEM] * 2,
+        out_specs=(VMEM, VMEM),
+        compiler_params=limit,
+        name="rows",
+    )(tile, got)
+    got = lax.all_to_all(send, "row", split_axis=0, concat_axis=0, tiled=True)
     scale = blocks * rays / (TILE * TILE)
     return pl.pallas_call(
-        functools.partial(spread_kernel, scale),
+        functools.partial(spread_kernel, "row", scale),
         out_shape=jax.ShapeDtypeStruct((TILE, TILE), jnp.float32),
-        in_specs=[VMEM] * 7,
+        in_specs=[VMEM] * 5,
         out_specs=VMEM,
         scratch_shapes=[
             pltpu.VMEM((WIDE, TILE), jnp.bfloat16),
@@ -209,7 +243,7 @@
         ],
         compiler_params=limit,
         name="spread",
-    )(over, tile, under, before, after, pairs, last)
+    )(tile, side, got, pairs, last)
 
 
 def solution(mesh):

time: 36.2 us -> 37.1 us (1.025)
  the two profiles are of different devices: /device:TPU:1 before, /device:TPU:0 now
where the time goes in v5:
time: 37.1 us; the launch traced here: 36.8 us
  blocking collectives  23.5 us (63%)
  Pallas kernels  5.75 us (15%)
  starting transfers between devices  3.28 us (9%)
  local copies, waits for them, and re-layouts  2.29 us (6%)
  waiting for transfers between devices  1.89 us (5%)
    all_to_all x1, blocking collectives, shards(): lax.all_to_all(outgoing.reshape(tiles, MOST, 2, rays), ('row', 'col'), sp...  15.3 us
    all_to_all x1, blocking collectives, shards(): got = lax.all_to_all(send, 'col', split_axis=0, concat_axis=0, tiled=True)  8.18 us
    all_to_all x1, starting transfers between devices, shards(): got = lax.all_to_all(send, 'row', split_axis=0, concat_axis=0, tiled=True)  3.28 us
    unnamed x5, local copies, waits for them, and re-layouts  2.29 us
    all_to_all x1, waiting for transfers between devices, shards(): got = lax.all_to_all(send, 'row', split_axis=0, concat_axis=0, tiled=True)  1.89 us
    pallas_call x1, Pallas kernels, shards(): pl.pallas_call(table_kernel, out_shape=(jax.ShapeDtypeStruct((STEP // 2,...  1.42 us
    pallas_call x1, Pallas kernels, shards(): pl.pallas_call(functools.partial(deposit_kernel, 'col'), out_shape=(jax.S...  1.37 us
    pallas_call x1, Pallas kernels, shards(): pl.pallas_call(functools.partial(spread_kernel, 'row', scale), out_shape=...  1.29 us
  transfers between devices with their start and end apart: 1, of which 1 were waited for; matrix products, arithmetic and copies ran while one was open for 0% of the time, Pallas kernels for 4%

profile of v5, /device:TPU:0, one launch (start us, length us, event | category | flops | bytes accessed | tf_op | source)
XLA Modules:
  0.0 36.8 jit_solution(3431264587436176658)
XLA Ops:
  0.0 0.7 %copy.4.dest_ref = s32[16,1]{1,0:T(8,128)S(1)} copy(s32[16,1]{0,1:T(1,128)} %param.4) | data formatting | bytes 128 | tf_op args[1]
  0.7 0.0 copy-start
  0.7 0.8 %copy-done = f32[16,2,384]{2,1,0:T(2,128)S(1)} copy-done((f32[16,2,384]{2,1,0:T(2,128)S(1)}, f32[16,2,384]{2,1,0:T(2,128)}, u32[]{:S(2)}) %copy-start) | copy-done | bytes 49176
  1.5 0.9 %place.1 = f32[64,2,384]{2,1,0:T(2,128)S(1)} custom-call(s32[16,1]{1,0:T(8,128)S(1)} %copy.4.dest_ref, f32[16,2,384]{2,1,0:T(2,128)S(1)} %copy-done), custom_call_target="tpu_custom_call" | custom-call | tf_op jit(solution)/shard_map/place/pallas_call | solution.py:183
  2.5 15.3 %all_to_all.15 = f32[16,4,2,384]{3,2,1,0:T(2,128)S(1)} all-to-all(f32[16,4,2,384]{3,2,1,0:T(2,128)S(1)} %bitcast.3), channel_id=1, replica_groups=mesh['maps'=2,'row'=4,'col'=4] {'row','col'}, dimensions={0} | all-to-all | bytes 393216 | tf_op jit(solution)/shard_map/all_to_all | solution.py:192
  17.8 1.4 %deposit.1 = (bf16[128,128]{1,0:T(8,128)(2,1)S(1)}, bf16[4,32,128]{2,1,0:T(8,128)(2,1)S(1)}) custom-call(f32[64,2,384]{2,1,0:T(2,128)S(1)} %bitcast.2), custom_call_target="tpu_custom_call" | custom-call | tf_op jit(solution)/shard_map/deposit/pallas_call | solution.py:208
  19.2 8.2 %all_to_all.16.got_ref = bf16[4,32,128]{2,1,0:T(8,128)(2,1)S(1)} all-to-all(bf16[4,32,128]{2,1,0:T(8,128)(2,1)S(1)} %get-tuple-element.12), channel_id=1, replica_groups=mesh['maps'=2,'row'=4,'col'=4] {'col'}, dimensions={0} | all-to-all | bytes 65536 | tf_op jit(solution)/shard_map/all_to_all | solution.py:220
  27.3 0.7 %rows.1 = (bf16[128,64]{1,0:T(8,128)(2,1)S(1)}, bf16[4,32,256]{2,1,0:T(8,128)(2,1)}) custom-call(bf16[128,128]{1,0:T(8,128)(2,1)S(1)} %get-tuple-element.11.tile_ref, bf16[4,32,128]{2,1,0:T(8,128)(2,1)S(1)} %all_to_all.16.got_ref), custom_call_target="tpu_custom_call" | custom-call | tf_op jit(solution)/shard_map/rows/pallas_call | solution.py:221
  28.1 3.3 %all-to-all-start.2 = ((bf16[4,32,256]{2,1,0:T(8,128)(2,1)}), bf16[4,32,256]{2,1,0:T(8,128)(2,1)S(1)}, u32[]{:S(2)}, u32[]{:S(2)}) async-start(bf16[4,32,256]{2,1,0:T(8,128)(2,1)} %get-tuple-element.14), calls=%async_computation.2 | async-start | bytes 131072 | tf_op jit(solution)/shard_map/all_to_all | solution.py:232
  31.4 0.0 copy-start.1
  31.4 0.8 %copy-done.1 = f32[65,65]{1,0:T(8,128)S(1)} copy-done((f32[65,65]{1,0:T(8,128)S(1)}, f32[65,65]{1,0:T(8,128)}, u32[]{:S(2)}) %copy-start.1) | copy-done | bytes 16924
  32.1 1.4 %table.1 = (bf16[8,768,256]{2,1,0:T(8,128)(2,1)S(1)}, bf16[192,128]{1,0:T(8,128)(2,1)S(1)}) custom-call(f32[65,65]{1,0:T(8,128)S(1)} %copy-done.1), custom_call_target="tpu_custom_call" | custom-call | flops 10000000 | bytes 6000000 | tf_op jit(solution)/shard_map/table/pallas_call | solution.py:195
  33.6 1.9 %all-to-all-done.2.got_ref = bf16[4,32,256]{2,1,0:T(8,128)(2,1)S(1)} async-done(((bf16[4,32,256]{2,1,0:T(8,128)(2,1)}), bf16[4,32,256]{2,1,0:T(8,128)(2,1)S(1)}, u32[]{:S(2)}, u32[]{:S(2)}) %all-to-all-start.2) | async-done | bytes 65568 | tf_op jit(solution)/shard_map/all_to_all | solution.py:232
  35.5 1.3 %spread.1 = f32[128,128]{1,0:T(8,128)} custom-call(bf16[128,128]{1,0:T(8,128)(2,1)S(1)} %get-tuple-element.11.tile_ref, bf16[128,64]{1,0:T(8,128)(2,1)S(1)} %get-tuple-element.13.side_ref, bf16[4,32,256]{2,1,0:T(8,128)(2,1)S(1)} %all-to-all-done.2.got_ref, bf16[8,768,256]{2,1,0:T(8,128)(2,1)S(1)} %get-tuple-element.15.pairs_ref, ...), custom_call_target="tpu_custom_call" | custom-call | tf_op jit(solution)/shard_map/spread/pallas_call | solution.py:234
Async XLA Ops:
  0.7 0.8 %copy-start = (f32[16,2,384]{2,1,0:T(2,128)S(1)}, f32[16,2,384]{2,1,0:T(2,128)}, u32[]{:S(2)}) copy-start(f32[16,2,384]{2,1,0:T(2,128)} %rays_ref.1) | copy-start | bytes 147460
  28.1 7.4 %all-to-all-start.2 = ((bf16[4,32,256]{2,1,0:T(8,128)(2,1)}), bf16[4,32,256]{2,1,0:T(8,128)(2,1)S(1)}, u32[]{:S(2)}, u32[]{:S(2)}) async-start(bf16[4,32,256]{2,1,0:T(8,128)(2,1)} %get-tuple-element.14), calls=%async_computation.2 | async-start | bytes 131072 | tf_op jit(solution)/shard_map/all_to_all | solution.py:232
  31.4 0.8 %copy-start.1 = (f32[65,65]{1,0:T(8,128)S(1)}, f32[65,65]{1,0:T(8,128)}, u32[]{:S(2)}) copy-start(f32[65,65]{1,0:T(8,128)} %profile_ref.1) | copy-start | bytes 50704

commit v6 on v3

--- a/solution.py
+++ b/solution.py
@@ -23,7 +23,7 @@
 SMEM = pl.BlockSpec(memory_space=pltpu.SMEM)
 
 
-def place_kernel(dest_ref, rays_ref, out_ref, count_ref):
+def place_kernel(dest_ref, rays_ref, out_ref, count_ref, done):
     blocks = rays_ref.shape[0]
     tiles = out_ref.shape[0] // MOST
     empty = jnp.full((MOST,) + rays_ref.shape[1:], -2.0, jnp.float32)
@@ -33,16 +33,22 @@
         out_ref[pl.ds(t * MOST, MOST)] = empty
         return carry
 
-    lax.fori_loop(0, tiles, clear, 0)
+    lax.fori_loop(0, tiles, clear, 0, unroll=4)
 
     def place(b, carry):
-        t = dest_ref[b, 0]
+        t = dest_ref[0, b]
         rank = count_ref[t]
         count_ref[t] = rank + 1
-        out_ref[t * MOST + rank] = rays_ref[b]
+        pltpu.make_async_copy(rays_ref.at[b], out_ref.at[t * MOST + rank], done.at[b]).start()
         return carry
 
-    lax.fori_loop(0, blocks, place, 0)
+    lax.fori_loop(0, blocks, place, 0, unroll=4)
+
+    def finish(b, carry):
+        pltpu.make_async_copy(rays_ref.at[b], out_ref.at[b], done.at[b]).wait()
+        return carry
+
+    lax.fori_loop(0, blocks, finish, 0, unroll=4)
 
 
 def table_kernel(profile_ref, pairs_ref, last_ref):
@@ -119,7 +125,6 @@
     tile = total.astype(jnp.bfloat16)
     turned = tile.astype(jnp.float32).T.astype(jnp.bfloat16)
     tile_ref[...] = tile
-    send_ref[...] = jnp.zeros(send_ref.shape, jnp.bfloat16)
     row_count, col_count = lax.axis_size(rows_axis), lax.axis_size(cols_axis)
     row, col = lax.axis_index(rows_axis), lax.axis_index(cols_axis)
     low, high = slice(0, HALO), slice(TILE - HALO, TILE)
@@ -181,12 +186,12 @@
     outgoing = pl.pallas_call(
         place_kernel,
         out_shape=jax.ShapeDtypeStruct((tiles * MOST, 2, rays), jnp.float32),
-        in_specs=[SMEM, VMEM],
+        in_specs=[SMEM, pl.BlockSpec(memory_space=pltpu.HBM)],
         out_specs=VMEM,
-        scratch_shapes=[pltpu.SMEM((tiles,), jnp.int32)],
-        compiler_params=limit,
+        scratch_shapes=[pltpu.SMEM((tiles,), jnp.int32), pltpu.SemaphoreType.DMA((blocks,))],
+        compiler_params=pltpu.CompilerParams(vmem_limit_bytes=56 * 1024 * 1024),
         name="place",
-    )(destination, positions)
+    )(destination.T, positions)
     received = lax.all_to_all(
         outgoing.reshape(tiles, MOST, 2, rays), ("row", "col"), split_axis=0, concat_axis=0, tiled=True
     ).reshape(tiles * MOST, 2, rays)
@@ -202,6 +207,7 @@
         cost_estimate=pl.CostEstimate(flops=10_000_000, bytes_accessed=6_000_000, transcendentals=0),
         name="table",
     )(profile)
+    received, pairs, last = lax.optimization_barrier((received, pairs, last))
     tile, send = pl.pallas_call(
         functools.partial(deposit_kernel, "row", "col"),
         out_shape=(

time: 33.1 us -> 32.1 us (0.970)
  the two profiles are of different devices: /device:TPU:1 before, /device:TPU:0 now
where the time goes in v6:
time: 32.1 us; the launch traced here: 31.7 us
  blocking collectives  11 us (34%)
  starting transfers between devices  7.37 us (23%)
  Pallas kernels  6.62 us (21%)
  waiting for transfers between devices  5.94 us (19%)
  local copies, waits for them, and re-layouts  0.76 us (2%)
    all_to_all x1, blocking collectives, shards(): lax.all_to_all(send, ('row', 'col'), split_axis=0, concat_axis=0, tiled=T...  11 us
    all_to_all x1, starting transfers between devices, shards(): lax.all_to_all(outgoing.reshape(tiles, MOST, 2, rays), ('row', 'col'), sp...  7.37 us
    all_to_all x1, waiting for transfers between devices, shards(): lax.all_to_all(outgoing.reshape(tiles, MOST, 2, rays), ('row', 'col'), sp...  5.94 us
    pallas_call x1, Pallas kernels, shards(): pl.pallas_call(place_kernel, out_shape=jax.ShapeDtypeStruct((tiles * MOST...  2.39 us
    pallas_call x1, Pallas kernels, shards(): pl.pallas_call(table_kernel, out_shape=(jax.ShapeDtypeStruct((STEP // 2,...  1.42 us
    pallas_call x1, Pallas kernels, shards(): pl.pallas_call(functools.partial(deposit_kernel, 'row', 'col'), out_shape...  1.41 us
    pallas_call x1, Pallas kernels, shards(): pl.pallas_call(functools.partial(spread_kernel, 'row', 'col', scale), out...  1.39 us
    unnamed x2, local copies, waits for them, and re-layouts  0.76 us
  transfers between devices with their start and end apart: 1, of which 1 were waited for; matrix products, arithmetic and copies ran while one was open for 0% of the time, Pallas kernels for 4%

profile of v6, /device:TPU:0, one launch (start us, length us, event | category | flops | bytes accessed | tf_op | source)
XLA Modules:
  0.0 31.7 jit_solution(6280228548696661039)
XLA Ops:
  0.0 2.4 %place.1 = f32[64,2,384]{2,1,0:T(2,128)} custom-call(s32[1,16]{1,0:T(1,128)} %bitcast.5, f32[16,2,384]{2,1,0:T(2,128)} %rays_ref.1), custom_call_target="tpu_custom_call" | custom-call | tf_op jit(solution)/shard_map/place/pallas_call | solution.py:186
  2.4 7.4 %all-to-all-start = ((f32[16,4,2,384]{3,2,1,0:T(2,128)}), f32[16,4,2,384]{3,2,1,0:T(2,128)S(1)}, u32[]{:S(2)}, u32[]{:S(2)}) async-start(f32[16,4,2,384]{3,2,1,0:T(2,128)} %bitcast.4), calls=%async_computation | async-start | bytes 393216 | tf_op jit(solution)/shard_map/all_to_all | solution.py:195
  9.8 0.0 copy-start
  9.8 0.8 %copy-done = f32[65,65]{1,0:T(8,128)S(1)} copy-done((f32[65,65]{1,0:T(8,128)S(1)}, f32[65,65]{1,0:T(8,128)}, u32[]{:S(2)}) %copy-start) | copy-done | bytes 16924
  10.5 1.4 %table.1 = (bf16[8,768,256]{2,1,0:T(8,128)(2,1)S(1)}, bf16[192,128]{1,0:T(8,128)(2,1)S(1)}) custom-call(f32[65,65]{1,0:T(8,128)S(1)} %copy-done), custom_call_target="tpu_custom_call" | custom-call | flops 10000000 | bytes 6000000 | tf_op jit(solution)/shard_map/table/pallas_call | solution.py:198
  12.0 5.9 %all-to-all-done = f32[16,4,2,384]{3,2,1,0:T(2,128)S(1)} async-done(((f32[16,4,2,384]{3,2,1,0:T(2,128)}), f32[16,4,2,384]{3,2,1,0:T(2,128)S(1)}, u32[]{:S(2)}, u32[]{:S(2)}) %all-to-all-start) | async-done | bytes 196640 | tf_op jit(solution)/shard_map/all_to_all | solution.py:195
  17.9 1.4 %deposit.1 = (bf16[128,128]{1,0:T(8,128)(2,1)S(1)}, bf16[16,32,128]{2,1,0:T(8,128)(2,1)S(1)}) custom-call(f32[64,2,384]{2,1,0:T(2,128)S(1)} %bitcast.3), custom_call_target="tpu_custom_call" | custom-call | tf_op jit(solution)/shard_map/deposit/pallas_call | solution.py:211
  19.3 11.0 %all_to_all.10.got_ref = bf16[16,32,128]{2,1,0:T(8,128)(2,1)S(1)} all-to-all(bf16[16,32,128]{2,1,0:T(8,128)(2,1)S(1)} %get-tuple-element.16), channel_id=1, replica_groups=mesh['maps'=2,'row'=4,'col'=4] {'row','col'}, dimensions={0} | all-to-all | bytes 262144 | tf_op jit(solution)/shard_map/all_to_all | solution.py:223
  30.3 1.4 %spread.1 = f32[128,128]{1,0:T(8,128)} custom-call(bf16[128,128]{1,0:T(8,128)(2,1)S(1)} %get-tuple-element.15.tile_ref, bf16[16,32,128]{2,1,0:T(8,128)(2,1)S(1)} %all_to_all.10.got_ref, bf16[8,768,256]{2,1,0:T(8,128)(2,1)S(1)} %get-tuple-element.17.pairs_ref, bf16[192,128]{1,0:T(8,128)(2,1)S(1)} %get-tuple-element.18.last_ref), custom_call_target="tpu_custom_call" | custom-call | tf_op jit(solution)/shard_map/spread/pallas_call | solution.py:225
Async XLA Ops:
  2.4 15.5 %all-to-all-start = ((f32[16,4,2,384]{3,2,1,0:T(2,128)}), f32[16,4,2,384]{3,2,1,0:T(2,128)S(1)}, u32[]{:S(2)}, u32[]{:S(2)}) async-start(f32[16,4,2,384]{3,2,1,0:T(2,128)} %bitcast.4), calls=%async_computation | async-start | bytes 393216 | tf_op jit(solution)/shard_map/all_to_all | solution.py:195
  9.8 0.8 %copy-start = (f32[65,65]{1,0:T(8,128)S(1)}, f32[65,65]{1,0:T(8,128)}, u32[]{:S(2)}) copy-start(f32[65,65]{1,0:T(8,128)} %profile_ref.1) | copy-start | bytes 50704

commit v7 on v4

v7 whole, which is shorter than its diff:
```python
import functools

import jax
import jax.numpy as jnp
from jax import lax
from jax.experimental import pallas as pl
from jax.experimental.pallas import tpu as pltpu
from jax.sharding import PartitionSpec as P

TILE = 128
HALO = 32
MOST = 4
DISC = 2 * HALO + 1
STEP = 16
LONG = TILE + STEP
TURNS = 2 * HALO // STEP
WIDE = TILE + 2 * HALO
DEPTH = TURNS * WIDE
LANES = 128
BATCH = 8

VMEM = pl.BlockSpec(memory_space=pltpu.VMEM)
LIMIT = pltpu.CompilerParams(vmem_limit_bytes=32 * 1024 * 1024)


def pack_kernel(dest_ref, rays_ref, out_ref, meta):
    blocks = rays_ref.shape[0]
    half = blocks // 2
    lane = lax.broadcasted_iota(jnp.int32, (blocks, LANES), 1)
    place = lax.broadcasted_iota(jnp.int32, (blocks, LANES), 0)

    def laid(column):
        return jnp.sum(jnp.where(lane == place, column, 0.0), axis=0, keepdims=True)

    meta[...] = jnp.zeros(meta.shape, jnp.float32)
    meta[0:1, :blocks] = dest_ref[...].astype(jnp.float32)
    for k in range(2):
        coords = rays_ref[:, k, :]
        meta[k : k + 1, LANES : 2 * LANES] = laid(jnp.min(coords, axis=1, keepdims=True))
        meta[k : k + 1, 2 * LANES : 3 * LANES] = laid(jnp.max(coords, axis=1, keepdims=True))
    col_count = lax.axis_size("col")
    for t in range(out_ref.shape[0]):
        at = (t // col_count) % 2 * half
        out_ref[t, :half] = rays_ref[at : at + half]
        out_ref[t, half] = meta[...]


def table_kernel(profile_ref, pairs_ref, last_ref):
    a = lax.broadcasted_iota(jnp.int32, (DISC, DISC), 0) - HALO
    c = lax.broadcasted_iota(jnp.int32, (DISC, DISC), 1) - HALO
    weights = jnp.where(a * a + c * c <= HALO * HALO, profile_ref[...], 0.0)
    kernel = (weights / jnp.sum(weights)).astype(jnp.bfloat16)
    source = lax.broadcasted_iota(jnp.int32, (DISC, 2 * TILE), 0)
    target = lax.broadcasted_iota(jnp.int32, (DISC, 2 * TILE), 1)
    mirror = jnp.where((source + target) % (2 * TILE) == 0, 1.0, 0.0).astype(jnp.bfloat16)
    mirrored = jnp.dot(kernel, mirror, preferred_element_type=jnp.float32)

    def band(row, first, rows):
        wide = jnp.broadcast_to(mirrored[row : row + 1, :], (rows, 2 * TILE))
        rolled = pltpu.roll(wide, first, 1, stride=1, stride_axis=0)
        return rolled[:, :TILE].astype(jnp.bfloat16)

    for s in range(STEP):
        half = pl.ds((s % 2) * TILE, TILE)
        for u in range(TURNS):
            row = u * STEP + s
            pairs_ref[s // 2, pl.ds(u * TILE, TILE), half] = band(row, HALO, TILE)
            side = TURNS * TILE + u * 2 * HALO
            pairs_ref[s // 2, pl.ds(side, HALO), half] = band(row, 0, HALO)
            pairs_ref[s // 2, pl.ds(side + HALO, HALO), half] = band(row, HALO + TILE, HALO)
    last_ref[:TILE, :] = band(2 * HALO, HALO, TILE)
    last_ref[TILE : TILE + HALO, :] = band(2 * HALO, 0, HALO)
    last_ref[TILE + HALO :, :] = band(2 * HALO, HALO + TILE, HALO)


def hats(coords, offset, cell):
    low = jnp.floor(coords)
    near = jnp.maximum(0.0, 1.0 - jnp.abs(coords - low)).astype(jnp.bfloat16)
    far = jnp.maximum(0.0, 1.0 - jnp.abs(coords - (low + 1.0))).astype(jnp.bfloat16)
    low = low + offset
    here, there = low.astype(jnp.bfloat16), (low + 1.0).astype(jnp.bfloat16)
    zero = jnp.zeros((), jnp.bfloat16)
    return jnp.where(cell == here, near, jnp.where(cell == there, far, zero))


def gather_codes(got_ref, codes, table, done):
    last = got_ref.shape[1] - 1
    row_count, col_count = lax.axis_size("row"), lax.axis_size("col")
    row, col = lax.axis_index("row"), lax.axis_index("col")
    tile = got_ref[:, last, 0, :LANES]
    tile_row = jnp.floor((tile + 0.5) / col_count)
    dr = tile_row - row.astype(jnp.float32)
    dc = tile - tile_row * col_count - col.astype(jnp.float32)

    def touches(d, k):
        least = got_ref[:, last, k, LANES : 2 * LANES]
        most = got_ref[:, last, k, 2 * LANES : 3 * LANES]
        before = (d == -1.0) & (most > TILE - HALO - 1.0)
        after = (d == 1.0) & (least < HALO)
        return (d == 0.0) | before | after

    reach = (tile >= 0.0) & touches(dr, 0) & touches(dc, 1)
    kind = jnp.where(dr == 0.0, 1.0, jnp.where(dr < 0.0, 2.0, 3.0))
    codes[...] = jnp.where(reach, 4.0 * kind + dc + 1.0, 0.0).astype(jnp.int32)
    copy = pltpu.make_async_copy(codes, table, done)
    copy.start()
    copy.wait()


def add_half(parity, got_ref, total, codes, table, done, lists):
    sources, held, _, rays = got_ref.shape
    half = held - 1
    gather_codes(got_ref, codes, table, done)
    room = sources * half + BATCH

    def sort(source, counts):
        one, two, three = counts
        for k in range(half):
            code = table[source, parity * half + k]
            entry = (source * held + k) * 4 + (code & 3)
            kind = code >> 2
            lists[one] = entry
            lists[room + two] = entry
            lists[2 * room + three] = entry
            one = one + (kind == 1).astype(jnp.int32)
            two = two + (kind == 2).astype(jnp.int32)
            three = three + (kind == 3).astype(jnp.int32)
        return one, two, three

    zero = jnp.int32(0)
    counts = lax.fori_loop(0, sources, sort, (zero, zero, zero))

    def steps(extent, start):
        cell = lax.broadcasted_iota(jnp.int32, (extent, rays), 0) + start
        return cell.astype(jnp.float32).astype(jnp.bfloat16)

    order = lax.broadcasted_iota(jnp.int32, (WIDE, rays), 0)
    order = jnp.where(order < TILE, order, jnp.where(order < TILE + HALO, order - WIDE + HALO, order - HALO))
    across = order.astype(jnp.float32).astype(jnp.bfloat16)

    for kind, (rows, start, at, batch) in enumerate(
        ((TILE, 0, HALO, BATCH), (HALO, TILE - HALO, 0, BATCH), (HALO, 0, HALO + TILE, BATCH))
    ):
        count, base = counts[kind], kind * room
        for k in range(batch):
            lists[base + count + k] = 3
        down = steps(rows, start)

        def add(step, sums, base=base, down=down, batch=batch):
            for k in range(batch):
                entry = lists[base + step * batch + k]
                slot = entry >> 2
                block = got_ref[slot // held, slot % held]
                offset = (((entry & 3) - 1) * TILE).astype(jnp.float32)
                sums = sums + lax.dot_general(
                    hats(block[0:1, :], 0.0, down),
                    hats(block[1:2, :], offset, across),
                    (((1,), (1,)), ((), ())),
                    preferred_element_type=jnp.float32,
                )
            return sums

        turns = (count + batch - 1) // batch
        total[at : at + rows, :] = lax.fori_loop(0, turns, add, total[at : at + rows, :])


def first_kernel(got_ref, total_ref, codes, table, done, lists):
    total_ref[...] = jnp.zeros(total_ref.shape, jnp.float32)
    add_half(lax.axis_index("row") % 2, got_ref, total_ref, codes, table, done, lists)


def second_kernel(scale, got_ref, total_ref, pairs_ref, last_ref, out_ref,
                  total, left, codes, table, done, lists):
    total[...] = total_ref[...]
    add_half(1 - lax.axis_index("row") % 2, got_ref, total, codes, table, done, lists)
    own = total[:, :TILE].astype(jnp.bfloat16)
    side = total[:, TILE:].astype(jnp.bfloat16)
    for u in range(TURNS):
        left[:, u * TILE : (u + 1) * TILE] = own[u * STEP : u * STEP + LONG, :]
        at = TURNS * TILE + u * 2 * HALO
        left[:, at : at + 2 * HALO] = side[u * STEP : u * STEP + LONG, :]
    sums = jnp.dot(own[2 * HALO :, :], last_ref[:TILE, :], preferred_element_type=jnp.float32)
    sums = sums + jnp.dot(side[2 * HALO :, :], last_ref[TILE:, :], preferred_element_type=jnp.float32)
    for p in range(STEP // 2):
        both = jnp.dot(left[...], pairs_ref[p], preferred_element_type=jnp.float32)
        sums = sums + both[2 * p : 2 * p + TILE, :TILE]
        sums = sums + both[2 * p + 1 : 2 * p + 1 + TILE, TILE:]
    out_ref[...] = sums / scale


def packed(positions, destination):
    row_count, col_count = lax.axis_size("row"), lax.axis_size("col")
    tiles = row_count * col_count
    blocks, _, rays = positions.shape
    if blocks <= 12 * MOST:
        return pl.pallas_call(
            pack_kernel,
            out_shape=jax.ShapeDtypeStruct((tiles, blocks // 2 + 1, 2, rays), jnp.float32),
            in_specs=[VMEM, VMEM],
            out_specs=VMEM,
            scratch_shapes=[pltpu.VMEM((2, rays), jnp.float32)],
            compiler_params=LIMIT,
            name="pack",
        )(destination.T, positions)
    room = 12 * MOST
    targets = destination[:, 0]
    pair = jnp.arange(row_count // 2, dtype=jnp.int32)[:, None, None]
    col = jnp.arange(col_count, dtype=jnp.int32)[None, :, None]
    down = targets // col_count - 2 * pair
    over = targets % col_count - col
    near = (down >= -1) & (down <= 2) & (jnp.abs(over) <= 1)
    picked = jnp.argsort(jnp.logical_not(near).astype(jnp.int32), axis=2, stable=True)[:, :, :room]
    valid = jnp.take_along_axis(near, picked, axis=2)
    label = jnp.where(valid, targets[picked], -1).astype(jnp.float32)
    least, most = jnp.min(positions, axis=2)[picked], jnp.max(positions, axis=2)[picked]
    spare = ((0, 0), (0, 0), (0, LANES - room))
    meta = jnp.stack(
        [
            jnp.concatenate([jnp.pad(row, spare) for row in (label, least[..., 0], most[..., 0])], 2),
            jnp.concatenate([jnp.pad(row, spare) for row in (label, least[..., 1], most[..., 1])], 2),
        ],
        axis=2,
    )
    halves = positions[picked].reshape(row_count // 2, col_count, 2, room // 2, 2, rays)
    halves = jnp.transpose(halves, (0, 2, 1, 3, 4, 5))
    metas = jnp.broadcast_to(meta[:, None, :, None], halves.shape[:3] + (1, 2, rays))
    return jnp.concatenate([halves, metas], axis=3).reshape(tiles, room // 2 + 1, 2, rays)


def shards(positions, destination, profile):
    blocks, _, rays = positions.shape
    outgoing = packed(positions, destination)
    sources, held = outgoing.shape[0], outgoing.shape[1]
    mine = lax.all_to_all(outgoing, ("row", "col"), split_axis=0, concat_axis=0, tiled=True)
    other = lax.ppermute(mine, "row", [(i, i ^ 1) for i in range(lax.axis_size("row"))])
    pairs, last = pl.pallas_call(
        table_kernel,
        out_shape=(
            jax.ShapeDtypeStruct((STEP // 2, DEPTH, 2 * TILE), jnp.bfloat16),
            jax.ShapeDtypeStruct((WIDE, TILE), jnp.bfloat16),
        ),
        in_specs=[VMEM],
        out_specs=(VMEM, VMEM),
        compiler_params=LIMIT,
        cost_estimate=pl.CostEstimate(flops=10_000_000, bytes_accessed=6_000_000, transcendentals=0),
        name="table",
    )(profile)
    scratch = [
        pltpu.VMEM((sources, LANES), jnp.int32),
        pltpu.SMEM((sources, LANES), jnp.int32),
        pltpu.SemaphoreType.DMA,
        pltpu.SMEM((3 * (sources * (held - 1) + BATCH),), jnp.int32),
    ]
    total = pl.pallas_call(
        first_kernel,
        out_shape=jax.ShapeDtypeStruct((WIDE, WIDE), jnp.float32),
        in_specs=[VMEM],
        out_specs=VMEM,
        scratch_shapes=scratch,
        compiler_params=LIMIT,
        cost_estimate=pl.CostEstimate(flops=2_000_000_000, bytes_accessed=4_000_000, transcendentals=0),
        name="first",
    )(mine)
    return pl.pallas_call(
        functools.partial(second_kernel, blocks * rays / (TILE * TILE)),
        out_shape=jax.ShapeDtypeStruct((TILE, TILE), jnp.float32),
        in_specs=[VMEM] * 4,
        out_specs=VMEM,
        scratch_shapes=[
            pltpu.VMEM((WIDE, WIDE), jnp.float32),
            pltpu.VMEM((LONG, DEPTH), jnp.bfloat16),
        ] + scratch,
        compiler_params=LIMIT,
        name="second",
    )(other, total, pairs, last)


def solution(mesh):
    placed = (P(("maps", "row", "col"), None, None), P(("maps", "row", "col"), None), P())
    return jax.shard_map(
        shards, mesh=mesh, in_specs=placed, out_specs=P(("maps", "row"), "col"), check_vma=False
    )
```

time: 36.2 us -> 35.4 us (0.978); the launches traced: 35.8 us -> 35.5 us
  starting transfers between devices: 10.3 us -> 0.82 us
  Pallas kernels: 5.02 us -> 12.1 us
  blocking collectives: 15 us -> 20.3 us
  waiting for transfers between devices: 3.01 us -> 0.01 us
    ppermute x4 -> x1, starting transfers between devices: 10.3 us -> 0.82 us  [shards(): lax.ppermute(mine, 'row', [(i, i ^ 1) for i in range(lax.axis_size('row'))])]
    pallas_call x3, Pallas kernels: 3.6 us -> 10.7 us  [the longest x1 5.91 us: shards(): pl.pallas_call(functools.partial(second_kernel, blocks * rays / (TILE * T...]
    all_to_all x1, blocking collectives: 15 us -> 20.3 us  [shards(): lax.all_to_all(outgoing, ('row', 'col'), split_axis=0, concat_axis=0, til...]
    ppermute x4 -> x1, waiting for transfers between devices: 3.01 us -> 0.01 us  [shards(): lax.ppermute(mine, 'row', [(i, i ^ 1) for i in range(lax.axis_size('row'))])]
    unnamed x7 -> x6, local copies, waits for them, and re-layouts: 2.31 us -> 2.22 us
  transfers between devices with their start and end apart: 4 -> 1, of which waited for: 1 -> 0; matrix products, arithmetic and copies ran while one was open for 0% -> 0% of each run, Pallas kernels for 4% -> 17%
where the time goes in v7:
time: 35.4 us; the launch traced here: 35.5 us
  blocking collectives  20.3 us (57%)
  Pallas kernels  12.1 us (34%)
  local copies, waits for them, and re-layouts  2.22 us (6%)
  starting transfers between devices  0.82 us (2%)
    all_to_all x1, blocking collectives, shards(): lax.all_to_all(outgoing, ('row', 'col'), split_axis=0, concat_axis=0, til...  20.3 us
    pallas_call x1, Pallas kernels, shards(): pl.pallas_call(functools.partial(second_kernel, blocks * rays / (TILE * T...  5.91 us
    pallas_call x1, Pallas kernels, shards(): pl.pallas_call(first_kernel, out_shape=jax.ShapeDtypeStruct((WIDE, WIDE),...  4.64 us
    unnamed x6, local copies, waits for them, and re-layouts  2.22 us
    pallas_call x1, Pallas kernels, shards(): pl.pallas_call(table_kernel, out_shape=(jax.ShapeDtypeStruct((STEP // 2,...  1.42 us
    ppermute x1, starting transfers between devices, shards(): lax.ppermute(mine, 'row', [(i, i ^ 1) for i in range(lax.axis_size('row'))])  0.82 us
  transfers between devices with their start and end apart: 1, of which 0 were waited for; matrix products, arithmetic and copies ran while one was open for 0% of the time, Pallas kernels for 17%

profile of v7, /device:TPU:1, one launch (start us, length us, event | category | flops | bytes accessed | tf_op | source)
XLA Modules:
  0.0 35.5 jit_solution(2141888490458534265)
XLA Ops:
  0.0 0.0 copy-start
  0.0 0.8 %copy-done = f32[16,2,384]{2,1,0:T(2,128)S(1)} copy-done((f32[16,2,384]{2,1,0:T(2,128)S(1)}, f32[16,2,384]{2,1,0:T(2,128)}, u32[]{:S(2)}) %copy-start) | copy-done | bytes 49176
  0.8 0.0 copy-start.1
  0.8 0.7 %copy-done.1 = s32[16,1]{0,1:T(1,128)S(1)} copy-done((s32[16,1]{0,1:T(1,128)S(1)}, s32[16,1]{0,1:T(1,128)}, u32[]{:S(2)}) %copy-start.1) | copy-done | bytes 88
  1.5 0.1 pack.1
  1.6 20.3 %all_to_all.5.got_ref = f32[16,9,2,384]{3,2,1,0:T(2,128)S(1)} all-to-all(f32[16,9,2,384]{3,2,1,0:T(2,128)S(1)} %pack.1), channel_id=1, replica_groups=mesh['maps'=2,'row'=4,'col'=4] {'row','col'}, dimensions={0} | all-to-all | bytes 884736 | tf_op jit(solution)/shard_map/all_to_all | solution.py:234
  21.9 0.8 %collective-permute-start = (f32[16,9,2,384]{3,2,1,0:T(2,128)S(1)}, f32[16,9,2,384]{3,2,1,0:T(2,128)S(1)}, u32[]{:S(2)}, u32[]{:S(2)}) collective-permute-start(f32[16,9,2,384]{3,2,1,0:T(2,128)S(1)} %all_to_all.5.got_ref), channel_id=1, source_target_pairs={{0,4},{4,0},{8,12},{12,8},{1,5},{5,1},{9,13},{13,9},{2,6},{6,2},{1... | collective-permute-start | bytes 1327112 | tf_op jit(solution)/shard_map/ppermute | solution.py:235
  22.7 0.0 copy-start.2
  22.7 0.8 %copy-done.2 = f32[65,65]{1,0:T(8,128)S(1)} copy-done((f32[65,65]{1,0:T(8,128)S(1)}, f32[65,65]{1,0:T(8,128)}, u32[]{:S(2)}) %copy-start.2) | copy-done | bytes 16924
  23.5 1.4 %table.1 = (bf16[8,768,256]{2,1,0:T(8,128)(2,1)S(1)}, bf16[192,128]{1,0:T(8,128)(2,1)S(1)}) custom-call(f32[65,65]{1,0:T(8,128)S(1)} %copy-done.2), custom_call_target="tpu_custom_call" | custom-call | flops 10000000 | bytes 6000000 | tf_op jit(solution)/shard_map/table/pallas_call | solution.py:236
  24.9 4.6 %first.1.total_ref = f32[192,192]{1,0:T(8,128)S(1)} custom-call(f32[16,9,2,384]{3,2,1,0:T(2,128)S(1)} %all_to_all.5.got_ref), custom_call_target="tpu_custom_call" | custom-call | flops 2000000000 | bytes 4000000 | tf_op jit(solution)/shard_map/first/pallas_call | solution.py:254
  29.6 0.0 collective-permute-done.got_ref
  29.6 5.9 %second.1 = f32[128,128]{1,0:T(8,128)} custom-call(f32[16,9,2,384]{3,2,1,0:T(2,128)S(1)} %collective-permute-done.got_ref, f32[192,192]{1,0:T(8,128)S(1)} %first.1.total_ref, bf16[8,768,256]{2,1,0:T(8,128)(2,1)S(1)} %get-tuple-element.7.pairs_ref, bf16[192,128]{1,0:T(8,128)(2,1)S(1)} %get-tuple-element.8.last_ref), custom_call_target="tpu_custom_call" | custom-call | tf_op jit(solution)/shard_map/second/pallas_call | solution.py:264
Async XLA Ops:
  0.0 0.8 %copy-start = (f32[16,2,384]{2,1,0:T(2,128)S(1)}, f32[16,2,384]{2,1,0:T(2,128)}, u32[]{:S(2)}) copy-start(f32[16,2,384]{2,1,0:T(2,128)} %rays_ref.1) | copy-start | bytes 147460
  0.8 0.7 %copy-start.1 = (s32[16,1]{0,1:T(1,128)S(1)}, s32[16,1]{0,1:T(1,128)}, u32[]{:S(2)}) copy-start(s32[16,1]{0,1:T(1,128)} %param.4) | copy-start | bytes 196
  21.9 7.7 %collective-permute-start = (f32[16,9,2,384]{3,2,1,0:T(2,128)S(1)}, f32[16,9,2,384]{3,2,1,0:T(2,128)S(1)}, u32[]{:S(2)}, u32[]{:S(2)}) collective-permute-start(f32[16,9,2,384]{3,2,1,0:T(2,128)S(1)} %all_to_all.5.got_ref), channel_id=1, source_target_pairs={{0,4},{4,0},{8,12},{12,8},{1,5},{5,1},{9,13},{13,9},{2,6},{6,2},{1... | collective-permute-start | bytes 1327112 | tf_op jit(solution)/shard_map/ppermute | solution.py:235
  22.7 0.8 %copy-start.2 = (f32[65,65]{1,0:T(8,128)S(1)}, f32[65,65]{1,0:T(8,128)}, u32[]{:S(2)}) copy-start(f32[65,65]{1,0:T(8,128)} %profile_ref.1) | copy-start | bytes 50704

commit v8 on v6

--- a/solution.py
+++ b/solution.py
@@ -16,39 +16,38 @@
 TURNS = 2 * HALO // STEP
 WIDE = TILE + 2 * HALO
 DEPTH = TURNS * WIDE
-BITS = 16
+LANES = 128
 BATCH = 8
 
 VMEM = pl.BlockSpec(memory_space=pltpu.VMEM)
-SMEM = pl.BlockSpec(memory_space=pltpu.SMEM)
-
-
-def place_kernel(dest_ref, rays_ref, out_ref, count_ref, done):
+
+
+def place_kernel(dest_ref, rays_ref, out_ref, labels, coords):
     blocks = rays_ref.shape[0]
-    tiles = out_ref.shape[0] // MOST
-    empty = jnp.full((MOST,) + rays_ref.shape[1:], -2.0, jnp.float32)
-
-    def clear(t, carry):
-        count_ref[t] = 0
-        out_ref[pl.ds(t * MOST, MOST)] = empty
-        return carry
-
-    lax.fori_loop(0, tiles, clear, 0, unroll=4)
-
-    def place(b, carry):
-        t = dest_ref[0, b]
-        rank = count_ref[t]
-        count_ref[t] = rank + 1
-        pltpu.make_async_copy(rays_ref.at[b], out_ref.at[t * MOST + rank], done.at[b]).start()
-        return carry
-
-    lax.fori_loop(0, blocks, place, 0, unroll=4)
-
-    def finish(b, carry):
-        pltpu.make_async_copy(rays_ref.at[b], out_ref.at[b], done.at[b]).wait()
-        return carry
-
-    lax.fori_loop(0, blocks, finish, 0, unroll=4)
+    rows = out_ref.shape[0]
+    shape = (blocks, blocks)
+    earlier = lax.broadcasted_iota(jnp.int32, shape, 0)
+    later = lax.broadcasted_iota(jnp.int32, shape, 1)
+    across = jnp.broadcast_to(dest_ref[...].astype(jnp.float32), shape)
+    down = jnp.sum(jnp.where(earlier == later, across, 0.0), axis=1, keepdims=True)
+    same = jnp.where((down == across) & (earlier < later), 1.0, 0.0)
+    rank = jnp.sum(same, axis=0, keepdims=True)
+    place = (dest_ref[...].astype(jnp.float32) * (2.0 * MOST) + rank).astype(jnp.int32)
+    labels[0:1, :blocks] = place
+    labels[0:1, blocks : 2 * blocks] = place + MOST
+    for b in range(blocks):
+        coords[b : b + 1, :] = rays_ref[b, 0:1, :]
+        coords[blocks + b : blocks + b + 1, :] = rays_ref[b, 1:2, :]
+    target = lax.broadcasted_iota(jnp.int32, (rows, 2 * blocks), 0)
+    chosen = labels[0:1, : 2 * blocks] == target
+    select = jnp.where(chosen, 1.0, 0.0).astype(jnp.bfloat16)
+    rest = coords[...]
+    total = jnp.where(jnp.sum(jnp.where(chosen, 1.0, 0.0), axis=1, keepdims=True) > 0.0, 0.0, -2.0)
+    for _ in range(3):
+        part = rest.astype(jnp.bfloat16)
+        rest = rest - part.astype(jnp.float32)
+        total = total + jnp.dot(select, part, preferred_element_type=jnp.float32)
+    out_ref[...] = total
 
 
 def table_kernel(profile_ref, pairs_ref, last_ref):
@@ -90,18 +89,22 @@
 
 
 def deposit_kernel(rows_axis, cols_axis, rays_ref, tile_ref, send_ref, list_ref):
-    slots, _, rays = rays_ref.shape
-    lane = lax.broadcasted_iota(jnp.int32, (BITS, 128), 1)
-    place = lax.broadcasted_iota(jnp.int32, (BITS, 128), 0)
-    power = jnp.where(lane == 0, (1 << place).astype(jnp.float32), 0.0)
+    sources, held, rays = rays_ref.shape
+    slots = sources * MOST
+    step = 4 * held
+    lane = lax.broadcasted_iota(jnp.int32, (step, LANES), 1)
+    place = lax.broadcasted_iota(jnp.int32, (step, LANES), 0)
+    bit = place // held * MOST + place % held
+    power = jnp.where((lane == 0) & (place % held < MOST), (1 << bit).astype(jnp.float32), 0.0)
     count, empty = jnp.int32(0), jnp.int32(0)
-    for at in range(0, slots, BITS):
-        heads = rays_ref[at : at + BITS, 0, :128]
+    for at in range(0, sources, 4):
+        heads = rays_ref[at : at + 4, :, :LANES].reshape(step, LANES)
         mask = jnp.sum(jnp.where(heads > -1.0, power, 0.0)).astype(jnp.int32)
-        for k in range(BITS):
+        for k in range(4 * MOST):
             filled = (mask >> k) & 1
-            list_ref[count] = at + k
-            empty = jnp.where(filled == 1, empty, at + k)
+            entry = (at + k // MOST) * held + k % MOST
+            list_ref[count] = entry
+            empty = jnp.where(filled == 1, empty, entry)
             count = count + filled
     for k in range(BATCH):
         list_ref[count + k] = empty
@@ -110,15 +113,18 @@
     cell = cell.astype(jnp.bfloat16)
 
     def add(batch, total):
+        firsts, seconds = [], []
         for k in range(BATCH):
-            block = rays_ref[list_ref[batch * BATCH + k]]
-            total = total + lax.dot_general(
-                hats(block[0:1, :], cell),
-                hats(block[1:2, :], cell),
-                (((1,), (1,)), ((), ())),
-                preferred_element_type=jnp.float32,
-            )
-        return total
+            entry = list_ref[batch * BATCH + k]
+            source, slot = entry // held, entry % held
+            firsts.append(hats(rays_ref[source, pl.ds(slot, 1), :], cell))
+            seconds.append(hats(rays_ref[source, pl.ds(slot + MOST, 1), :], cell))
+        return total + lax.dot_general(
+            jnp.concatenate(firsts, axis=1),
+            jnp.concatenate(seconds, axis=1),
+            (((1,), (1,)), ((), ())),
+            preferred_element_type=jnp.float32,
+        )
 
     batches = (count + BATCH - 1) // BATCH
     total = lax.fori_loop(0, batches, add, jnp.zeros((TILE, TILE), jnp.float32))
@@ -185,16 +191,19 @@
     limit = pltpu.CompilerParams(vmem_limit_bytes=32 * 1024 * 1024)
     outgoing = pl.pallas_call(
         place_kernel,
-        out_shape=jax.ShapeDtypeStruct((tiles * MOST, 2, rays), jnp.float32),
-        in_specs=[SMEM, pl.BlockSpec(memory_space=pltpu.HBM)],
+        out_shape=jax.ShapeDtypeStruct((tiles * 2 * MOST, rays), jnp.float32),
+        in_specs=[VMEM, VMEM],
         out_specs=VMEM,
-        scratch_shapes=[pltpu.SMEM((tiles,), jnp.int32), pltpu.SemaphoreType.DMA((blocks,))],
+        scratch_shapes=[
+            pltpu.VMEM((1, max(LANES, 2 * blocks)), jnp.int32),
+            pltpu.VMEM((2 * blocks, rays), jnp.float32),
+        ],
         compiler_params=pltpu.CompilerParams(vmem_limit_bytes=56 * 1024 * 1024),
         name="place",
     )(destination.T, positions)
     received = lax.all_to_all(
-        outgoing.reshape(tiles, MOST, 2, rays), ("row", "col"), split_axis=0, concat_axis=0, tiled=True
-    ).reshape(tiles * MOST, 2, rays)
+        outgoing.reshape(tiles, 2 * MOST, rays), ("row", "col"), split_axis=0, concat_axis=0, tiled=True
+    )
     pairs, last = pl.pallas_call(
         table_kernel,
         out_shape=(

time: 32.1 us -> 32.1 us (level)
  the two profiles are of different devices: /device:TPU:0 before, /device:TPU:1 now
where the time goes in v8:
time: 32.1 us; the launch traced here: 31.9 us
  blocking collectives  12 us (37%)
  starting transfers between devices  7.32 us (23%)
  Pallas kernels  6.14 us (19%)
  waiting for transfers between devices  5.64 us (18%)
  local copies, waits for them, and re-layouts  0.76 us (2%)
    all_to_all x1, blocking collectives, shards(): lax.all_to_all(send, ('row', 'col'), split_axis=0, concat_axis=0, tiled=T...  12 us
    all_to_all x1, starting transfers between devices, shards(): lax.all_to_all(outgoing.reshape(tiles, 2 * MOST, rays), ('row', 'col'), s...  7.32 us
    all_to_all x1, waiting for transfers between devices, shards(): lax.all_to_all(outgoing.reshape(tiles, 2 * MOST, rays), ('row', 'col'), s...  5.64 us
    pallas_call x1, Pallas kernels, shards(): pl.pallas_call(place_kernel, out_shape=jax.ShapeDtypeStruct((tiles * 2 *...  1.86 us
    pallas_call x1, Pallas kernels, shards(): pl.pallas_call(functools.partial(deposit_kernel, 'row', 'col'), out_shape...  1.46 us
    pallas_call x1, Pallas kernels, shards(): pl.pallas_call(table_kernel, out_shape=(jax.ShapeDtypeStruct((STEP // 2,...  1.42 us
    pallas_call x1, Pallas kernels, shards(): pl.pallas_call(functools.partial(spread_kernel, 'row', 'col', scale), out...  1.39 us
    unnamed x2, local copies, waits for them, and re-layouts  0.76 us
  transfers between devices with their start and end apart: 1, of which 1 were waited for; matrix products, arithmetic and copies ran while one was open for 0% of the time, Pallas kernels for 4%

profile of v8, /device:TPU:1, one launch (start us, length us, event | category | flops | bytes accessed | tf_op | source)
XLA Modules:
  0.0 31.9 jit_solution(11852738461920664809)
XLA Ops:
  0.0 1.9 %place.1 = f32[128,384]{1,0:T(8,128)} custom-call(s32[1,16]{1,0:T(1,128)} %bitcast.3, f32[16,2,384]{2,1,0:T(2,128)} %rays_ref.1), custom_call_target="tpu_custom_call" | custom-call | tf_op jit(solution)/shard_map/place/pallas_call | solution.py:192
  1.9 7.3 %all-to-all-start = ((f32[16,8,384]{2,1,0:T(8,128)}), f32[16,8,384]{2,1,0:T(8,128)S(1)}, u32[]{:S(2)}, u32[]{:S(2)}) async-start(f32[16,8,384]{2,1,0:T(8,128)} %bitcast.2), calls=%async_computation | async-start | bytes 393216 | tf_op jit(solution)/shard_map/all_to_all | solution.py:204
  9.2 0.0 copy-start
  9.2 0.8 %copy-done = f32[65,65]{1,0:T(8,128)S(1)} copy-done((f32[65,65]{1,0:T(8,128)S(1)}, f32[65,65]{1,0:T(8,128)}, u32[]{:S(2)}) %copy-start) | copy-done | bytes 16924
  10.0 1.4 %table.1 = (bf16[8,768,256]{2,1,0:T(8,128)(2,1)S(1)}, bf16[192,128]{1,0:T(8,128)(2,1)S(1)}) custom-call(f32[65,65]{1,0:T(8,128)S(1)} %copy-done), custom_call_target="tpu_custom_call" | custom-call | flops 10000000 | bytes 6000000 | tf_op jit(solution)/shard_map/table/pallas_call | solution.py:207
  11.4 5.6 %all-to-all-done.rays_ref = f32[16,8,384]{2,1,0:T(8,128)S(1)} async-done(((f32[16,8,384]{2,1,0:T(8,128)}), f32[16,8,384]{2,1,0:T(8,128)S(1)}, u32[]{:S(2)}, u32[]{:S(2)}) %all-to-all-start) | async-done | bytes 196640 | tf_op jit(solution)/shard_map/all_to_all | solution.py:204
  17.0 1.5 %deposit.1 = (bf16[128,128]{1,0:T(8,128)(2,1)S(1)}, bf16[16,32,128]{2,1,0:T(8,128)(2,1)S(1)}) custom-call(f32[16,8,384]{2,1,0:T(8,128)S(1)} %all-to-all-done.rays_ref), custom_call_target="tpu_custom_call" | custom-call | tf_op jit(solution)/shard_map/deposit/pallas_call | solution.py:220
  18.5 12.0 %all_to_all.10.got_ref = bf16[16,32,128]{2,1,0:T(8,128)(2,1)S(1)} all-to-all(bf16[16,32,128]{2,1,0:T(8,128)(2,1)S(1)} %get-tuple-element.16), channel_id=1, replica_groups=mesh['maps'=2,'row'=4,'col'=4] {'row','col'}, dimensions={0} | all-to-all | bytes 262144 | tf_op jit(solution)/shard_map/all_to_all | solution.py:232
  30.5 1.4 %spread.1 = f32[128,128]{1,0:T(8,128)} custom-call(bf16[128,128]{1,0:T(8,128)(2,1)S(1)} %get-tuple-element.15.tile_ref, bf16[16,32,128]{2,1,0:T(8,128)(2,1)S(1)} %all_to_all.10.got_ref, bf16[8,768,256]{2,1,0:T(8,128)(2,1)S(1)} %get-tuple-element.17.pairs_ref, bf16[192,128]{1,0:T(8,128)(2,1)S(1)} %get-tuple-element.18.last_ref), custom_call_target="tpu_custom_call" | custom-call | tf_op jit(solution)/shard_map/spread/pallas_call | solution.py:234
Async XLA Ops:
  1.9 15.2 %all-to-all-start = ((f32[16,8,384]{2,1,0:T(8,128)}), f32[16,8,384]{2,1,0:T(8,128)S(1)}, u32[]{:S(2)}, u32[]{:S(2)}) async-start(f32[16,8,384]{2,1,0:T(8,128)} %bitcast.2), calls=%async_computation | async-start | bytes 393216 | tf_op jit(solution)/shard_map/all_to_all | solution.py:204
  9.2 0.8 %copy-start = (f32[65,65]{1,0:T(8,128)S(1)}, f32[65,65]{1,0:T(8,128)}, u32[]{:S(2)}) copy-start(f32[65,65]{1,0:T(8,128)} %profile_ref.1) | copy-start | bytes 50704

commit v9 on v4

v9 whole, which is shorter than its diff:
```python
import functools

import jax
import jax.numpy as jnp
from jax import lax
from jax.experimental import pallas as pl
from jax.experimental.pallas import tpu as pltpu
from jax.sharding import PartitionSpec as P

TILE = 128
HALO = 32
MOST = 4
DISC = 2 * HALO + 1
STEP = 16
LONG = TILE + STEP
TURNS = 2 * HALO // STEP
WIDE = TILE + 2 * HALO
DEPTH = TURNS * WIDE
LANES = 128
BATCH = 8
ROOM = 5
NONE = 64.0

VMEM = pl.BlockSpec(memory_space=pltpu.VMEM)
SMEM = pl.BlockSpec(memory_space=pltpu.SMEM)
LIMIT = pltpu.CompilerParams(vmem_limit_bytes=32 * 1024 * 1024)


def touches(distance, least, most):
    before = (distance == -1.0) & (most > TILE - HALO - 1.0)
    after = (distance == 1.0) & (least < HALO)
    return (distance == 0.0) | before | after


def pack_kernel(turn_ref, dest_ref, rays_ref, out_ref, labels, parts):
    blocks, _, rays = rays_ref.shape
    tiles = out_ref.shape[0] // 8
    row_count, col_count = lax.axis_size("row"), lax.axis_size("col")
    lane = lax.broadcasted_iota(jnp.int32, (blocks, LANES), 1)
    place = lax.broadcasted_iota(jnp.int32, (blocks, LANES), 0)

    def laid(column):
        return jnp.sum(jnp.where(lane == place, column, 0.0), axis=0, keepdims=True)

    labels[...] = jnp.full(labels.shape, -1.0, jnp.float32)
    labels[0:1, :blocks] = dest_ref[...].astype(jnp.float32)
    label = labels[...]
    first, second = rays_ref[:, 0, :], rays_ref[:, 1, :]
    least_row, most_row = laid(jnp.min(first, 1, keepdims=True)), laid(jnp.max(first, 1, keepdims=True))
    least_col, most_col = laid(jnp.min(second, 1, keepdims=True)), laid(jnp.max(second, 1, keepdims=True))

    tile = lax.broadcasted_iota(jnp.int32, (tiles, LANES), 0)
    lane = lax.broadcasted_iota(jnp.int32, (tiles, LANES), 1)
    odd = (tile // col_count % 2).astype(jnp.float32)
    base = (tile // col_count).astype(jnp.float32) - odd
    label_row = jnp.floor((label + 0.5) / col_count)
    dc = label - label_row * col_count - (tile % col_count).astype(jnp.float32)
    aside = touches(dc, least_col, most_col) & (label >= 0.0)

    def coded(row):
        dr = label_row - row
        reach = aside & touches(dr, least_row, most_row)
        kind = jnp.where(dr == 0.0, 0.0, 2.0) + jnp.where(dc == 0.0, 0.0, 1.0)
        return reach, jnp.where(reach, 16.0 * kind + 4.0 * (dr + 1.0) + dc + 1.0, NONE)

    reach_even, code_even = coded(base)
    reach_odd, code_odd = coded(base + 1.0)
    reach = jnp.where(reach_even | reach_odd, 1.0, 0.0)
    earlier = lax.broadcasted_iota(jnp.int32, (LANES, LANES), 0)
    later = lax.broadcasted_iota(jnp.int32, (LANES, LANES), 1)
    before = jnp.where(earlier < later, 1.0, 0.0).astype(jnp.bfloat16)
    rank = jnp.dot(reach.astype(jnp.bfloat16), before, preferred_element_type=jnp.float32)
    most = jnp.max(jnp.max((rank + 1.0) * reach, axis=1, keepdims=True), axis=0, keepdims=True)
    turns = jnp.floor((most + (2.0 * ROOM - 0.5)) / (2.0 * ROOM))
    rank = rank - 2.0 * ROOM * turn_ref[0].astype(jnp.float32)
    slot = jnp.floor((rank - odd) * 0.5)
    mine = (reach > 0.0) & (slot * 2.0 + odd == rank) & (slot >= 0.0) & (slot < ROOM)
    slot = jnp.where(mine, slot, -1.0)

    meta = jnp.where(lane == 16, turns, NONE)
    for k in range(ROOM):
        for at, code in ((k, code_even), (8 + k, code_odd)):
            found = jnp.sum(jnp.where(slot == k, code - NONE, 0.0), axis=1, keepdims=True) + NONE
            meta = jnp.where(lane == at, found, meta)

    width = parts.shape[0]
    parts[...] = jnp.zeros(parts.shape, jnp.float32)
    parts[:blocks, :rays] = first
    parts[:blocks, rays:] = second[:, :LANES]
    parts[blocks : 2 * blocks, : 2 * LANES] = second[:, LANES:]
    parts[2 * blocks : 3 * blocks, 2 * LANES :] = second[:, LANES:]
    parts[3 * blocks : 3 * blocks + tiles, 2 * LANES : 3 * LANES] = meta

    source = lax.broadcasted_iota(jnp.int32, (LANES, width), 0)
    target = lax.broadcasted_iota(jnp.int32, (LANES, width), 1)
    wider = jnp.where((target % blocks == source) & (target < 3 * blocks), 1.0, 0.0)
    slot = jnp.dot(
        slot.astype(jnp.bfloat16), wider.astype(jnp.bfloat16), preferred_element_type=jnp.float32
    )
    source = lax.broadcasted_iota(jnp.int32, (8 * tiles, tiles), 1)
    target = lax.broadcasted_iota(jnp.int32, (8 * tiles, tiles), 0)
    taller = jnp.where(target // 8 == source, 1.0, 0.0).astype(jnp.bfloat16)
    slot = jnp.dot(taller, slot.astype(jnp.bfloat16), preferred_element_type=jnp.float32)
    row = lax.broadcasted_iota(jnp.int32, (8 * tiles, width), 0)
    group = lax.broadcasted_iota(jnp.int32, (8 * tiles, width), 1)
    within = row % 8
    low = (2 * (within - ROOM)).astype(jnp.float32)
    head = (group < blocks) & (within < ROOM) & (slot == within.astype(jnp.float32))
    even = (group >= blocks) & (group < 2 * blocks) & (within >= ROOM) & (slot == low)
    uneven = (group >= 2 * blocks) & (group < 3 * blocks) & (within >= ROOM) & (slot == low + 1.0)
    codes = (group - 3 * blocks == row // 8) & (group >= 3 * blocks) & (within == 7)
    select = jnp.where(head | even | uneven | codes, 1.0, 0.0).astype(jnp.bfloat16)
    rest = parts[...]
    total = jnp.zeros(out_ref.shape, jnp.float32)
    for _ in range(3):
        part = rest.astype(jnp.bfloat16)
        rest = rest - part.astype(jnp.float32)
        total = total + jnp.dot(select, part, preferred_element_type=jnp.float32)
    out_ref[...] = total


def table_kernel(profile_ref, pairs_ref, last_ref):
    a = lax.broadcasted_iota(jnp.int32, (DISC, DISC), 0) - HALO
    c = lax.broadcasted_iota(jnp.int32, (DISC, DISC), 1) - HALO
    weights = jnp.where(a * a + c * c <= HALO * HALO, profile_ref[...], 0.0)
    kernel = (weights / jnp.sum(weights)).astype(jnp.bfloat16)
    source = lax.broadcasted_iota(jnp.int32, (DISC, 2 * TILE), 0)
    target = lax.broadcasted_iota(jnp.int32, (DISC, 2 * TILE), 1)
    mirror = jnp.where((source + target) % (2 * TILE) == 0, 1.0, 0.0).astype(jnp.bfloat16)
    mirrored = jnp.dot(kernel, mirror, preferred_element_type=jnp.float32)

    def band(row, first, rows):
        wide = jnp.broadcast_to(mirrored[row : row + 1, :], (rows, 2 * TILE))
        rolled = pltpu.roll(wide, first, 1, stride=1, stride_axis=0)
        return rolled[:, :TILE].astype(jnp.bfloat16)

    for s in range(STEP):
        half = pl.ds((s % 2) * TILE, TILE)
        for u in range(TURNS):
            row = u * STEP + s
            pairs_ref[s // 2, pl.ds(u * TILE, TILE), half] = band(row, HALO, TILE)
            side = TURNS * TILE + u * 2 * HALO
            pairs_ref[s // 2, pl.ds(side, HALO), half] = band(row, 0, HALO)
            pairs_ref[s // 2, pl.ds(side + HALO, HALO), half] = band(row, HALO + TILE, HALO)
    last_ref[:TILE, :] = band(2 * HALO, HALO, TILE)
    last_ref[TILE : TILE + HALO, :] = band(2 * HALO, 0, HALO)
    last_ref[TILE + HALO :, :] = band(2 * HALO, HALO + TILE, HALO)


def hats(coords, offset, cell):
    low = jnp.floor(coords)
    near = jnp.maximum(0.0, 1.0 - jnp.abs(coords - low)).astype(jnp.bfloat16)
    far = jnp.maximum(0.0, 1.0 - jnp.abs(coords - (low + 1.0))).astype(jnp.bfloat16)
    low = low + offset
    here, there = low.astype(jnp.bfloat16), (low + 1.0).astype(jnp.bfloat16)
    zero = jnp.zeros((), jnp.bfloat16)
    return jnp.where(cell == here, near, jnp.where(cell == there, far, zero))


def add_half(got_ref, total, codes, table, done, lists):
    sources = got_ref.shape[0]
    rays = 3 * LANES
    codes[...] = got_ref[:, 7, 2 * LANES : 3 * LANES].astype(jnp.int32)
    copy = pltpu.make_async_copy(codes, table, done)
    copy.start()
    copy.wait()
    room = sources * ROOM + BATCH
    first_lane = lax.axis_index("row") % 2 * 8

    def sort(source, carry):
        turns, counts = carry[0], list(carry[1:])
        turns = jnp.maximum(turns, table[source, 16])
        for k in range(ROOM):
            code = table[source, first_lane + k]
            entry = (source * 8 + k) * 16 + (code & 15)
            kind = code >> 4
            for j in range(4):
                lists[j * room + counts[j]] = entry
                counts[j] = counts[j] + (kind == j).astype(jnp.int32)
        return (turns, *counts)

    turns, *counts = lax.fori_loop(0, sources, sort, (jnp.int32(0),) * 5)

    def cells(extent):
        cell = lax.broadcasted_iota(jnp.int32, (extent, rays), 0)
        if extent != TILE:
            cell = jnp.where(cell < HALO, cell - HALO, cell + (TILE - HALO))
        return cell.astype(jnp.float32).astype(jnp.bfloat16)

    own, halo = cells(TILE), cells(2 * HALO)
    inner, outer = slice(0, TILE), slice(TILE, WIDE)
    for kind, (rows, cols, down, across, batch) in enumerate(
        (
            (inner, inner, own, own, BATCH),
            (inner, outer, own, halo, BATCH // 2),
            (outer, inner, halo, own, BATCH // 2),
            (outer, outer, halo, halo, BATCH // 2),
        )
    ):
        count, base = counts[kind], kind * room
        for k in range(batch):
            lists[base + count + k] = 15

        def add(step, sums, base=base, down=down, across=across, batch=batch):
            firsts, seconds = [], []
            for k in range(batch):
                entry = lists[base + step * batch + k]
                source, slot = entry >> 7, (entry >> 4) & 7
                row_offset = ((((entry >> 2) & 3) - 1) * TILE).astype(jnp.float32)
                col_offset = (((entry & 3) - 1) * TILE).astype(jnp.float32)
                head = got_ref[source, pl.ds(slot, 1), :]
                tail = got_ref[source, pl.ds(ROOM + (slot >> 1), 1), :]
                tail = jnp.where((slot & 1) == 1, tail[:, 2 * LANES :], tail[:, : 2 * LANES])
                second = jnp.concatenate([head[:, rays:], tail], axis=1)
                firsts.append(hats(head[:, :rays], row_offset, down))
                seconds.append(hats(second, col_offset, across))
            return sums + lax.dot_general(
                jnp.concatenate(firsts, axis=1),
                jnp.concatenate(seconds, axis=1),
                (((1,), (1,)), ((), ())),
                preferred_element_type=jnp.float32,
            )

        total[rows, cols] = lax.fori_loop(0, (count + batch - 1) // batch, add, total[rows, cols])
    return turns


def first_kernel(got_ref, before_ref, total_ref, turns_ref, *scratch):
    if before_ref is None:
        total_ref[...] = jnp.zeros(total_ref.shape, jnp.float32)
    else:
        total_ref[...] = before_ref[...]
    turns_ref[0] = add_half(got_ref, total_ref, *scratch)


def second_kernel(scale, got_ref, before_ref, pairs_ref, last_ref, out_ref, total, left, *scratch):
    total[...] = before_ref[...]
    add_half(got_ref, total, *scratch)
    cells = total[...].astype(jnp.bfloat16)
    cells = jnp.concatenate([cells[TILE : TILE + HALO], cells[:TILE], cells[TILE + HALO :]], axis=0)
    own, side = cells[:, :TILE], cells[:, TILE:]
    for u in range(TURNS):
        left[:, u * TILE : (u + 1) * TILE] = own[u * STEP : u * STEP + LONG, :]
        at = TURNS * TILE + u * 2 * HALO
        left[:, at : at + 2 * HALO] = side[u * STEP : u * STEP + LONG, :]
    sums = jnp.dot(own[2 * HALO :, :], last_ref[:TILE, :], preferred_element_type=jnp.float32)
    sums = sums + jnp.dot(side[2 * HALO :, :], last_ref[TILE:, :], preferred_element_type=jnp.float32)
    for p in range(STEP // 2):
        both = jnp.dot(left[...], pairs_ref[p], preferred_element_type=jnp.float32)
        sums = sums + both[2 * p : 2 * p + TILE, :TILE]
        sums = sums + both[2 * p + 1 : 2 * p + 1 + TILE, TILE:]
    out_ref[...] = sums / scale


def shards(positions, destination, profile):
    blocks, _, rays = positions.shape
    row_count, col_count = lax.axis_size("row"), lax.axis_size("col")
    tiles = row_count * col_count
    width = -(-(3 * blocks + tiles) // LANES) * LANES

    def exchange(turn):
        outgoing = pl.pallas_call(
            pack_kernel,
            out_shape=jax.ShapeDtypeStruct((8 * tiles, rays + LANES), jnp.float32),
            in_specs=[SMEM, VMEM, VMEM],
            out_specs=VMEM,
            scratch_shapes=[
                pltpu.VMEM((1, LANES), jnp.float32),
                pltpu.VMEM((width, rays + LANES), jnp.float32),
            ],
            compiler_params=pltpu.CompilerParams(vmem_limit_bytes=56 * 1024 * 1024),
            name="pack",
        )(turn, destination.T, positions)
        return lax.all_to_all(
            outgoing.reshape(tiles, 8, rays + LANES), ("row", "col"), split_axis=0, concat_axis=0, tiled=True
        )

    scratch = [
        pltpu.VMEM((tiles, LANES), jnp.int32),
        pltpu.SMEM((tiles, LANES), jnp.int32),
        pltpu.SemaphoreType.DMA,
        pltpu.SMEM((4 * (tiles * ROOM + BATCH),), jnp.int32),
    ]

    def deposit(mine, before, pairs, last):
        other = lax.ppermute(mine, "row", [(i, i ^ 1) for i in range(row_count)])
        kernel, given = first_kernel, (mine, before)
        if before is None:
            kernel, given = lambda got, *refs: first_kernel(got, None, *refs), (mine,)
        total, turns = pl.pallas_call(
            kernel,
            out_shape=(
                jax.ShapeDtypeStruct((WIDE, WIDE), jnp.float32),
                jax.ShapeDtypeStruct((1,), jnp.int32),
            ),
            in_specs=[VMEM] * len(given),
            out_specs=(VMEM, SMEM),
            scratch_shapes=scratch,
            compiler_params=LIMIT,
            cost_estimate=pl.CostEstimate(flops=2_000_000_000, bytes_accessed=4_000_000, transcendentals=0),
            name="first",
        )(*given)
        out, total = pl.pallas_call(
            functools.partial(second_kernel, blocks * rays / (TILE * TILE)),
            out_shape=(
                jax.ShapeDtypeStruct((TILE, TILE), jnp.float32),
                jax.ShapeDtypeStruct((WIDE, WIDE), jnp.float32),
            ),
            in_specs=[VMEM] * 4,
            out_specs=(VMEM, VMEM),
            scratch_shapes=[pltpu.VMEM((LONG, DEPTH), jnp.bfloat16)] + scratch,
            compiler_params=LIMIT,
            name="second",
        )(other, total, pairs, last)
        return out, total, turns[0]

    mine = exchange(jnp.zeros((1,), jnp.int32))
    pairs, last = pl.pallas_call(
        table_kernel,
        out_shape=(
            jax.ShapeDtypeStruct((STEP // 2, DEPTH, 2 * TILE), jnp.bfloat16),
            jax.ShapeDtypeStruct((WIDE, TILE), jnp.bfloat16),
        ),
        in_specs=[VMEM],
        out_specs=(VMEM, VMEM),
        compiler_params=LIMIT,
        cost_estimate=pl.CostEstimate(flops=10_000_000, bytes_accessed=6_000_000, transcendentals=0),
        name="table",
    )(profile)
    mine, pairs, last = lax.optimization_barrier((mine, pairs, last))
    out, total, turns = deposit(mine, None, pairs, last)

    def more(state):
        turn, _, total = state
        out, total, _ = deposit(exchange(jnp.full((1,), turn, jnp.int32)), total, pairs, last)
        return turn + 1, out, total

    return lax.while_loop(lambda state: state[0] < turns, more, (jnp.int32(1), out, total))[1]


def solution(mesh):
    placed = (P(("maps", "row", "col"), None, None), P(("maps", "row", "col"), None), P())
    return jax.shard_map(
        shards, mesh=mesh, in_specs=placed, out_specs=P(("maps", "row"), "col"), check_vma=False
    )
```

time: 36.2 us -> 29.9 us (0.83)
  blocking collectives: 15 us -> 0 us
  Pallas kernels: 5.02 us -> 14.3 us
  waiting for transfers between devices: 3.01 us -> 5.54 us
  starting transfers between devices: 10.3 us -> 8.15 us
  local copies, waits for them, and re-layouts: 2.4 us -> 0.78 us
  loops' own time: 0 us -> 0.69 us
    all_to_all x1 -> x0, blocking collectives: 15 us -> none  [shards(): lax.all_to_all(outgoing.reshape(tiles, MOST, 2, rays), ('row', 'col'), sp...]
    ppermute x4 -> x1, starting transfers between devices: 10.3 us -> 0.82 us  [deposit(): other = lax.ppermute(mine, 'row', [(i, i ^ 1) for i in range(row_count)])]
    pallas_call x3, Pallas kernels: 3.6 us -> 11.3 us  [the longest x1 4.99 us: deposit(): pl.pallas_call(functools.partial(second_kernel, blocks * rays / (TILE * T...]
    all_to_all x0 -> x1, starting transfers between devices: none -> 7.33 us  [exchange(): lax.all_to_all(outgoing.reshape(tiles, 8, rays + LANES), ('row', 'col'),...]
    all_to_all x0 -> x1, waiting for transfers between devices: none -> 5.54 us  [exchange(): lax.all_to_all(outgoing.reshape(tiles, 8, rays + LANES), ('row', 'col'),...]
    ppermute x4 -> x1, waiting for transfers between devices: 3.01 us -> 0.01 us  [deposit(): other = lax.ppermute(mine, 'row', [(i, i ^ 1) for i in range(row_count)])]
    pallas_call x1, Pallas kernels: 1.42 us -> 3.04 us  [shards(): pl.pallas_call(table_kernel, out_shape=(jax.ShapeDtypeStruct((STEP // 2,...]
    unnamed x7 -> x8, local copies, waits for them, and re-layouts: 2.31 us -> 0.78 us
  transfers between devices with their start and end apart: 4 -> 2, of which waited for: 1 -> 1; matrix products, arithmetic and copies ran while one was open for 0% -> 0% of each run, Pallas kernels for 4% -> 24%
where the time goes in v9:
time: 29.9 us; the launch traced here: 29.5 us
  Pallas kernels  14.3 us (48%)
  starting transfers between devices  8.15 us (27%)
  waiting for transfers between devices  5.54 us (19%)
  local copies, waits for them, and re-layouts  0.78 us (3%)
  loops' own time  0.69 us (2%)
    all_to_all x1, starting transfers between devices, exchange(): lax.all_to_all(outgoing.reshape(tiles, 8, rays + LANES), ('row', 'col'),...  7.33 us
    all_to_all x1, waiting for transfers between devices, exchange(): lax.all_to_all(outgoing.reshape(tiles, 8, rays + LANES), ('row', 'col'),...  5.54 us
    pallas_call x1, Pallas kernels, deposit(): pl.pallas_call(functools.partial(second_kernel, blocks * rays / (TILE * T...  4.99 us
    pallas_call x1, Pallas kernels, deposit(): pl.pallas_call(kernel, out_shape=(jax.ShapeDtypeStruct((WIDE, WIDE), jnp....  3.94 us
    pallas_call x1, Pallas kernels, shards(): pl.pallas_call(table_kernel, out_shape=(jax.ShapeDtypeStruct((STEP // 2,...  3.04 us
    pallas_call x1, Pallas kernels, exchange(): pl.pallas_call(pack_kernel, out_shape=jax.ShapeDtypeStruct((8 * tiles, ra...  2.32 us
    ppermute x1, starting transfers between devices, deposit(): other = lax.ppermute(mine, 'row', [(i, i ^ 1) for i in range(row_count)])  0.82 us
    unnamed x8, local copies, waits for them, and re-layouts  0.78 us
  transfers between devices with their start and end apart: 2, of which 1 were waited for; matrix products, arithmetic and copies ran while one was open for 0% of the time, Pallas kernels for 24%

profile of v9, /device:TPU:1, one launch (start us, length us, event | category | flops | bytes accessed | tf_op | source)
XLA Modules:
  0.0 29.5 jit_solution(14996111188852525224)
XLA Ops:
  0.0 2.3 %pack.2 = f32[128,512]{1,0:T(8,128)} custom-call(s32[1]{0:T(128)} %constant.2.clone.1.turn_ref, s32[1,16]{1,0:T(1,128)} %bitcast.14, f32[16,2,384]{2,1,0:T(2,128)} %rays_ref.1), custom_call_target="tpu_custom_call" | custom-call | tf_op jit(solution)/shard_map/pack/pallas_call | solution.py:262
  2.3 7.3 %all-to-all-start.1 = ((f32[16,8,512]{2,1,0:T(8,128)}), f32[16,8,512]{2,1,0:T(8,128)S(1)}, u32[]{:S(2)}, u32[]{:S(2)}) async-start(f32[16,8,512]{2,1,0:T(8,128)} %bitcast.13), calls=%async_computation.1 | async-start | bytes 524288 | tf_op jit(solution)/shard_map/all_to_all | solution.py:274
  9.7 0.0 copy-start
  9.7 0.8 %copy-done = f32[65,65]{1,0:T(8,128)S(1)} copy-done((f32[65,65]{1,0:T(8,128)S(1)}, f32[65,65]{1,0:T(8,128)}, u32[]{:S(2)}) %copy-start) | copy-done | bytes 16924
  10.4 3.0 %table.1 = (bf16[8,768,256]{2,1,0:T(8,128)(2,1)}, bf16[192,128]{1,0:T(8,128)(2,1)S(1)}) custom-call(f32[65,65]{1,0:T(8,128)S(1)} %copy-done), custom_call_target="tpu_custom_call" | custom-call | flops 10000000 | bytes 6000000 | tf_op jit(solution)/shard_map/table/pallas_call | solution.py:318
  13.5 5.5 %all-to-all-done.1.got = f32[16,8,512]{2,1,0:T(8,128)S(1)} async-done(((f32[16,8,512]{2,1,0:T(8,128)}), f32[16,8,512]{2,1,0:T(8,128)S(1)}, u32[]{:S(2)}, u32[]{:S(2)}) %all-to-all-start.1) | async-done | bytes 262176 | tf_op jit(solution)/shard_map/all_to_all | solution.py:274
  19.0 0.8 %collective-permute-start.1 = (f32[16,8,512]{2,1,0:T(8,128)S(1)}, f32[16,8,512]{2,1,0:T(8,128)S(1)}, u32[]{:S(2)}, u32[]{:S(2)}) collective-permute-start(f32[16,8,512]{2,1,0:T(8,128)S(1)} %all-to-all-done.1.got), channel_id=1, source_target_pairs={{0,4},{4,0},{8,12},{12,8},{1,5},{5,1},{9,13},{13,9},{2,6},{6,2},{1... | collective-permute-start | bytes 786440 | tf_op jit(solution)/shard_map/ppermute | solution.py:286
  19.8 0.0 copy-start.1
  19.8 3.9 %first.2 = (f32[192,192]{1,0:T(8,128)S(1)}, s32[1]{0:T(128)}) custom-call(f32[16,8,512]{2,1,0:T(8,128)S(1)} %all-to-all-done.1.got), custom_call_target="tpu_custom_call" | custom-call | flops 2000000000 | bytes 4000000 | tf_op jit(solution)/shard_map/first/pallas_call | solution.py:290
  23.8 0.0 copy-start.3
  23.8 0.0 copy-start.4
  23.8 0.0 collective-permute-done.1.got_ref
  23.8 0.0 copy-done.1
  23.8 5.0 %second.2 = (f32[128,128]{1,0:T(8,128)}, f32[192,192]{1,0:T(8,128)S(1)}) custom-call(f32[16,8,512]{2,1,0:T(8,128)S(1)} %collective-permute-done.1.got_ref, f32[192,192]{1,0:T(8,128)S(1)} %get-tuple-element.62.before_ref, bf16[8,768,256]{2,1,0:T(8,128)(2,1)S(1)} %copy-done.1, bf16[192,128]{1,0:T(8,128)(2,1)S(1)} %get-tuple-element.146.last_ref), custom_call_target="tpu_custom_call" | custom-call | tf_op jit(solution)/shard_map/second/pallas_call | solution.py:303
  28.8 0.0 copy-done.3
  28.8 0.0 copy-done.4
  28.8 0.7 %while.12 = (s32[]{:T(128)}, f32[128,128]{1,0:T(8,128)}, f32[192,192]{1,0:T(8,128)S(1)}, s32[]{:T(128)}, s32[16,1]{0,1:T(1,128)S(1)}, /*index=5*/f32[16,2,384]{2...) while((s32[]{:T(128)}, f32[128,128]{1,0:T(8,128)}, ...), condition=%wide.region_1.0_spmd, body=%wide.region_0.0_spmd.sunk | while | flops 2000000000 | bytes 18155936 | solution.py:338
Async XLA Ops:
  2.3 16.7 %all-to-all-start.1 = ((f32[16,8,512]{2,1,0:T(8,128)}), f32[16,8,512]{2,1,0:T(8,128)S(1)}, u32[]{:S(2)}, u32[]{:S(2)}) async-start(f32[16,8,512]{2,1,0:T(8,128)} %bitcast.13), calls=%async_computation.1 | async-start | bytes 524288 | tf_op jit(solution)/shard_map/all_to_all | solution.py:274
  9.7 0.8 %copy-start = (f32[65,65]{1,0:T(8,128)S(1)}, f32[65,65]{1,0:T(8,128)}, u32[]{:S(2)}) copy-start(f32[65,65]{1,0:T(8,128)} %profile_ref.1) | copy-start | bytes 50704
  19.0 4.8 %collective-permute-start.1 = (f32[16,8,512]{2,1,0:T(8,128)S(1)}, f32[16,8,512]{2,1,0:T(8,128)S(1)}, u32[]{:S(2)}, u32[]{:S(2)}) collective-permute-start(f32[16,8,512]{2,1,0:T(8,128)S(1)} %all-to-all-done.1.got), channel_id=1, source_target_pairs={{0,4},{4,0},{8,12},{12,8},{1,5},{5,1},{9,13},{13,9},{2,6},{6,2},{1... | collective-permute-start | bytes 786440 | tf_op jit(solution)/shard_map/ppermute | solution.py:286
  19.8 4.0 %copy-start.1 = (bf16[8,768,256]{2,1,0:T(8,128)(2,1)S(1)}, bf16[8,768,256]{2,1,0:T(8,128)(2,1)}, u32[]{:S(2)}) copy-start(bf16[8,768,256]{2,1,0:T(8,128)(2,1)} %get-tuple-element.145.pairs_ref) | copy-start | bytes 9437188
  23.8 5.0 %copy-start.3 = (f32[16,2,384]{2,1,0:T(2,128)S(1)}, f32[16,2,384]{2,1,0:T(2,128)}, u32[]{:S(2)}) copy-start(f32[16,2,384]{2,1,0:T(2,128)} %rays_ref.1) | copy-start | bytes 147460
  23.8 5.0 %copy-start.4 = (s32[16,1]{0,1:T(1,128)S(1)}, s32[16,1]{0,1:T(1,128)}, u32[]{:S(2)}) copy-start(s32[16,1]{0,1:T(1,128)} %param.6) | copy-start | bytes 196

commit v10 on v9

--- a/solution.py
+++ b/solution.py
@@ -147,17 +147,13 @@
     last_ref[TILE + HALO :, :] = band(2 * HALO, HALO + TILE, HALO)
 
 
-def hats(coords, offset, cell):
-    low = jnp.floor(coords)
-    near = jnp.maximum(0.0, 1.0 - jnp.abs(coords - low)).astype(jnp.bfloat16)
-    far = jnp.maximum(0.0, 1.0 - jnp.abs(coords - (low + 1.0))).astype(jnp.bfloat16)
-    low = low + offset
-    here, there = low.astype(jnp.bfloat16), (low + 1.0).astype(jnp.bfloat16)
+def hats(row, cell):
+    near, far, here, there = (value.astype(jnp.bfloat16) for value in row)
     zero = jnp.zeros((), jnp.bfloat16)
-    return jnp.where(cell == here, near, jnp.where(cell == there, far, zero))
-
-
-def add_half(got_ref, total, codes, table, done, lists):
+    return jnp.maximum(zero, jnp.minimum((cell - here) + near, (there - cell) + far))
+
+
+def add_half(got_ref, total, codes, table, done, lists, stage, facts):
     sources = got_ref.shape[0]
     rays = 3 * LANES
     codes[...] = got_ref[:, 7, 2 * LANES : 3 * LANES].astype(jnp.int32)
@@ -168,8 +164,7 @@
     first_lane = lax.axis_index("row") % 2 * 8
 
     def sort(source, carry):
-        turns, counts = carry[0], list(carry[1:])
-        turns = jnp.maximum(turns, table[source, 16])
+        counts = list(carry)
         for k in range(ROOM):
             code = table[source, first_lane + k]
             entry = (source * 8 + k) * 16 + (code & 15)
@@ -177,15 +172,15 @@
             for j in range(4):
                 lists[j * room + counts[j]] = entry
                 counts[j] = counts[j] + (kind == j).astype(jnp.int32)
-        return (turns, *counts)
-
-    turns, *counts = lax.fori_loop(0, sources, sort, (jnp.int32(0),) * 5)
+        return tuple(counts)
+
+    counts = lax.fori_loop(0, sources, sort, (jnp.int32(0),) * 4)
 
     def cells(extent):
         cell = lax.broadcasted_iota(jnp.int32, (extent, rays), 0)
         if extent != TILE:
             cell = jnp.where(cell < HALO, cell - HALO, cell + (TILE - HALO))
-        return cell.astype(jnp.float32).astype(jnp.bfloat16)
+        return (2 * cell).astype(jnp.float32).astype(jnp.bfloat16)
 
     own, halo = cells(TILE), cells(2 * HALO)
     inner, outer = slice(0, TILE), slice(TILE, WIDE)
@@ -202,18 +197,33 @@
             lists[base + count + k] = 15
 
         def add(step, sums, base=base, down=down, across=across, batch=batch):
-            firsts, seconds = [], []
             for k in range(batch):
                 entry = lists[base + step * batch + k]
                 source, slot = entry >> 7, (entry >> 4) & 7
-                row_offset = ((((entry >> 2) & 3) - 1) * TILE).astype(jnp.float32)
-                col_offset = (((entry & 3) - 1) * TILE).astype(jnp.float32)
+                row_offset = ((((entry >> 2) & 3) - 1) * (2 * TILE)).astype(jnp.float32)
+                col_offset = (((entry & 3) - 1) * (2 * TILE)).astype(jnp.float32)
                 head = got_ref[source, pl.ds(slot, 1), :]
                 tail = got_ref[source, pl.ds(ROOM + (slot >> 1), 1), :]
-                tail = jnp.where((slot & 1) == 1, tail[:, 2 * LANES :], tail[:, : 2 * LANES])
-                second = jnp.concatenate([head[:, rays:], tail], axis=1)
-                firsts.append(hats(head[:, :rays], row_offset, down))
-                seconds.append(hats(second, col_offset, across))
+                stage[0, k : k + 1, :] = head[:, :rays]
+                stage[1, k : k + 1, :LANES] = head[:, rays:]
+                stage[1, k : k + 1, LANES:] = jnp.where(
+                    (slot & 1) == 1, tail[:, 2 * LANES :], tail[:, : 2 * LANES]
+                )
+                stage[2, k : k + 1, :] = jnp.full((1, rays), row_offset)
+                stage[3, k : k + 1, :] = jnp.full((1, rays), col_offset)
+            for axis in range(2):
+                coords = stage[axis]
+                low = jnp.floor(coords)
+                facts[4 * axis] = 1.0 - (coords - low)
+                facts[4 * axis + 1] = 1.0 - ((low + 1.0) - coords)
+                here = 2.0 * low + stage[2 + axis]
+                facts[4 * axis + 2] = here
+                facts[4 * axis + 3] = here + 2.0
+            firsts, seconds = [], []
+            for k in range(batch):
+                row = [facts[j, k : k + 1, :] for j in range(8)]
+                firsts.append(hats(row[:4], down))
+                seconds.append(hats(row[4:], across))
             return sums + lax.dot_general(
                 jnp.concatenate(firsts, axis=1),
                 jnp.concatenate(seconds, axis=1),
@@ -222,15 +232,14 @@
             )
 
         total[rows, cols] = lax.fori_loop(0, (count + batch - 1) // batch, add, total[rows, cols])
-    return turns
-
-
-def first_kernel(got_ref, before_ref, total_ref, turns_ref, *scratch):
+
+
+def first_kernel(got_ref, before_ref, total_ref, *scratch):
     if before_ref is None:
         total_ref[...] = jnp.zeros(total_ref.shape, jnp.float32)
     else:
         total_ref[...] = before_ref[...]
-    turns_ref[0] = add_half(got_ref, total_ref, *scratch)
+    add_half(got_ref, total_ref, *scratch)
 
 
 def second_kernel(scale, got_ref, before_ref, pairs_ref, last_ref, out_ref, total, left, *scratch):
@@ -280,6 +289,8 @@
         pltpu.SMEM((tiles, LANES), jnp.int32),
         pltpu.SemaphoreType.DMA,
         pltpu.SMEM((4 * (tiles * ROOM + BATCH),), jnp.int32),
+        pltpu.VMEM((4, BATCH, rays), jnp.float32),
+        pltpu.VMEM((8, BATCH, rays), jnp.float32),
     ]
 
     def deposit(mine, before, pairs, last):
@@ -287,14 +298,11 @@
         kernel, given = first_kernel, (mine, before)
         if before is None:
             kernel, given = lambda got, *refs: first_kernel(got, None, *refs), (mine,)
-        total, turns = pl.pallas_call(
+        total = pl.pallas_call(
             kernel,
-            out_shape=(
-                jax.ShapeDtypeStruct((WIDE, WIDE), jnp.float32),
-                jax.ShapeDtypeStruct((1,), jnp.int32),
-            ),
+            out_shape=jax.ShapeDtypeStruct((WIDE, WIDE), jnp.float32),
             in_specs=[VMEM] * len(given),
-            out_specs=(VMEM, SMEM),
+            out_specs=VMEM,
             scratch_shapes=scratch,
             compiler_params=LIMIT,
             cost_estimate=pl.CostEstimate(flops=2_000_000_000, bytes_accessed=4_000_000, transcendentals=0),
@@ -312,7 +320,7 @@
             compiler_params=LIMIT,
             name="second",
         )(other, total, pairs, last)
-        return out, total, turns[0]
+        return out, total
 
     mine = exchange(jnp.zeros((1,), jnp.int32))
     pairs, last = pl.pallas_call(
@@ -328,11 +336,12 @@
         name="table",
     )(profile)
     mine, pairs, last = lax.optimization_barrier((mine, pairs, last))
-    out, total, turns = deposit(mine, None, pairs, last)
+    out, total = deposit(mine, None, pairs, last)
+    turns = jnp.max(mine[:, 7, 2 * LANES + 16]).astype(jnp.int32)
 
     def more(state):
         turn, _, total = state
-        out, total, _ = deposit(exchange(jnp.full((1,), turn, jnp.int32)), total, pairs, last)
+        out, total = deposit(exchange(jnp.full((1,), turn, jnp.int32)), total, pairs, last)
         return turn + 1, out, total
 
     return lax.while_loop(lambda state: state[0] < turns, more, (jnp.int32(1), out, total))[1]

time: 29.9 us -> 31.1 us (1.040)
  Pallas kernels: 14.3 us -> 15 us
  other arithmetic: 0 us -> 0.69 us
  loops' own time: 0.69 us -> 0.01 us
  between operations: 0.07 us -> 0.73 us
    pallas_call x1, Pallas kernels: 4.99 us -> 6.13 us  [deposit(): pl.pallas_call(functools.partial(second_kernel, blocks * rays / (TILE * T...]
    reduce_max x0 -> x1, other arithmetic: none -> 0.69 us  [shards(): turns = jnp.max(mine[:, 7, 2 * LANES + 16]).astype(jnp.int32)]
    another operation x1, loops' own time: 0.69 us -> 0.01 us  [shards(): lax.while_loop(lambda state: state[0] < turns, more, (jnp.int32(1), out,...]
    pallas_call x1, Pallas kernels: 3.94 us -> 3.52 us  [deposit(): pl.pallas_call(kernel, out_shape=jax.ShapeDtypeStruct((WIDE, WIDE), jnp.f...]
  transfers between devices with their start and end apart: 2 -> 2, of which waited for: 1 -> 1; matrix products, arithmetic and copies ran while one was open for 0% -> 2% of each run, Pallas kernels for 24% -> 21%
where the time goes in v10:
time: 31.1 us; the launch traced here: 30.9 us
  Pallas kernels  15 us (48%)
  starting transfers between devices  8.15 us (26%)
  waiting for transfers between devices  5.54 us (18%)
  local copies, waits for them, and re-layouts  0.78 us (3%)
  between operations  0.73 us (2%)
  other arithmetic  0.69 us (2%)
    all_to_all x1, starting transfers between devices, exchange(): lax.all_to_all(outgoing.reshape(tiles, 8, rays + LANES), ('row', 'col'),...  7.33 us
    pallas_call x1, Pallas kernels, deposit(): pl.pallas_call(functools.partial(second_kernel, blocks * rays / (TILE * T...  6.13 us
    all_to_all x1, waiting for transfers between devices, exchange(): lax.all_to_all(outgoing.reshape(tiles, 8, rays + LANES), ('row', 'col'),...  5.54 us
    pallas_call x1, Pallas kernels, deposit(): pl.pallas_call(kernel, out_shape=jax.ShapeDtypeStruct((WIDE, WIDE), jnp.f...  3.52 us
    pallas_call x1, Pallas kernels, shards(): pl.pallas_call(table_kernel, out_shape=(jax.ShapeDtypeStruct((STEP // 2,...  3.04 us
    pallas_call x1, Pallas kernels, exchange(): pl.pallas_call(pack_kernel, out_shape=jax.ShapeDtypeStruct((8 * tiles, ra...  2.33 us
    ppermute x1, starting transfers between devices, deposit(): other = lax.ppermute(mine, 'row', [(i, i ^ 1) for i in range(row_count)])  0.82 us
    unnamed x8, local copies, waits for them, and re-layouts  0.78 us
  transfers between devices with their start and end apart: 2, of which 1 were waited for; matrix products, arithmetic and copies ran while one was open for 2% of the time, Pallas kernels for 21%

profile of v10, /device:TPU:1, one launch (start us, length us, event | category | flops | bytes accessed | tf_op | source)
XLA Modules:
  0.0 30.9 jit_solution(4920755455556644848)
XLA Ops:
  0.0 2.3 %pack.2 = f32[128,512]{1,0:T(8,128)} custom-call(s32[1]{0:T(128)} %constant.2.clone.1.turn_ref, s32[1,16]{1,0:T(1,128)} %bitcast.13, f32[16,2,384]{2,1,0:T(2,128)} %rays_ref.1), custom_call_target="tpu_custom_call" | custom-call | tf_op jit(solution)/shard_map/pack/pallas_call | solution.py:271
  2.3 7.3 %all-to-all-start.1 = ((f32[16,8,512]{2,1,0:T(8,128)}), f32[16,8,512]{2,1,0:T(8,128)S(1)}, u32[]{:S(2)}, u32[]{:S(2)}) async-start(f32[16,8,512]{2,1,0:T(8,128)} %bitcast.12), calls=%async_computation.1 | async-start | bytes 524288 | tf_op jit(solution)/shard_map/all_to_all | solution.py:283
  9.7 0.0 copy-start
  9.7 0.8 %copy-done = f32[65,65]{1,0:T(8,128)S(1)} copy-done((f32[65,65]{1,0:T(8,128)S(1)}, f32[65,65]{1,0:T(8,128)}, u32[]{:S(2)}) %copy-start) | copy-done | bytes 16924
  10.4 3.0 %table.1 = (bf16[8,768,256]{2,1,0:T(8,128)(2,1)}, bf16[192,128]{1,0:T(8,128)(2,1)S(1)}) custom-call(f32[65,65]{1,0:T(8,128)S(1)} %copy-done), custom_call_target="tpu_custom_call" | custom-call | flops 10000000 | bytes 6000000 | tf_op jit(solution)/shard_map/table/pallas_call | solution.py:326
  13.5 5.5 %all-to-all-done.1.got = f32[16,8,512]{2,1,0:T(8,128)S(1)} async-done(((f32[16,8,512]{2,1,0:T(8,128)}), f32[16,8,512]{2,1,0:T(8,128)S(1)}, u32[]{:S(2)}, u32[]{:S(2)}) %all-to-all-start.1) | async-done | bytes 262176 | tf_op jit(solution)/shard_map/all_to_all | solution.py:283
  19.0 0.8 %collective-permute-start.1 = (f32[16,8,512]{2,1,0:T(8,128)S(1)}, f32[16,8,512]{2,1,0:T(8,128)S(1)}, u32[]{:S(2)}, u32[]{:S(2)}) collective-permute-start(f32[16,8,512]{2,1,0:T(8,128)S(1)} %all-to-all-done.1.got), channel_id=1, source_target_pairs={{0,4},{4,0},{8,12},{12,8},{1,5},{5,1},{9,13},{13,9},{2,6},{6,2},{1... | collective-permute-start | bytes 786440 | tf_op jit(solution)/shard_map/ppermute | solution.py:297
  19.8 0.7 %slice_reduce_fusion = f32[]{:T(128)} fusion(f32[16,8,512]{2,1,0:T(8,128)S(1)} %all-to-all-done.1.got), kind=kLoop, calls=%fused_computation | loop fusion | flops 15 | bytes 68 | tf_op jit(solution)/shard_map/reduce_max | solution.py:340
  21.2 0.0 copy-start.1
  21.2 3.5 %first.2.before_ref = f32[192,192]{1,0:T(8,128)S(1)} custom-call(f32[16,8,512]{2,1,0:T(8,128)S(1)} %all-to-all-done.1.got), custom_call_target="tpu_custom_call" | custom-call | flops 2000000000 | bytes 4000000 | tf_op jit(solution)/shard_map/first/pallas_call | solution.py:301
  24.7 0.0 copy-start.3
  24.7 0.0 copy-start.4
  24.7 0.0 collective-permute-done.1.got_ref
  24.7 0.0 copy-done.1
  24.7 6.1 %second.2 = (f32[128,128]{1,0:T(8,128)}, f32[192,192]{1,0:T(8,128)S(1)}) custom-call(f32[16,8,512]{2,1,0:T(8,128)S(1)} %collective-permute-done.1.got_ref, f32[192,192]{1,0:T(8,128)S(1)} %first.2.before_ref, bf16[8,768,256]{2,1,0:T(8,128)(2,1)S(1)} %copy-done.1, bf16[192,128]{1,0:T(8,128)(2,1)S(1)} %get-tuple-element.139.last_ref), custom_call_target="tpu_custom_call" | custom-call | tf_op jit(solution)/shard_map/second/pallas_call | solution.py:311
  30.9 0.0 copy-done.3
  30.9 0.0 copy-done.4
  (1 shorter events, 0.0 us)
Async XLA Ops:
  2.3 16.7 %all-to-all-start.1 = ((f32[16,8,512]{2,1,0:T(8,128)}), f32[16,8,512]{2,1,0:T(8,128)S(1)}, u32[]{:S(2)}, u32[]{:S(2)}) async-start(f32[16,8,512]{2,1,0:T(8,128)} %bitcast.12), calls=%async_computation.1 | async-start | bytes 524288 | tf_op jit(solution)/shard_map/all_to_all | solution.py:283
  9.7 0.8 %copy-start = (f32[65,65]{1,0:T(8,128)S(1)}, f32[65,65]{1,0:T(8,128)}, u32[]{:S(2)}) copy-start(f32[65,65]{1,0:T(8,128)} %profile_ref.1) | copy-start | bytes 50704
  19.0 5.7 %collective-permute-start.1 = (f32[16,8,512]{2,1,0:T(8,128)S(1)}, f32[16,8,512]{2,1,0:T(8,128)S(1)}, u32[]{:S(2)}, u32[]{:S(2)}) collective-permute-start(f32[16,8,512]{2,1,0:T(8,128)S(1)} %all-to-all-done.1.got), channel_id=1, source_target_pairs={{0,4},{4,0},{8,12},{12,8},{1,5},{5,1},{9,13},{13,9},{2,6},{6,2},{1... | collective-permute-start | bytes 786440 | tf_op jit(solution)/shard_map/ppermute | solution.py:297
  21.2 3.6 %copy-start.1 = (bf16[8,768,256]{2,1,0:T(8,128)(2,1)S(1)}, bf16[8,768,256]{2,1,0:T(8,128)(2,1)}, u32[]{:S(2)}) copy-start(bf16[8,768,256]{2,1,0:T(8,128)(2,1)} %get-tuple-element.138.pairs_ref) | copy-start | bytes 9437188
  24.7 6.2 %copy-start.3 = (f32[16,2,384]{2,1,0:T(2,128)S(1)}, f32[16,2,384]{2,1,0:T(2,128)}, u32[]{:S(2)}) copy-start(f32[16,2,384]{2,1,0:T(2,128)} %rays_ref.1) | copy-start | bytes 147460
  24.7 6.2 %copy-start.4 = (s32[16,1]{0,1:T(1,128)S(1)}, s32[16,1]{0,1:T(1,128)}, u32[]{:S(2)}) copy-start(s32[16,1]{0,1:T(1,128)} %param.6) | copy-start | bytes 196

commit v11 on v9

v11 whole, which is shorter than its diff:
```python
import functools

import jax
import jax.numpy as jnp
from jax import lax
from jax.experimental import pallas as pl
from jax.experimental.pallas import tpu as pltpu
from jax.sharding import PartitionSpec as P

TILE = 128
HALO = 32
MOST = 4
DISC = 2 * HALO + 1
STEP = 16
LONG = TILE + STEP
TURNS = 2 * HALO // STEP
WIDE = TILE + 2 * HALO
LANES = 128
SPAN = 64
BATCH = 4
ROOM = 5
NONE = 64.0

VMEM = pl.BlockSpec(memory_space=pltpu.VMEM)
SMEM = pl.BlockSpec(memory_space=pltpu.SMEM)
LIMIT = pltpu.CompilerParams(vmem_limit_bytes=32 * 1024 * 1024)


def touches(distance, least, most):
    before = (distance == -1.0) & (most > TILE - HALO - 1.0)
    after = (distance == 1.0) & (least < HALO)
    return (distance == 0.0) | before | after


def pack_kernel(turn_ref, dest_ref, rays_ref, out_ref, labels, parts):
    blocks, _, rays = rays_ref.shape
    tiles = out_ref.shape[0] // 8
    width = parts.shape[0]
    col_count = lax.axis_size("col")
    skip = 0.0 if turn_ref is None else 2.0 * ROOM * turn_ref[0].astype(jnp.float32)
    lane = lax.broadcasted_iota(jnp.int32, (blocks, width), 1)
    place = lax.broadcasted_iota(jnp.int32, (blocks, width), 0)
    there = (lane % blocks == place) & (lane < 3 * blocks)

    def laid(column):
        return jnp.sum(jnp.where(there, column, 0.0), axis=0, keepdims=True)

    labels[...] = jnp.full(labels.shape, -1.0, jnp.float32)
    for g in range(3):
        labels[0:1, g * blocks : (g + 1) * blocks] = dest_ref[...].astype(jnp.float32)
    label = labels[...]
    label_row = jnp.floor((label + 0.5) / col_count)
    label_col = label - label_row * col_count
    first, second = rays_ref[:, 0, :], rays_ref[:, 1, :]
    least_row, most_row = laid(jnp.min(first, 1, keepdims=True)), laid(jnp.max(first, 1, keepdims=True))
    least_col, most_col = laid(jnp.min(second, 1, keepdims=True)), laid(jnp.max(second, 1, keepdims=True))
    earlier = lax.broadcasted_iota(jnp.int32, (width, width), 0)
    later = lax.broadcasted_iota(jnp.int32, (width, width), 1)
    earlier = jnp.where((earlier < later % blocks) & (later < 3 * blocks), 1.0, 0.0).astype(jnp.bfloat16)

    def chosen(tile):
        odd = (tile // col_count % 2).astype(jnp.float32)
        row = (tile // col_count).astype(jnp.float32) - odd
        dc = label_col - (tile % col_count).astype(jnp.float32)
        aside = touches(dc, least_col, most_col) & (label >= 0.0)

        def coded(dr):
            reach = aside & touches(dr, least_row, most_row)
            kind = jnp.where(dr == 0.0, 0.0, 16.0)
            return reach, jnp.where(reach, kind + 4.0 * (dr + 1.0) + dc + 1.0, NONE)

        reach_even, code_even = coded(label_row - row)
        reach_odd, code_odd = coded(label_row - row - 1.0)
        reach = jnp.where(reach_even | reach_odd, 1.0, 0.0)
        rank = jnp.dot(reach.astype(jnp.bfloat16), earlier, preferred_element_type=jnp.float32)
        left = rank - skip - odd
        slot = jnp.floor(left * 0.5)
        mine = (reach > 0.0) & (slot * 2.0 == left) & (slot >= 0.0) & (slot < ROOM)
        return jnp.where(mine, slot, -1.0), code_even, code_odd, (rank + 1.0) * reach

    slot, code_even, code_odd, most = chosen(lax.broadcasted_iota(jnp.int32, (tiles, width), 0))
    most = jnp.max(jnp.max(most, axis=1, keepdims=True), axis=0, keepdims=True)
    turns = jnp.floor((most + (2.0 * ROOM - 0.5)) / (2.0 * ROOM))
    lane = lax.broadcasted_iota(jnp.int32, (tiles, width), 1)
    meta = jnp.where(lane == 16, turns, NONE)
    for k in range(ROOM):
        for at, code in ((k, code_even), (8 + k, code_odd)):
            here = (slot == k) & (lane < blocks)
            found = jnp.sum(jnp.where(here, code - NONE, 0.0), axis=1, keepdims=True) + NONE
            meta = jnp.where(lane == at, found, meta)

    parts[...] = jnp.zeros(parts.shape, jnp.float32)
    parts[:blocks, :rays] = first
    parts[:blocks, rays:] = second[:, :LANES]
    parts[blocks : 2 * blocks, : 2 * LANES] = second[:, LANES:]
    parts[2 * blocks : 3 * blocks, 2 * LANES :] = second[:, LANES:]
    parts[3 * blocks : 3 * blocks + tiles, 2 * LANES : 3 * LANES] = meta[:, :LANES]

    row = lax.broadcasted_iota(jnp.int32, (8 * tiles, width), 0)
    group = lax.broadcasted_iota(jnp.int32, (8 * tiles, width), 1)
    slot = chosen(row // 8)[0]
    within = row % 8
    low = (2 * (within - ROOM)).astype(jnp.float32)
    head = (group < blocks) & (within < ROOM) & (slot == within.astype(jnp.float32))
    even = (group >= blocks) & (group < 2 * blocks) & (within >= ROOM) & (slot == low)
    uneven = (group >= 2 * blocks) & (group < 3 * blocks) & (within >= ROOM) & (slot == low + 1.0)
    codes = (group - 3 * blocks == row // 8) & (group >= 3 * blocks) & (within == 7)
    select = jnp.where(head | even | uneven | codes, 1.0, 0.0).astype(jnp.bfloat16)
    rest = parts[...]
    total = jnp.zeros(out_ref.shape, jnp.float32)
    for _ in range(3):
        part = rest.astype(jnp.bfloat16)
        rest = rest - part.astype(jnp.float32)
        total = total + jnp.dot(select, part, preferred_element_type=jnp.float32)
    out_ref[...] = total


def table_kernel(profile_ref, pairs_ref, last_ref):
    a = lax.broadcasted_iota(jnp.int32, (DISC, DISC), 0) - HALO
    c = lax.broadcasted_iota(jnp.int32, (DISC, DISC), 1) - HALO
    weights = jnp.where(a * a + c * c <= HALO * HALO, profile_ref[...], 0.0)
    kernel = (weights / jnp.sum(weights)).astype(jnp.bfloat16)
    source = lax.broadcasted_iota(jnp.int32, (DISC, LANES), 0)
    target = lax.broadcasted_iota(jnp.int32, (DISC, LANES), 1)
    mirror = jnp.where((source + target) % LANES == 0, 1.0, 0.0).astype(jnp.bfloat16)
    mirrored = jnp.dot(kernel, mirror, preferred_element_type=jnp.float32)
    left = lax.broadcasted_iota(jnp.int32, (LANES, LANES), 1) < SPAN

    def band(row, start):
        wide = jnp.broadcast_to(mirrored[row : row + 1, :], (LANES, LANES))
        return pltpu.roll(wide, start, 1, stride=1, stride_axis=0)

    for u in range(TURNS):
        for s in range(0, STEP, 2):
            row = u * STEP + s
            both = jnp.where(left, band(row, 0), band(row + 1, SPAN))
            pairs_ref[u * LANES : (u + 1) * LANES, s * SPAN : (s + 2) * SPAN] = both.astype(jnp.bfloat16)
    last_ref[...] = jnp.where(left, band(2 * HALO, 0), 0.0).astype(jnp.bfloat16)


def hats(row, cell):
    near, far, here, there = (value.astype(jnp.bfloat16) for value in row)
    zero = jnp.zeros((), jnp.bfloat16)
    return jnp.maximum(zero, jnp.minimum((cell - here) + near, (there - cell) + far))


def add_half(got_ref, total, codes, table, done, lists, stage, facts):
    sources = got_ref.shape[0]
    rays = 3 * LANES
    codes[...] = got_ref[:, 7, 2 * LANES : 3 * LANES].astype(jnp.int32)
    copy = pltpu.make_async_copy(codes, table, done)
    copy.start()
    copy.wait()
    room = sources * ROOM + BATCH
    first_lane = lax.axis_index("row") % 2 * 8

    def sort(source, carry):
        turns, inner, outer = carry
        turns = jnp.maximum(turns, table[source, 16])
        for k in range(ROOM):
            code = table[source, first_lane + k]
            entry = (source * 8 + k) * 16 + (code & 15)
            lists[inner] = entry
            lists[room + outer] = entry
            inner = inner + (code < 16).astype(jnp.int32)
            outer = outer + ((code >> 4) == 1).astype(jnp.int32)
        return turns, inner, outer

    turns, inner, outer = lax.fori_loop(0, sources, sort, (jnp.int32(0),) * 3)

    def doubled(cell):
        return (2 * cell).astype(jnp.float32).astype(jnp.bfloat16)

    across = doubled(lax.broadcasted_iota(jnp.int32, (WIDE, rays), 0) - HALO)
    own = doubled(lax.broadcasted_iota(jnp.int32, (TILE, rays), 0))
    edge = lax.broadcasted_iota(jnp.int32, (2 * HALO, rays), 0)
    edge = doubled(jnp.where(edge < HALO, edge - HALO, edge + (TILE - HALO)))

    def add(base, down, step, sums):
        for k in range(BATCH):
            entry = lists[base + step * BATCH + k]
            source, slot = entry >> 7, (entry >> 4) & 7
            head = got_ref[source, pl.ds(slot, 1), :]
            tail = got_ref[source, pl.ds(ROOM + (slot >> 1), 1), :]
            stage[0, k : k + 1, :] = head[:, :rays]
            stage[1, k : k + 1, :LANES] = head[:, rays:]
            stage[1, k : k + 1, LANES:] = jnp.where(
                (slot & 1) == 1, tail[:, 2 * LANES :], tail[:, : 2 * LANES]
            )
            for axis, shift in enumerate(((entry >> 2) & 3, entry & 3)):
                offset = ((shift - 1) * (2 * TILE)).astype(jnp.float32)
                stage[2 + axis, k : k + 1, :] = jnp.full((1, rays), offset)
        for axis in range(2):
            coords = stage[axis]
            low = jnp.floor(coords)
            facts[4 * axis] = 1.0 - (coords - low)
            facts[4 * axis + 1] = 1.0 - ((low + 1.0) - coords)
            here = 2.0 * low + stage[2 + axis]
            facts[4 * axis + 2] = here
            facts[4 * axis + 3] = here + 2.0
        firsts, seconds = [], []
        for k in range(BATCH):
            row = [facts[j, k : k + 1, :] for j in range(8)]
            firsts.append(hats(row[:4], down))
            seconds.append(hats(row[4:], across))
        return sums + lax.dot_general(
            jnp.concatenate(firsts, axis=1),
            jnp.concatenate(seconds, axis=1),
            (((1,), (1,)), ((), ())),
            preferred_element_type=jnp.float32,
        )

    top, middle, bottom = slice(0, HALO), slice(HALO, HALO + TILE), slice(HALO + TILE, WIDE)
    for count, base in ((inner, 0), (outer, room)):
        for k in range(BATCH):
            lists[base + count + k] = 15
    steps = (inner + BATCH - 1) // BATCH
    total[middle] = lax.fori_loop(0, steps, functools.partial(add, 0, own), total[middle])
    steps = (outer + BATCH - 1) // BATCH
    sums = jnp.concatenate([total[top], total[bottom]], axis=0)
    sums = lax.fori_loop(0, steps, functools.partial(add, room, edge), sums)
    total[top] = sums[:HALO]
    total[bottom] = sums[HALO:]
    return turns


def first_kernel(got_ref, before_ref, total_ref, turns_ref, *scratch):
    if before_ref is None:
        total_ref[...] = jnp.zeros(total_ref.shape, jnp.float32)
    else:
        total_ref[...] = before_ref[...]
    turns_ref[0] = add_half(got_ref, total_ref, *scratch)


def second_kernel(scale, got_ref, before_ref, pairs_ref, last_ref, out_ref, total, left, *scratch):
    total[...] = before_ref[...]
    add_half(got_ref, total, *scratch)
    cells = total[...]
    blocks = [cells[:, at : at + LANES].astype(jnp.bfloat16) for at in (0, SPAN)]
    for h in range(2):
        for u in range(TURNS):
            left[h * LONG : (h + 1) * LONG, u * LANES : (u + 1) * LANES] = blocks[h][
                u * STEP : u * STEP + LONG, :
            ]
    lowest = jnp.concatenate([block[2 * HALO :, :] for block in blocks], axis=0)
    ends = jnp.dot(lowest, last_ref[...], preferred_element_type=jnp.float32)
    evens = [ends[:TILE], ends[TILE:]]
    odds = [jnp.zeros((TILE, LANES), jnp.float32)] * 2
    for p in range(0, STEP * SPAN, 2 * LANES):
        both = jnp.dot(left[...], pairs_ref[:, p : p + 2 * LANES], preferred_element_type=jnp.float32)
        for h in range(2):
            for lanes in (0, LANES):
                s = (p + lanes) // SPAN
                part = both[h * LONG : (h + 1) * LONG, lanes : lanes + LANES]
                evens[h] = evens[h] + part[s : s + TILE]
                odds[h] = odds[h] + part[s + 1 : s + 1 + TILE]
    low = evens[0] + pltpu.roll(odds[0], SPAN, 1)
    high = pltpu.roll(evens[1], SPAN, 1) + odds[1]
    lane = lax.broadcasted_iota(jnp.int32, (TILE, LANES), 1)
    out_ref[...] = jnp.where(lane < SPAN, low, high) / scale


def shards(positions, destination, profile):
    blocks, _, rays = positions.shape
    row_count, col_count = lax.axis_size("row"), lax.axis_size("col")
    tiles = row_count * col_count
    width = -(-(3 * blocks + tiles) // LANES) * LANES

    def exchange(turn):
        kernel, given = pack_kernel, (turn, destination.T, positions)
        if turn is None:
            kernel, given = functools.partial(pack_kernel, None), (destination.T, positions)
        outgoing = pl.pallas_call(
            kernel,
            out_shape=jax.ShapeDtypeStruct((8 * tiles, rays + LANES), jnp.float32),
            in_specs=[SMEM, VMEM, VMEM][-len(given) :],
            out_specs=VMEM,
            scratch_shapes=[
                pltpu.VMEM((1, width), jnp.float32),
                pltpu.VMEM((width, rays + LANES), jnp.float32),
            ],
            compiler_params=pltpu.CompilerParams(vmem_limit_bytes=60 * 1024 * 1024),
            name="pack",
        )(*given)
        return lax.all_to_all(
            outgoing.reshape(tiles, 8, rays + LANES), ("row", "col"), split_axis=0, concat_axis=0, tiled=True
        )

    scratch = [
        pltpu.VMEM((tiles, LANES), jnp.int32),
        pltpu.SMEM((tiles, LANES), jnp.int32),
        pltpu.SemaphoreType.DMA,
        pltpu.SMEM((2 * (tiles * ROOM + BATCH),), jnp.int32),
        pltpu.VMEM((4, BATCH, rays), jnp.float32),
        pltpu.VMEM((8, BATCH, rays), jnp.float32),
    ]

    def deposit(mine, before, pairs, last):
        other = lax.ppermute(mine, "row", [(i, i ^ 1) for i in range(row_count)])
        kernel, given = first_kernel, (mine, before)
        if before is None:
            kernel, given = lambda got, *refs: first_kernel(got, None, *refs), (mine,)
        total, turns = pl.pallas_call(
            kernel,
            out_shape=(
                jax.ShapeDtypeStruct((WIDE, WIDE), jnp.float32),
                jax.ShapeDtypeStruct((1,), jnp.int32),
            ),
            in_specs=[VMEM] * len(given),
            out_specs=(VMEM, SMEM),
            scratch_shapes=scratch,
            compiler_params=LIMIT,
            cost_estimate=pl.CostEstimate(flops=2_000_000_000, bytes_accessed=4_000_000, transcendentals=0),
            name="first",
        )(*given)
        out, total = pl.pallas_call(
            functools.partial(second_kernel, blocks * rays / (TILE * TILE)),
            out_shape=(
                jax.ShapeDtypeStruct((TILE, TILE), jnp.float32),
                jax.ShapeDtypeStruct((WIDE, WIDE), jnp.float32),
            ),
            in_specs=[VMEM] * 4,
            out_specs=(VMEM, VMEM),
            scratch_shapes=[pltpu.VMEM((2 * LONG, TURNS * LANES), jnp.bfloat16)] + scratch,
            compiler_params=LIMIT,
            name="second",
        )(other, total, pairs, last)
        return out, total, turns[0]

    mine = exchange(None)
    pairs, last = pl.pallas_call(
        table_kernel,
        out_shape=(
            jax.ShapeDtypeStruct((TURNS * LANES, STEP * SPAN), jnp.bfloat16),
            jax.ShapeDtypeStruct((LANES, LANES), jnp.bfloat16),
        ),
        in_specs=[VMEM],
        out_specs=(VMEM, VMEM),
        compiler_params=LIMIT,
        cost_estimate=pl.CostEstimate(flops=10_000_000, bytes_accessed=6_000_000, transcendentals=0),
        name="table",
    )(profile)
    mine, pairs, last = lax.optimization_barrier((mine, pairs, last))
    out, total, turns = deposit(mine, None, pairs, last)

    def more(state):
        turn, _, total = state
        out, total, _ = deposit(exchange(jnp.full((1,), turn, jnp.int32)), total, pairs, last)
        return turn + 1, out, total

    return lax.while_loop(lambda state: state[0] < turns, more, (jnp.int32(1), out, total))[1]


def solution(mesh):
    placed = (P(("maps", "row", "col"), None, None), P(("maps", "row", "col"), None), P())
    return jax.shard_map(
        shards, mesh=mesh, in_specs=placed, out_specs=P(("maps", "row"), "col"), check_vma=False
    )
```

time: 29.9 us -> 31.5 us (1.054); the launches traced: 29.5 us -> 31.9 us
  waiting for transfers between devices: 5.54 us -> 8.46 us
  Pallas kernels: 14.3 us -> 13.8 us
    all_to_all x1, waiting for transfers between devices: 5.54 us -> 8.45 us  [exchange(): lax.all_to_all(outgoing.reshape(tiles, 8, rays + LANES), ('row', 'col'),...]
    pallas_call x2, Pallas kernels: 5.36 us -> 3.07 us  [the longest x1 2.19 us: exchange(): pl.pallas_call(kernel, out_shape=jax.ShapeDtypeStruct((8 * tiles, rays +...]
    pallas_call x1, Pallas kernels: 4.99 us -> 6.11 us  [deposit(): pl.pallas_call(functools.partial(second_kernel, blocks * rays / (TILE * T...]
    pallas_call x1, Pallas kernels: 3.94 us -> 4.62 us  [deposit(): pl.pallas_call(kernel, out_shape=(jax.ShapeDtypeStruct((WIDE, WIDE), jnp....]
    unnamed x8 -> x6, local copies, waits for them, and re-layouts: 0.78 us -> 0.66 us
  transfers between devices with their start and end apart: 2 -> 2, of which waited for: 1 -> 1; matrix products, arithmetic and copies ran while one was open for 0% -> 0% of each run, Pallas kernels for 24% -> 17%
where the time goes in v11:
time: 31.5 us; the launch traced here: 31.9 us
  Pallas kernels  13.8 us (44%)
  waiting for transfers between devices  8.46 us (27%)
  starting transfers between devices  8.27 us (26%)
  loops' own time  0.69 us (2%)
  local copies, waits for them, and re-layouts  0.66 us (2%)
    all_to_all x1, waiting for transfers between devices, exchange(): lax.all_to_all(outgoing.reshape(tiles, 8, rays + LANES), ('row', 'col'),...  8.45 us
    all_to_all x1, starting transfers between devices, exchange(): lax.all_to_all(outgoing.reshape(tiles, 8, rays + LANES), ('row', 'col'),...  7.45 us
    pallas_call x1, Pallas kernels, deposit(): pl.pallas_call(functools.partial(second_kernel, blocks * rays / (TILE * T...  6.11 us
    pallas_call x1, Pallas kernels, deposit(): pl.pallas_call(kernel, out_shape=(jax.ShapeDtypeStruct((WIDE, WIDE), jnp....  4.62 us
    pallas_call x1, Pallas kernels, exchange(): pl.pallas_call(kernel, out_shape=jax.ShapeDtypeStruct((8 * tiles, rays +...  2.19 us
    pallas_call x1, Pallas kernels, shards(): pl.pallas_call(table_kernel, out_shape=(jax.ShapeDtypeStruct((TURNS * LAN...  0.88 us
    ppermute x1, starting transfers between devices, deposit(): other = lax.ppermute(mine, 'row', [(i, i ^ 1) for i in range(row_count)])  0.82 us
    another operation x1, loops' own time, shards(): lax.while_loop(lambda state: state[0] < turns, more, (jnp.int32(1), out,...  0.69 us
  transfers between devices with their start and end apart: 2, of which 1 were waited for; matrix products, arithmetic and copies ran while one was open for 0% of the time, Pallas kernels for 17%

profile of v11, /device:TPU:1, one launch (start us, length us, event | category | flops | bytes accessed | tf_op | source)
XLA Modules:
  0.0 31.9 jit_solution(10805878600053619295)
XLA Ops:
  0.0 0.0 copy-start.2
  0.0 0.7 %copy-done.2 = s32[16,1]{0,1:T(1,128)S(1)} copy-done((s32[16,1]{0,1:T(1,128)S(1)}, s32[16,1]{0,1:T(1,128)}, u32[]{:S(2)}) %copy-start.2) | copy-done | bytes 88
  0.7 2.2 %pack.2 = f32[128,512]{1,0:T(8,128)} custom-call(s32[1,16]{1,0:T(1,128)S(1)} %bitcast.14, f32[16,2,384]{2,1,0:T(2,128)} %rays_ref.1), custom_call_target="tpu_custom_call" | custom-call | tf_op jit(solution)/shard_map/pack/pallas_call | solution.py:273
  2.8 0.0 copy-start
  2.8 7.5 %all-to-all-start.1 = ((f32[16,8,512]{2,1,0:T(8,128)}), f32[16,8,512]{2,1,0:T(8,128)S(1)}, u32[]{:S(2)}, u32[]{:S(2)}) async-start(f32[16,8,512]{2,1,0:T(8,128)} %bitcast.13), calls=%async_computation.1 | async-start | bytes 524288 | tf_op jit(solution)/shard_map/all_to_all | solution.py:285
  10.3 0.0 copy-done
  10.3 0.9 %table.1 = (bf16[512,1024]{1,0:T(8,128)(2,1)S(1)}, bf16[128,128]{1,0:T(8,128)(2,1)S(1)}) custom-call(f32[65,65]{1,0:T(8,128)S(1)} %copy-done), custom_call_target="tpu_custom_call" | custom-call | flops 10000000 | bytes 6000000 | tf_op jit(solution)/shard_map/table/pallas_call | solution.py:331
  11.2 8.5 %all-to-all-done.1.got = f32[16,8,512]{2,1,0:T(8,128)S(1)} async-done(((f32[16,8,512]{2,1,0:T(8,128)}), f32[16,8,512]{2,1,0:T(8,128)S(1)}, u32[]{:S(2)}, u32[]{:S(2)}) %all-to-all-start.1) | async-done | bytes 262176 | tf_op jit(solution)/shard_map/all_to_all | solution.py:285
  19.6 0.8 %collective-permute-start.1 = (f32[16,8,512]{2,1,0:T(8,128)S(1)}, f32[16,8,512]{2,1,0:T(8,128)S(1)}, u32[]{:S(2)}, u32[]{:S(2)}) collective-permute-start(f32[16,8,512]{2,1,0:T(8,128)S(1)} %all-to-all-done.1.got), channel_id=1, source_target_pairs={{0,4},{4,0},{8,12},{12,8},{1,5},{5,1},{9,13},{13,9},{2,6},{6,2},{1... | collective-permute-start | bytes 786440 | tf_op jit(solution)/shard_map/ppermute | solution.py:299
  20.5 4.6 %first.2 = (f32[192,192]{1,0:T(8,128)S(1)}, s32[1]{0:T(128)}) custom-call(f32[16,8,512]{2,1,0:T(8,128)S(1)} %all-to-all-done.1.got), custom_call_target="tpu_custom_call" | custom-call | flops 2000000000 | bytes 4000000 | tf_op jit(solution)/shard_map/first/pallas_call | solution.py:303
  25.1 0.0 collective-permute-done.1.got_ref
  25.1 0.0 copy-start.1
  25.1 6.1 %second.2 = (f32[128,128]{1,0:T(8,128)}, f32[192,192]{1,0:T(8,128)S(1)}) custom-call(f32[16,8,512]{2,1,0:T(8,128)S(1)} %collective-permute-done.1.got_ref, f32[192,192]{1,0:T(8,128)S(1)} %get-tuple-element.62.before_ref, bf16[512,1024]{1,0:T(8,128)(2,1)S(1)} %get-tuple-element.145.pairs_ref, bf16[128,128]{1,0:T(8,128)(2,1)S(1)} %get-tuple-element.146.last_ref), custom_call_target="tpu_custom_call" | custom-call | tf_op jit(solution)/shard_map/second/pallas_call | solution.py:316
  31.2 0.0 copy-done.1
  31.2 0.7 %while.12 = (s32[]{:T(128)}, f32[128,128]{1,0:T(8,128)}, f32[192,192]{1,0:T(8,128)S(1)}, s32[]{:T(128)}, s32[16,1]{0,1:T(1,128)S(1)}, /*index=5*/f32[16,2,384]{2...) while((s32[]{:T(128)}, f32[128,128]{1,0:T(8,128)}, ...), condition=%wide.region_1.0_spmd, body=%wide.region_0.0_spmd.sunk | while | flops 2000000000 | bytes 5572997 | solution.py:351
Async XLA Ops:
  0.0 0.7 %copy-start.2 = (s32[16,1]{0,1:T(1,128)S(1)}, s32[16,1]{0,1:T(1,128)}, u32[]{:S(2)}) copy-start(s32[16,1]{0,1:T(1,128)} %param.6) | copy-start | bytes 196
  2.8 7.5 %copy-start = (f32[65,65]{1,0:T(8,128)S(1)}, f32[65,65]{1,0:T(8,128)}, u32[]{:S(2)}) copy-start(f32[65,65]{1,0:T(8,128)} %profile_ref.1) | copy-start | bytes 50704
  2.8 16.8 %all-to-all-start.1 = ((f32[16,8,512]{2,1,0:T(8,128)}), f32[16,8,512]{2,1,0:T(8,128)S(1)}, u32[]{:S(2)}, u32[]{:S(2)}) async-start(f32[16,8,512]{2,1,0:T(8,128)} %bitcast.13), calls=%async_computation.1 | async-start | bytes 524288 | tf_op jit(solution)/shard_map/all_to_all | solution.py:285
  19.6 5.5 %collective-permute-start.1 = (f32[16,8,512]{2,1,0:T(8,128)S(1)}, f32[16,8,512]{2,1,0:T(8,128)S(1)}, u32[]{:S(2)}, u32[]{:S(2)}) collective-permute-start(f32[16,8,512]{2,1,0:T(8,128)S(1)} %all-to-all-done.1.got), channel_id=1, source_target_pairs={{0,4},{4,0},{8,12},{12,8},{1,5},{5,1},{9,13},{13,9},{2,6},{6,2},{1... | collective-permute-start | bytes 786440 | tf_op jit(solution)/shard_map/ppermute | solution.py:299
  25.1 6.1 %copy-start.1 = (f32[16,2,384]{2,1,0:T(2,128)S(1)}, f32[16,2,384]{2,1,0:T(2,128)}, u32[]{:S(2)}) copy-start(f32[16,2,384]{2,1,0:T(2,128)} %rays_ref.1) | copy-start | bytes 147460
